TPU v7x, 256 devices: a whole 4x4x8 slice. The times are simulated.
256 devices in a mesh: term: 8 (over y, x_lo), sector: 32 (over x_hi, z, core).
Axes of the slice: x: 4 (x_hi: 2, x_lo: 2; x = x_hi * 2 + x_lo), y: 4, z: 8, core: 2. Of those that a mesh axis runs over, the one named last changes fastest.
Arguments:
- psi: bfloat16 [32, 512, 512], P('sector'), may hold values from -6 to 6
- left_blocks: bfloat16 [64, 32, 512, 512], P('term', 'sector'), may hold values from -0.09375 to 0.09375
- right_ops: bfloat16 [64, 512, 512], P('term'), may hold values from -0.25 to 0.25
- sector_rows: int32 [32], replicated, may hold values from 128 to 512, as said below
- connect: int32 [64, 32], replicated, may hold values from 0 to 31, each once within a row
- term_order: int32 [64], replicated, may hold values from 0 to 63, each once
- sector_at: int32 [32], replicated, may hold values from 0 to 31, each once
Outputs:
- sigma: float32 [32, 512, 512], P('sector', None, 'term')
Inputs may be any that keep to these rules, and one draw needn't show every extreme that they name: `sector_rows`: live rows of each sector; rows from this count up to 512 of a block are padding. Some sector has exactly 512 and some exactly 128. `connect`: each row is a permutation of the sector ids. `term_order`: A permutation of the terms. `sector_at`: A permutation of the sector ids.
All inputs are finite; a program needn't handle non-finite values.
Results may differ from a plain program's by a relative error of at most 0.0003.
Values may be sent and summed in bfloat16 or wider, within the bound.
No kernel may reach another device: no remote copies, remote signals or barrier semaphores. Data moves between devices by JAX's collectives and lax.ppermute only.
A program may use at most 128 MiB of HBM per device.

v0:
```python
import jax
import jax.numpy as jnp
from jax import lax
from jax.sharding import PartitionSpec as P


def on_device(psi, left_blocks, right_ops, sector_rows, connect, term_order, sector_at):
    group = lax.axis_index("term")
    place = lax.axis_index("sector")
    per_group = left_blocks.shape[0]
    capacity = psi.shape[1]
    count_sectors = sector_at.shape[0]
    ids = jnp.arange(count_sectors, dtype=jnp.int32)
    position = jnp.sum(jnp.where(sector_at[None, :] == ids[:, None], ids[None, :], 0), axis=1)
    target = sector_at[place]
    my_terms = lax.dynamic_slice_in_dim(term_order, group * per_group, per_group)
    my_sources = connect[my_terms, target]
    gathered = lax.all_gather(psi, "sector", axis=0, tiled=True)
    blocks = gathered[position[my_sources]]
    row_index = jnp.arange(capacity, dtype=jnp.int32)
    live_rows = row_index[None, :] < sector_rows[my_sources][:, None]
    blocks = jnp.where(live_rows[:, :, None], blocks, jnp.zeros((), blocks.dtype))
    inner_part = jnp.einsum(
        "kab,kbc->kac", left_blocks[:, 0], blocks, preferred_element_type=jnp.float32
    )
    outer_part = jnp.einsum(
        "kac,kcd->kad",
        inner_part,
        right_ops.astype(jnp.float32),
        precision=lax.Precision.HIGHEST,
        preferred_element_type=jnp.float32,
    )
    summed = jnp.sum(outer_part, axis=0)
    summed = jnp.where(
        (row_index < sector_rows[target])[:, None], summed, jnp.zeros((), summed.dtype)
    )
    return lax.psum_scatter(summed[None], "term", scatter_dimension=2, tiled=True)


def solution(mesh):
    placed = (
        P("sector", None, None),
        P("term", "sector", None, None),
        P("term", None, None),
        P(),
        P(),
        P(),
        P(),
    )
    return jax.shard_map(
        on_device, mesh=mesh, in_specs=placed, out_specs=P("sector", None, "term"), check_vma=False
    )
```

profile of v0, /device:TPU:4, one launch (start us, length us, event | category | flops | bytes accessed | tf_op | source)
XLA Modules:
  0.0 264.9 jit_solution(13737106770206382898)
XLA Ops:
  6.5 0.0 copy-start
  6.5 0.0 all-gather.2.cloned.1.call-start
  6.5 0.7 all-gather.2.cloned.1.call-update
  7.3 0.0 all-reduce.4.cloned.1.call-start
  7.3 1.2 dynamic_slice.9
  10.5 1.2 dynamic_slice.10
  11.7 0.7 fusion.18
  12.5 0.0 copy-done
  12.5 0.6 gather_fusion
  13.1 1.3 gather_fusion.1
  14.4 0.8 select_reduce_fusion
  15.2 0.6 gather_fusion.2
  15.9 0.7 iota_compare_fusion.2
  16.5 0.1 iota_compare_fusion.1
  16.6 131.8 %all-gather.2.cloned.1.call-done = bf16[32,512,512]{2,1,0:T(8,128)(2,1)} async-done(((bf16[1,512,512]{2,1,0:T(8,128)(2,1)}), bf16[32,512,512]{2,1,0:T(8,128)(2,1)}) %all-gather.2.cloned.1.call-update) | async-done | bytes 16777232 | tf_op jit(solution)/shard_map/all_gather | solution.py:18
  148.4 8.5 %gather_fusion.3 = bf16[8,512,512]{2,1,0:T(8,128)(2,1)} fusion(bf16[32,512,512]{2,1,0:T(8,128)(2,1)} %all-gather.2.cloned.1.call-done, s32[1024]{0:T(1024)S(1)} %pad_clamp_fusion), kind=kCustom, calls=%fused_computation.3 | custom fusion | bytes 8388640 | tf_op jit(solution)/shard_map/gather | solution.py:19
  156.9 0.0 copy-start.1
  156.9 6.0 %fusion.2 = f32[8,512,512]{2,1,0:T(8,128)S(1)} fusion(bf16[8,1,512,512]{3,2,1,0:T(8,128)(2,1)} %param.8, bf16[8,512,512]{2,1,0:T(8,128)(2,1)} %gather_fusion.3, pred[8,512]{1,0:T(8,128)(4,1)S(1)} %iota_compare_fusion.1), kind=kOutput, calls=%fused_computation.6 | convolution fusion | flops 2149580800 | bytes 16781312 | tf_op jit(solution)/shard_map/kab,kbc->kac/dot_general | solution.py:23
  163.0 0.0 copy-done.1
  163.0 0.0 copy-start.2
  163.0 6.7 %fusion.13 = f32[1,512,512]{2,1,0:T(8,128)S(1)} fusion(bf16[8,512,512]{2,1,0:T(8,128)(2,1)S(1)} %copy-done.1, f32[8,512,512]{2,1,0:T(8,128)S(1)} %fusion.2, pred[512]{0:T(512)(128)(4,1)S(1)} %iota_compare_fusion.2), kind=kOutput, calls=%fused_computation.13 | convolution fusion | flops 12885164032 | bytes 13632000 | tf_op jit(solution)/shard_map/kac,kcd->kad/dot_general | solution.py:26
  169.7 2.0 copy.16
  171.6 0.0 all-reduce.4.cloned.1.call-update
  171.7 0.0 copy-done.2
  171.7 0.6 dynamic-slice
  172.9 83.5 %all-reduce.4.cloned.1.call-done = f32[1,512,512]{1,0,2:T(1,128)} async-done(((f32[1,512,512]{1,0,2:T(1,128)}), f32[1,512,512]{1,0,2:T(1,128)}) %all-reduce.4.cloned.1.call-update) | async-done | bytes 1048592
  256.5 0.9 constant_dynamic-slice_fusion
  257.4 0.7 copy.17
  (4 shorter events, 0.0 us)
Async XLA Ops:
  6.5 5.9 %copy-start = (s32[64,32]{0,1:T(8,128)S(1)}, s32[64,32]{0,1:T(8,128)}, u32[]{:S(2)}) copy-start(s32[64,32]{0,1:T(8,128)} %param.11) | copy-start | bytes 24580
  6.5 141.9 %all-gather.2.cloned.1.call-start = ((), (), s32[]{:S(2)}) async-start(), calls=%async_computation | async-start | bytes 17301504 | tf_op jit(solution)/shard_map/all_gather | solution.py:18
  7.3 249.2 %all-reduce.4.cloned.1.call-start = ((), (), s32[]{:S(2)}) async-start(), calls=%async_computation.1 | async-start | bytes 2097152
  156.9 6.0 %copy-start.1 = (bf16[8,512,512]{2,1,0:T(8,128)(2,1)S(1)}, bf16[8,512,512]{2,1,0:T(8,128)(2,1)}, u32[]{:S(2)}) copy-start(bf16[8,512,512]{2,1,0:T(8,128)(2,1)} %param.9) | copy-start | bytes 12582916
  163.0 8.7 %copy-start.2 = (u32[256]{0:T(256)S(1)}, u32[256]{0:T(256)}, u32[]{:S(2)}) copy-start(u32[256]{0:T(256)} %constant.43) | copy-start | bytes 3076
Sparse Core Ops, SparseCore 0:
  10.1 138.2 all-gather.1
  171.8 84.6 all-reduce.3
where the time goes:
time: 265 us
  waiting for transfers between devices  216 us (82%)
  local copies, waits for them, and re-layouts  17.7 us (7%)
  between operations  16.1 us (6%)
  matrix products  12.7 us (5%)
    all_gather x1, waiting for transfers between devices, on_device(): gathered = lax.all_gather(psi, 'sector', axis=0, tiled=True)  132 us
    unnamed x3, waiting for transfers between devices  84.3 us
    gather x2, local copies, waits for them, and re-layouts, on_device(): blocks = gathered[position[my_sources]]  9.17 us
    dot_general x1, matrix products, on_device(): jnp.einsum('kac,kcd->kad', inner_part, right_ops.astype(jnp.float32), pre...  6.68 us
    dot_general x1, matrix products, on_device(): jnp.einsum('kab,kbc->kac', left_blocks[:, 0], blocks, preferred_element_t...  6.02 us
  transfers between devices with their start and end apart: 2, of which 2 were waited for; matrix products, arithmetic and copies ran while one was open for 3% of the time, Pallas kernels for 0%

commit v1 on v0

v1 whole, which is shorter than its diff:
```python
import functools

import jax
import jax.numpy as jnp
from jax import lax
from jax.experimental import pallas as pl
from jax.experimental.pallas import tpu as pltpu
from jax.sharding import PartitionSpec as P

GROUPS = 8
SLOTS = 8
PLACES = 32
BLK = 512
PART = BLK // GROUPS


def place_permutation(f):
    return [(s, f(s)) for s in range(PLACES)]


def find_positions(sector_at, position):
    def put(p, carry):
        position[sector_at[p]] = p
        return carry

    lax.fori_loop(0, PLACES, put, 0)


def select_kernel(where, term_order, connect, sector_at, own, other, out, position, sem):
    find_positions(sector_at, position)
    place = where[1]
    core = lax.rem(place, 2)
    target = sector_at[place]

    def start(i, carry):
        p = position[connect[term_order[i], target]]
        half = lax.div(p, 2)
        mine = lax.rem(p, 2) == core
        dst = out.at[i]

        @pl.when(mine)
        def _():
            pltpu.make_async_copy(own.at[half], dst, sem).start()

        @pl.when(jnp.logical_not(mine))
        def _():
            pltpu.make_async_copy(other.at[half], dst, sem).start()

        return carry

    lax.fori_loop(0, GROUPS * SLOTS, start, 0)
    pltpu.make_async_copy(out, out, sem).wait()


def product_kernel(where, term_order, connect, sector_at, sector_rows, block, left, right, out, acc):
    k = pl.program_id(0)
    group, place = where[0], where[1]
    target = sector_at[place]
    source = connect[term_order[group * SLOTS + k], target]
    live = sector_rows[source]
    rows = lax.broadcasted_iota(jnp.int32, (BLK, BLK), 0)
    b = block[...].reshape(BLK, BLK)
    b = jnp.where(rows < live, b, jnp.zeros((), b.dtype))
    t = jnp.dot(b, right[0], preferred_element_type=jnp.float32)
    hi = t.astype(jnp.bfloat16)
    lo = (t - hi.astype(jnp.float32)).astype(jnp.bfloat16)
    l = left[0, 0]
    part = jnp.dot(l, hi, preferred_element_type=jnp.float32) + jnp.dot(
        l, lo, preferred_element_type=jnp.float32
    )

    @pl.when(k == 0)
    def _():
        acc[...] = part

    @pl.when(k > 0)
    def _():
        acc[...] += part

    @pl.when(k == SLOTS - 1)
    def _():
        total = jnp.where(rows < sector_rows[target], acc[...], 0.0)
        out[...] = total.T


def on_device(psi, left_blocks, right_ops, sector_rows, connect, term_order, sector_at):
    group = lax.axis_index("term")
    place = lax.axis_index("sector")
    where = jnp.stack([group, place]).astype(jnp.int32)
    smem = pl.BlockSpec(memory_space=pltpu.SMEM)
    hbm = pl.BlockSpec(memory_space=pl.ANY)

    part = lax.dynamic_slice_in_dim(psi[0], group * PART, PART)
    copies = jnp.broadcast_to(part[None], (PLACES // 2, PART, BLK))
    same_core = [[c + 2 * h for h in range(PLACES // 2)] for c in range(2)]
    own = lax.all_to_all(copies, "sector", 0, 0, axis_index_groups=same_core, tiled=True)
    other = lax.ppermute(own, "sector", place_permutation(lambda s: s ^ 1))
    chosen = pl.pallas_call(
        select_kernel,
        out_shape=jax.ShapeDtypeStruct((GROUPS * SLOTS, PART, BLK), psi.dtype),
        in_specs=[smem] * 4 + [hbm] * 2,
        out_specs=hbm,
        scratch_shapes=[pltpu.SMEM((PLACES,), jnp.int32), pltpu.SemaphoreType.DMA],
    )(where, term_order, connect, sector_at, own, other)
    blocks = lax.all_to_all(chosen, "term", 0, 0, tiled=True).reshape(GROUPS, SLOTS, PART, BLK)
    summed = pl.pallas_call(
        product_kernel,
        grid=(SLOTS,),
        out_shape=jax.ShapeDtypeStruct((BLK, BLK), jnp.float32),
        in_specs=[smem] * 5
        + [
            pl.BlockSpec((GROUPS, 1, PART, BLK), lambda k: (0, k, 0, 0)),
            pl.BlockSpec((1, 1, BLK, BLK), lambda k: (k, 0, 0, 0)),
            pl.BlockSpec((1, BLK, BLK), lambda k: (k, 0, 0)),
        ],
        out_specs=pl.BlockSpec((BLK, BLK), lambda k: (0, 0)),
        scratch_shapes=[pltpu.VMEM((BLK, BLK), jnp.float32)],
        compiler_params=pltpu.CompilerParams(vmem_limit_bytes=32 * 1024 * 1024),
    )(where, term_order, connect, sector_at, sector_rows, blocks, left_blocks, right_ops)
    parts = lax.all_to_all(summed.reshape(GROUPS, PART, BLK), "term", 0, 0, tiled=True)
    return jnp.sum(parts, axis=0).T[None]


def solution(mesh):
    placed = (
        P("sector", None, None),
        P("term", "sector", None, None),
        P("term", None, None),
        P(),
        P(),
        P(),
        P(),
    )
    return jax.shard_map(
        on_device, mesh=mesh, in_specs=placed, out_specs=P("sector", None, "term"), check_vma=False
    )
```

time: 265 us -> 258 us (0.974)
  waiting for transfers between devices: 216 us -> 0.62 us
  Pallas kernels: 0 us -> 141 us
  blocking collectives: 0 us -> 110 us
  between operations: 16.1 us -> 0.11 us
  local copies, waits for them, and re-layouts: 17.7 us -> 3.63 us
  matrix products: 12.7 us -> 0 us
    pallas_call x0 -> x2, Pallas kernels: none -> 141 us  [the longest x1 130 us: on_device(): pl.pallas_call(select_kernel, out_shape=jax.ShapeDtypeStruct((GROUPS * SL...]
    all_gather x1 -> x0, waiting for transfers between devices: 132 us -> none  [on_device(): gathered = lax.all_gather(psi, 'sector', axis=0, tiled=True)]
    all_to_all x0 -> x3, blocking collectives: none -> 110 us  [the longest x1 55.1 us: on_device(): lax.all_to_all(chosen, 'term', 0, 0, tiled=True)]
    unnamed x3 -> x0, waiting for transfers between devices: 84.3 us -> none
    dot_general x2 -> x0, matrix products: 12.7 us -> none  [the longest x1 6.68 us: on_device(): jnp.einsum('kac,kcd->kad', inner_part, right_ops.astype(jnp.float32), pre...]
    gather x4 -> x0, local copies, waits for them, and re-layouts: 11.1 us -> none  [the longest x2 9.17 us: on_device(): blocks = gathered[position[my_sources]]]
  transfers between devices with their start and end apart: 2 -> 1, of which waited for: 2 -> 1; matrix products, arithmetic and copies ran while one was open for 3% -> 1% of each run, Pallas kernels for 0% -> 0%
where the time goes in v1:
time: 258 us; the launch traced here: 256 us
  Pallas kernels  141 us (55%)
  blocking collectives  110 us (43%)
  local copies, waits for them, and re-layouts  3.63 us (1%)
    pallas_call x1, Pallas kernels, on_device(): pl.pallas_call(select_kernel, out_shape=jax.ShapeDtypeStruct((GROUPS * SL...  130 us
    all_to_all x1, blocking collectives, on_device(): lax.all_to_all(chosen, 'term', 0, 0, tiled=True)  55.1 us
    all_to_all x1, blocking collectives, on_device(): lax.all_to_all(copies, 'sector', 0, 0, axis_index_groups=same_core, tiled...  36.9 us
    all_to_all x1, blocking collectives, on_device(): lax.all_to_all(summed.reshape(GROUPS, PART, BLK), 'term', 0, 0, tiled=True)  17.7 us
    pallas_call x1, Pallas kernels, on_device(): pl.pallas_call(product_kernel, grid=(SLOTS,), out_shape=jax.ShapeDtypeStr...  11.2 us
  transfers between devices with their start and end apart: 1, of which 1 were waited for; matrix products, arithmetic and copies ran while one was open for 1% of the time, Pallas kernels for 0%

profile of v1, /device:TPU:4, one launch (start us, length us, event | category | flops | bytes accessed | tf_op | source)
XLA Modules:
  0.0 256.5 jit_solution(6231042296985036237)
XLA Ops:
  0.0 0.0 copy-start
  0.0 1.0 copy-done
  1.0 0.1 broadcast_in_dim.12
  1.2 36.9 %all_to_all.15.own = bf16[16,64,512]{2,1,0:T(8,128)(2,1)S(1)} all-to-all(bf16[16,64,512]{2,1,0:T(8,128)(2,1)S(1)} %broadcast_in_dim.12), channel_id=1, replica_groups={{0,2,4,6,8,10,12,14,16,18,20,22,24,26,28,30},{1,3,5,7,9,11,13,15,17,19,..., dimensions={0} | all-to-all | bytes 2097152 | tf_op jit(solution)/shard_map/all_to_all | solution.py:96
  38.1 0.0 copy-start.8
  38.1 0.0 collective-permute-start
  38.1 1.4 copy.9.connect
  39.5 0.6 pad_add_fusion.where
  40.1 0.6 collective-permute-done.other
  40.8 0.0 copy-done.8
  40.8 0.0 copy-start.9
  40.8 1.0 copy-done.9
  41.8 0.0 copy-start.3
  41.8 0.0 copy-start.7
  41.8 129.8 %shard_map.73 = bf16[64,64,512]{2,1,0:T(8,128)(2,1)} custom-call(s32[2]{0:T(128)} %pad_add_fusion.where, s32[64]{0:T(128)} %term_order.3, s32[64,32]{1,0:T(8,128)} %copy.9.connect, s32[32]{0:T(128)} %sector_at.3, bf16[16,64,512]{2,1,0:T(8,128)(2,1)} %copy-done.8, bf16[16,64,512]{2,1,0:T(8,128)(2,1)} %copy-done.9), custom_call_target="tpu_custom_call" | custom-call | tf_op jit(solution)/shard_map/pallas_call | solution.py:98
  171.6 0.0 copy-start.1
  171.6 0.0 copy-start.2
  171.6 0.0 copy-start.4
  171.7 0.0 copy-start.5
  171.7 0.0 copy-start.6
  171.7 55.1 %all_to_all.16 = bf16[64,64,512]{2,1,0:T(8,128)(2,1)S(1)} all-to-all(bf16[64,64,512]{2,1,0:T(8,128)(2,1)} %shard_map.73), channel_id=1, replica_groups=mesh['term'=8,'sector'=32] {'term'}, dimensions={0} | all-to-all | bytes 8388608 | tf_op jit(solution)/shard_map/all_to_all | solution.py:105
  226.8 0.0 copy-done.3
  226.8 0.0 copy-done.7
  226.8 0.0 copy-done.1
  226.8 0.0 copy-done.2
  226.8 0.0 copy-done.4
  226.8 0.0 copy-done.5
  226.8 0.0 copy-done.6
  226.8 11.2 %shard_map.74 = f32[512,512]{1,0:T(8,128)S(1)} custom-call(s32[2]{0:T(128)S(1)} %copy-done.6, s32[64]{0:T(128)S(1)} %copy-done.4, s32[64,32]{1,0:T(8,128)S(1)} %copy-done.3, s32[32]{0:T(128)S(1)} %copy-done.5, s32[32]{0:T(128)S(1)} %copy-done.7, bf16[8,8,64,512]{3,2,1,0:T(8,128)(2,1)S(1)} %bitcast.9, bf16[8,1,512,512]{3,2,1,0:T(8,128)(2,1)S(1)} %copy-done.1, ...), custom_call_target="tpu_custom_call" | custom-call | tf_op jit(solution)/shard_map/pallas_call | solution.py:106
  238.0 17.7 %all_to_all.17 = f32[8,64,512]{2,1,0:T(8,128)S(1)} all-to-all(f32[8,64,512]{2,1,0:T(8,128)S(1)} %bitcast.10), channel_id=1, replica_groups=mesh['term'=8,'sector'=32] {'term'}, dimensions={0} | all-to-all | bytes 2097152 | tf_op jit(solution)/shard_map/all_to_all | solution.py:120
  255.8 0.7 reduce_sum.9
  (1 shorter events, 0.0 us)
Async XLA Ops:
  0.0 1.0 copy-start
  38.1 2.7 %copy-start.8 = (bf16[16,64,512]{2,1,0:T(8,128)(2,1)}, bf16[16,64,512]{2,1,0:T(8,128)(2,1)S(1)}, u32[]{:S(2)}) copy-start(bf16[16,64,512]{2,1,0:T(8,128)(2,1)S(1)} %all_to_all.15.own) | copy-start | bytes 3145732
  38.1 2.7 %collective-permute-start = (bf16[16,64,512]{2,1,0:T(8,128)(2,1)S(1)}, bf16[16,64,512]{2,1,0:T(8,128)(2,1)S(1)}, u32[]{:S(2)}, u32[]{:S(2)}) collective-permute-start(bf16[16,64,512]{2,1,0:T(8,128)(2,1)S(1)} %all_to_all.15.own), channel_id=1, source_target_pairs={{0,1},{1,0},{2,3},{3,2},{4,5},{5,4},{6,7},{7,6},{8,9},{9,8},{10,11... | collective-permute-start | bytes 3145736 | tf_op jit(solution)/shard_map/ppermute | solution.py:97
  40.8 1.0 copy-start.9
  41.8 185.0 %copy-start.3 = (s32[64,32]{1,0:T(8,128)S(1)}, s32[64,32]{1,0:T(8,128)}, u32[]{:S(2)}) copy-start(s32[64,32]{1,0:T(8,128)} %copy.9.connect) | copy-start | bytes 24580
  41.8 185.0 %copy-start.7 = (s32[32]{0:T(128)S(1)}, s32[32]{0:T(128)}, u32[]{:S(2)}) copy-start(s32[32]{0:T(128)} %sector_rows.1) | copy-start | bytes 388
  171.6 55.1 %copy-start.1 = (bf16[8,1,512,512]{3,2,1,0:T(8,128)(2,1)S(1)}, bf16[8,1,512,512]{3,2,1,0:T(8,128)(2,1)}, u32[]{:S(2)}) copy-start(bf16[8,1,512,512]{3,2,1,0:T(8,128)(2,1)} %left.1) | copy-start | bytes 12582916
  171.6 55.1 %copy-start.2 = (bf16[8,512,512]{2,1,0:T(8,128)(2,1)S(1)}, bf16[8,512,512]{2,1,0:T(8,128)(2,1)}, u32[]{:S(2)}) copy-start(bf16[8,512,512]{2,1,0:T(8,128)(2,1)} %right.1) | copy-start | bytes 12582916
  171.6 55.1 %copy-start.4 = (s32[64]{0:T(128)S(1)}, s32[64]{0:T(128)}, u32[]{:S(2)}) copy-start(s32[64]{0:T(128)} %term_order.3) | copy-start | bytes 772
  171.7 55.1 %copy-start.5 = (s32[32]{0:T(128)S(1)}, s32[32]{0:T(128)}, u32[]{:S(2)}) copy-start(s32[32]{0:T(128)} %sector_at.3) | copy-start | bytes 388
  171.7 55.1 %copy-start.6 = (s32[2]{0:T(128)S(1)}, s32[2]{0:T(128)}, u32[]{:S(2)}) copy-start(s32[2]{0:T(128)} %pad_add_fusion.where) | copy-start | bytes 28

commit v2 on v1

--- a/solution.py
+++ b/solution.py
@@ -26,7 +26,7 @@
     lax.fori_loop(0, PLACES, put, 0)
 
 
-def select_kernel(where, term_order, connect, sector_at, own, other, out, position, sem):
+def select_kernel(where, term_order, connect, sector_at, own, other, out, position):
     find_positions(sector_at, position)
     place = where[1]
     core = lax.rem(place, 2)
@@ -36,20 +36,18 @@
         p = position[connect[term_order[i], target]]
         half = lax.div(p, 2)
         mine = lax.rem(p, 2) == core
-        dst = out.at[i]
 
         @pl.when(mine)
         def _():
-            pltpu.make_async_copy(own.at[half], dst, sem).start()
+            out[i] = own[half]
 
         @pl.when(jnp.logical_not(mine))
         def _():
-            pltpu.make_async_copy(other.at[half], dst, sem).start()
+            out[i] = other[half]
 
         return carry
 
     lax.fori_loop(0, GROUPS * SLOTS, start, 0)
-    pltpu.make_async_copy(out, out, sem).wait()
 
 
 def product_kernel(where, term_order, connect, sector_at, sector_rows, block, left, right, out, acc):
@@ -88,7 +86,7 @@
     place = lax.axis_index("sector")
     where = jnp.stack([group, place]).astype(jnp.int32)
     smem = pl.BlockSpec(memory_space=pltpu.SMEM)
-    hbm = pl.BlockSpec(memory_space=pl.ANY)
+    vmem = pl.BlockSpec(memory_space=pltpu.VMEM)
 
     part = lax.dynamic_slice_in_dim(psi[0], group * PART, PART)
     copies = jnp.broadcast_to(part[None], (PLACES // 2, PART, BLK))
@@ -98,9 +96,10 @@
     chosen = pl.pallas_call(
         select_kernel,
         out_shape=jax.ShapeDtypeStruct((GROUPS * SLOTS, PART, BLK), psi.dtype),
-        in_specs=[smem] * 4 + [hbm] * 2,
-        out_specs=hbm,
-        scratch_shapes=[pltpu.SMEM((PLACES,), jnp.int32), pltpu.SemaphoreType.DMA],
+        in_specs=[smem] * 4 + [vmem] * 2,
+        out_specs=vmem,
+        scratch_shapes=[pltpu.SMEM((PLACES,), jnp.int32)],
+        compiler_params=pltpu.CompilerParams(vmem_limit_bytes=32 * 1024 * 1024),
     )(where, term_order, connect, sector_at, own, other)
     blocks = lax.all_to_all(chosen, "term", 0, 0, tiled=True).reshape(GROUPS, SLOTS, PART, BLK)
     summed = pl.pallas_call(

time: 258 us -> 131 us (0.51)
  Pallas kernels: 141 us -> 14.6 us
    pallas_call x1, Pallas kernels: 130 us -> 3.38 us  [on_device(): pl.pallas_call(select_kernel, out_shape=jax.ShapeDtypeStruct((GROUPS * SL...]
where the time goes in v2:
time: 131 us; the launch traced here: 130 us
  blocking collectives  110 us (84%)
  Pallas kernels  14.6 us (11%)
  local copies, waits for them, and re-layouts  3.27 us (2%)
  waiting for transfers between devices  1.79 us (1%)
    all_to_all x1, blocking collectives, on_device(): lax.all_to_all(chosen, 'term', 0, 0, tiled=True)  54.9 us
    all_to_all x1, blocking collectives, on_device(): lax.all_to_all(copies, 'sector', 0, 0, axis_index_groups=same_core, tiled...  36.9 us
    all_to_all x1, blocking collectives, on_device(): lax.all_to_all(summed.reshape(GROUPS, PART, BLK), 'term', 0, 0, tiled=True)  17.7 us
    pallas_call x1, Pallas kernels, on_device(): pl.pallas_call(product_kernel, grid=(SLOTS,), out_shape=jax.ShapeDtypeStr...  11.2 us
    pallas_call x1, Pallas kernels, on_device(): pl.pallas_call(select_kernel, out_shape=jax.ShapeDtypeStruct((GROUPS * SL...  3.38 us
    unnamed x13, local copies, waits for them, and re-layouts  3.17 us
  transfers between devices with their start and end apart: 1, of which 1 were waited for; matrix products, arithmetic and copies ran while one was open for 1% of the time, Pallas kernels for 0%

profile of v2, /device:TPU:4, one launch (start us, length us, event | category | flops | bytes accessed | tf_op | source)
XLA Modules:
  0.0 130.1 jit_solution(9330432090028357338)
XLA Ops:
  0.0 0.0 copy-start
  0.0 1.0 copy-done
  1.0 0.1 broadcast_in_dim.12
  1.2 36.9 %all_to_all.15.own = bf16[16,64,512]{2,1,0:T(8,128)(2,1)S(1)} all-to-all(bf16[16,64,512]{2,1,0:T(8,128)(2,1)S(1)} %broadcast_in_dim.12), channel_id=1, replica_groups={{0,2,4,6,8,10,12,14,16,18,20,22,24,26,28,30},{1,3,5,7,9,11,13,15,17,19,..., dimensions={0} | all-to-all | bytes 2097152 | tf_op jit(solution)/shard_map/all_to_all | solution.py:94
  38.1 0.0 collective-permute-start
  38.1 0.8 copy.9.connect
  38.9 0.1 pad_add_fusion.where
  39.0 1.8 %collective-permute-done.other = bf16[16,64,512]{2,1,0:T(8,128)(2,1)S(1)} collective-permute-done((bf16[16,64,512]{2,1,0:T(8,128)(2,1)S(1)}, bf16[16,64,512]{2,1,0:T(8,128)(2,1)S(1)}, u32[]{:S(2)}, u32[]{:S(2)}) %collective-permute-start) | collective-permute-done | bytes 1048608 | tf_op jit(solution)/shard_map/ppermute | solution.py:95
  40.8 0.0 copy-start.3
  40.8 0.7 copy-done.3
  41.4 0.0 copy-start.4
  41.4 0.7 copy-done.4
  42.1 3.4 %shard_map.73 = bf16[64,64,512]{2,1,0:T(8,128)(2,1)S(1)} custom-call(s32[2]{0:T(128)S(1)} %pad_add_fusion.where, s32[64]{0:T(128)S(1)} %copy-done.3, s32[64,32]{1,0:T(8,128)S(1)} %copy.9.connect, s32[32]{0:T(128)S(1)} %copy-done.4, bf16[16,64,512]{2,1,0:T(8,128)(2,1)S(1)} %all_to_all.15.own, bf16[16,64,512]{2,1,0:T(8,128)(2,1)S(1)} %collective-permute-done.other), custom_call_target="tpu_custom_call" | custom-call | tf_op jit(solution)/shard_map/pallas_call | solution.py:96
  45.5 0.0 copy-start.1
  45.5 0.0 copy-start.2
  45.5 0.0 copy-start.5
  45.5 54.9 %all_to_all.16 = bf16[64,64,512]{2,1,0:T(8,128)(2,1)S(1)} all-to-all(bf16[64,64,512]{2,1,0:T(8,128)(2,1)S(1)} %shard_map.73), channel_id=1, replica_groups=mesh['term'=8,'sector'=32] {'term'}, dimensions={0} | all-to-all | bytes 8388608 | tf_op jit(solution)/shard_map/all_to_all | solution.py:104
  100.4 0.0 copy-done.1
  100.4 0.0 copy-done.2
  100.4 0.0 copy-done.5
  100.4 11.2 %shard_map.74 = f32[512,512]{1,0:T(8,128)S(1)} custom-call(s32[2]{0:T(128)S(1)} %pad_add_fusion.where, s32[64]{0:T(128)S(1)} %copy-done.3, s32[64,32]{1,0:T(8,128)S(1)} %copy.9.connect, s32[32]{0:T(128)S(1)} %copy-done.4, s32[32]{0:T(128)S(1)} %copy-done.5, bf16[8,8,64,512]{3,2,1,0:T(8,128)(2,1)S(1)} %bitcast.9, bf16[8,1,512,512]{3,2,1,0:T(8,128)(2,1)S(1)} %copy-done.1, ...), custom_call_target="tpu_custom_call" | custom-call | tf_op jit(solution)/shard_map/pallas_call | solution.py:105
  111.6 17.7 %all_to_all.17 = f32[8,64,512]{2,1,0:T(8,128)S(1)} all-to-all(f32[8,64,512]{2,1,0:T(8,128)S(1)} %bitcast.10), channel_id=1, replica_groups=mesh['term'=8,'sector'=32] {'term'}, dimensions={0} | all-to-all | bytes 2097152 | tf_op jit(solution)/shard_map/all_to_all | solution.py:119
  129.3 0.7 reduce_sum.9
  (1 shorter events, 0.0 us)
Async XLA Ops:
  0.0 1.0 copy-start
  38.1 2.7 %collective-permute-start = (bf16[16,64,512]{2,1,0:T(8,128)(2,1)S(1)}, bf16[16,64,512]{2,1,0:T(8,128)(2,1)S(1)}, u32[]{:S(2)}, u32[]{:S(2)}) collective-permute-start(bf16[16,64,512]{2,1,0:T(8,128)(2,1)S(1)} %all_to_all.15.own), channel_id=1, source_target_pairs={{0,1},{1,0},{2,3},{3,2},{4,5},{5,4},{6,7},{7,6},{8,9},{9,8},{10,11... | collective-permute-start | bytes 3145736 | tf_op jit(solution)/shard_map/ppermute | solution.py:95
  40.8 0.7 copy-start.3
  41.4 0.7 copy-start.4
  45.5 54.9 %copy-start.1 = (bf16[8,1,512,512]{3,2,1,0:T(8,128)(2,1)S(1)}, bf16[8,1,512,512]{3,2,1,0:T(8,128)(2,1)}, u32[]{:S(2)}) copy-start(bf16[8,1,512,512]{3,2,1,0:T(8,128)(2,1)} %left.1) | copy-start | bytes 12582916
  45.5 54.9 %copy-start.2 = (bf16[8,512,512]{2,1,0:T(8,128)(2,1)S(1)}, bf16[8,512,512]{2,1,0:T(8,128)(2,1)}, u32[]{:S(2)}) copy-start(bf16[8,512,512]{2,1,0:T(8,128)(2,1)} %right.1) | copy-start | bytes 12582916
  45.5 54.9 %copy-start.5 = (s32[32]{0:T(128)S(1)}, s32[32]{0:T(128)}, u32[]{:S(2)}) copy-start(s32[32]{0:T(128)} %sector_rows.1) | copy-start | bytes 388

commit v3 on v2

v3 whole, which is shorter than its diff:
```python
import functools

import jax
import jax.numpy as jnp
from jax import lax
from jax.experimental import pallas as pl
from jax.experimental.pallas import tpu as pltpu
from jax.sharding import PartitionSpec as P

GROUPS = 8
SLOTS = 8
PLACES = 32
BLK = 512
PEERS = 16
FRONT = 256
REST = BLK - FRONT
TALL = FRONT // 4
WIDE = BLK // 4
BOTH = ("term", "sector")
VMEM_LIMIT = 48 * 1024 * 1024


def flat(t, s):
    return t * PLACES + s


def place_of(h, z, c):
    return (h * 8 + z % 8) * 2 + c


def pairs(f):
    return [(flat(t, s), f(t, s)) for t in range(GROUPS) for s in range(PLACES)]


def ring_target(t, s):
    h, z, c = s // 16, s // 2 % 8, s % 2
    return flat(t, place_of(h, z + 1 - 2 * c, c))


FAR = pairs(lambda t, s: flat(t ^ 1, s ^ 16))
SWAP = pairs(lambda t, s: flat(t, s ^ 1))
RING = pairs(ring_target)
SAME_CORE = [[place_of(h, z, c) for h in range(2) for z in range(8)] for c in range(2)]
PEER_GROUPS = [
    [flat(t, place_of(h, z, c)) for t in range(GROUPS) for h in range(2)]
    for z in range(8)
    for c in range(2)
]


def index_kernel(term_order, connect, sector_at, sector_rows, front, mine, position):
    group, place = lax.axis_index("term"), lax.axis_index("sector")
    core = lax.rem(place, 2)
    half = lax.div(place, 16)
    z = lax.rem(lax.div(place, 2), 8)

    def put(p, carry):
        position[sector_at[p]] = p
        return carry

    lax.fori_loop(0, PLACES, put, 0)

    def note(k, carry):
        source = connect[sector_at[place], term_order[group * SLOTS + k]]
        p = position[source]
        step = lax.rem(lax.div(p, 2), 8) - z
        step = lax.rem(jnp.where(core == 0, -step, step) + 8, 8)
        mine[0, k] = step * 2 + jnp.where(lax.rem(p, 2) == core, 0, 1)
        mine[1, k] = jnp.where(lax.div(p, 16) == half, 0, 1)
        mine[2, k] = sector_rows[source]
        mine[3, k] = sector_rows[sector_at[place]]
        return carry

    lax.fori_loop(0, SLOTS, note, 0)

    def peer(m, carry):
        their_group = lax.div(m, 2)
        target = sector_at[lax.rem(m, 2) * 16 + lax.rem(place, 16)]

        def slot(k, carry):
            p = position[connect[target, term_order[their_group * SLOTS + k]]]
            front[m * SLOTS + k] = lax.div(p, 2) + jnp.where(lax.rem(p, 2) == core, 0, 16)
            return carry

        return lax.fori_loop(0, SLOTS, slot, carry)

    lax.fori_loop(0, PEERS, peer, 0)


def select_kernel(front, own, other, out):
    def slot(i, carry):
        at = front[i]

        @pl.when(at < 16)
        def _():
            out[i] = own[at]

        @pl.when(at >= 16)
        def _():
            out[i] = other[at - 16]

        return carry

    lax.fori_loop(0, PEERS * SLOTS, slot, 0, unroll=8)


def product_kernel(mine, front, left, right, *refs):
    blocks, (out, held, block, acc, sem) = refs[:PEERS], refs[PEERS:]
    k = pl.program_id(0)

    def fetch(j):
        for i, ref in enumerate(blocks):

            @pl.when(mine[0, j] == i)
            def _(ref=ref):
                slot = lax.rem(j, 2)
                pltpu.make_async_copy(ref.at[mine[1, j]], held.at[slot], sem.at[slot]).start()

    @pl.when(k == 0)
    def _():
        fetch(0)

    @pl.when(k < SLOTS - 1)
    def _():
        fetch(k + 1)

    now = lax.rem(k, 2)
    pltpu.make_async_copy(held.at[now], held.at[now], sem.at[now]).wait()
    live = mine[2, k]

    def rows(first, count):
        return lax.broadcasted_iota(jnp.int32, (count, BLK), 0) + first

    for m in range(PEERS):
        block[m // 4 * TALL : (m // 4 + 1) * TALL, m % 4 * WIDE : (m % 4 + 1) * WIDE] = front[m, 0]
    block[FRONT:, :] = held[now]
    b = block[...]
    b = jnp.where(rows(0, BLK) < live, b, jnp.zeros((), b.dtype))
    t = jnp.dot(b, right[0], preferred_element_type=jnp.float32)
    hi = t.astype(jnp.bfloat16)
    lo = (t - hi.astype(jnp.float32)).astype(jnp.bfloat16)
    part = jnp.dot(left[0, 0], hi, preferred_element_type=jnp.float32)
    part = part + jnp.dot(left[0, 0], lo, preferred_element_type=jnp.float32)

    @pl.when(k == 0)
    def _():
        acc[...] = part

    @pl.when(k > 0)
    def _():
        acc[...] += part

    @pl.when(k == SLOTS - 1)
    def _():
        out[...] = jnp.where(rows(0, BLK) < mine[3, 0], acc[...], 0.0).T


def on_device(psi, left_blocks, right_ops, sector_rows, connect, term_order, sector_at):
    group = lax.axis_index("term")
    smem = pl.BlockSpec(memory_space=pltpu.SMEM)
    vmem = pl.BlockSpec(memory_space=pltpu.VMEM)
    params = pltpu.CompilerParams(vmem_limit_bytes=VMEM_LIMIT)
    psi = psi[0]

    def hop(x, perm):
        return lax.ppermute(x, BOTH, perm)

    front_index, mine = pl.pallas_call(
        index_kernel,
        out_shape=(
            jax.ShapeDtypeStruct((PEERS * SLOTS,), jnp.int32),
            jax.ShapeDtypeStruct((4, SLOTS), jnp.int32),
        ),
        in_specs=[smem] * 4,
        out_specs=(smem, smem),
        scratch_shapes=[pltpu.SMEM((PLACES,), jnp.int32)],
        cost_estimate=pl.CostEstimate(flops=0, bytes_accessed=8 * 1024 * 1024, transcendentals=0),
    )(term_order, connect.T, sector_at, sector_rows)

    def chunk(h):
        m = group * 2 + h
        return lax.dynamic_slice(psi, (m // 4 * TALL, m % 4 * WIDE), (TALL, WIDE))

    copies = jnp.broadcast_to(jnp.stack([chunk(0), chunk(1)])[:, None], (2, 8, TALL, WIDE))
    own = lax.all_to_all(
        copies.reshape(PEERS, TALL, WIDE), "sector", 0, 0, axis_index_groups=SAME_CORE, tiled=True
    )
    own, front_index = lax.optimization_barrier((own, front_index))
    other = hop(own, SWAP)
    chosen = pl.pallas_call(
        select_kernel,
        out_shape=jax.ShapeDtypeStruct((PEERS * SLOTS, TALL, WIDE), psi.dtype),
        in_specs=[smem] + [vmem] * 2,
        out_specs=vmem,
        compiler_params=params,
    )(front_index, own, other)
    front = lax.all_to_all(chosen, BOTH, 0, 0, axis_index_groups=PEER_GROUPS, tiled=True)
    front = front.reshape(PEERS, SLOTS, TALL, WIDE)

    x = [jnp.stack([psi[FRONT:], hop(psi[FRONT:], FAR)])]
    y = [hop(x[0], SWAP)]
    for step in range(1, 5):
        x.append(hop(x[-1], RING))
        if step < 4:
            y.append(hop(y[-1], RING))
    x_swapped = [None] + [hop(v, SWAP) for v in x[1:]]
    y_swapped = [None] + [hop(v, SWAP) for v in y[1:]]
    blocks = []
    for step in range(4):
        blocks += [x[step], y[step]]
    blocks += [x[4], x_swapped[4]]
    for step in (3, 2, 1):
        blocks += [y_swapped[step], x_swapped[step]]

    summed = pl.pallas_call(
        product_kernel,
        out_shape=jax.ShapeDtypeStruct((BLK, BLK), jnp.float32),
        grid_spec=pltpu.PrefetchScalarGridSpec(
            num_scalar_prefetch=1,
            grid=(SLOTS,),
            in_specs=[
                pl.BlockSpec((PEERS, 1, TALL, WIDE), lambda k, mine: (0, k, 0, 0)),
                pl.BlockSpec((1, 1, BLK, BLK), lambda k, mine: (k, 0, 0, 0)),
                pl.BlockSpec((1, BLK, BLK), lambda k, mine: (k, 0, 0)),
            ]
            + [pl.BlockSpec(memory_space=pl.ANY)] * PEERS,
            out_specs=pl.BlockSpec((BLK, BLK), lambda k, mine: (0, 0)),
            scratch_shapes=[
                pltpu.VMEM((2, REST, BLK), jnp.bfloat16),
                pltpu.VMEM((BLK, BLK), jnp.bfloat16),
                pltpu.VMEM((BLK, BLK), jnp.float32),
                pltpu.SemaphoreType.DMA((2,)),
            ],
        ),
        compiler_params=params,
    )(mine, front, left_blocks, right_ops, *blocks)
    parts = lax.all_to_all(
        summed.reshape(GROUPS, BLK // GROUPS, BLK), "term", 0, 0, tiled=True
    )
    return jnp.sum(parts, axis=0).T[None]


def solution(mesh):
    placed = (
        P("sector", None, None),
        P("term", "sector", None, None),
        P("term", None, None),
        P(),
        P(),
        P(),
        P(),
    )
    return jax.shard_map(
        on_device, mesh=mesh, in_specs=placed, out_specs=P("sector", None, "term"), check_vma=False
    )
```

time: 131 us -> 108 us (0.82)
  blocking collectives: 110 us -> 21.8 us
  waiting for transfers between devices: 1.79 us -> 30.5 us
  starting transfers between devices: 0.01 us -> 26.2 us
  Pallas kernels: 14.6 us -> 21.9 us
  local copies, waits for them, and re-layouts: 3.27 us -> 6.67 us
    all_to_all x3 -> x1, blocking collectives: 110 us -> 21.8 us  [on_device(): lax.all_to_all(summed.reshape(GROUPS, BLK // GROUPS, BLK), 'term', 0, 0,...]
    ppermute x1 -> x17, waiting for transfers between devices: 1.79 us -> 26.9 us  [hop(): return lax.ppermute(x, BOTH, perm)]
    all_to_all x0 -> x2, starting transfers between devices: none -> 18.9 us  [the longest x1 11.4 us: on_device(): lax.all_to_all(copies.reshape(PEERS, TALL, WIDE), 'sector', 0, 0, axis_in...]
    ppermute x1 -> x17, starting transfers between devices: 0.01 us -> 7.35 us  [hop(): return lax.ppermute(x, BOTH, perm)]
    pallas_call x2 -> x3, Pallas kernels: 14.6 us -> 21.9 us  [the longest x1 13.6 us: on_device(): pl.pallas_call(product_kernel, out_shape=jax.ShapeDtypeStruct((BLK, BLK),...]
    all_to_all x0 -> x2, waiting for transfers between devices: none -> 3.57 us  [the longest x1 3.54 us: on_device(): lax.all_to_all(copies.reshape(PEERS, TALL, WIDE), 'sector', 0, 0, axis_in...]
    unnamed x13 -> x16, local copies, waits for them, and re-layouts: 3.17 us -> 4.2 us
  transfers between devices with their start and end apart: 1 -> 19, of which waited for: 1 -> 8; matrix products, arithmetic and copies ran while one was open for 1% -> 1% of each run, Pallas kernels for 0% -> 8%
where the time goes in v3:
time: 108 us
  waiting for transfers between devices  30.5 us (28%)
  starting transfers between devices  26.2 us (24%)
  Pallas kernels  21.9 us (20%)
  blocking collectives  21.8 us (20%)
  local copies, waits for them, and re-layouts  6.67 us (6%)
    ppermute x17, waiting for transfers between devices, hop(): return lax.ppermute(x, BOTH, perm)  26.9 us
    all_to_all x1, blocking collectives, on_device(): lax.all_to_all(summed.reshape(GROUPS, BLK // GROUPS, BLK), 'term', 0, 0,...  21.8 us
    pallas_call x1, Pallas kernels, on_device(): pl.pallas_call(product_kernel, out_shape=jax.ShapeDtypeStruct((BLK, BLK),...  13.6 us
    all_to_all x1, starting transfers between devices, on_device(): lax.all_to_all(copies.reshape(PEERS, TALL, WIDE), 'sector', 0, 0, axis_in...  11.4 us
    all_to_all x1, starting transfers between devices, on_device(): lax.all_to_all(chosen, BOTH, 0, 0, axis_index_groups=PEER_GROUPS, tiled=T...  7.45 us
    ppermute x17, starting transfers between devices, hop(): return lax.ppermute(x, BOTH, perm)  7.35 us
    pallas_call x1, Pallas kernels, on_device(): pl.pallas_call(index_kernel, out_shape=(jax.ShapeDtypeStruct((PEERS * SLO...  4.65 us
    unnamed x16, local copies, waits for them, and re-layouts  4.2 us
  transfers between devices with their start and end apart: 19, of which 8 were waited for; matrix products, arithmetic and copies ran while one was open for 1% of the time, Pallas kernels for 8%

profile of v3, /device:TPU:4, one launch (start us, length us, event | category | flops | bytes accessed | tf_op | source)
XLA Modules:
  0.0 107.9 jit_solution(13312580882523177971)
XLA Ops:
  0.0 1.0 fusion
  1.0 0.6 collective-permute-start.1
  1.6 0.7 constant_dynamic-slice_fusion.1
  2.4 0.8 broadcast_in_dim.4
  3.1 11.4 %all-to-all-start = ((bf16[16,64,128]{2,1,0:T(8,128)(2,1)}), bf16[16,64,128]{2,1,0:T(8,128)(2,1)S(1)}, u32[]{:S(2)}, u32[]{:S(2)}) async-start(bf16[16,64,128]{2,1,0:T(8,128)(2,1)} %bitcast.1), calls=%async_computation | async-start | bytes 524288 | tf_op jit(solution)/shard_map/all_to_all | solution.py:185
  14.6 0.0 collective-permute-done.1
  14.6 0.1 pad_maximum_fusion.refs_0_
  14.6 1.5 %collective-permute-start.3 = (bf16[2,256,512]{2,1,0:T(8,128)(2,1)S(1)}, bf16[2,256,512]{2,1,0:T(8,128)(2,1)S(1)}, u32[]{:S(2)}, u32[]{:S(2)}) collective-permute-start(bf16[2,256,512]{2,1,0:T(8,128)(2,1)S(1)} %pad_maximum_fusion.refs_0_), channel_id=1, source_target_pairs={{0,2},{1,15},{2,4},{3,1},{4,6},{5,3},{6,8},{7,5},{8,10},{9,7},{10,... | collective-permute-start | bytes 1572872 | tf_op jit(solution)/shard_map/ppermute | solution.py:166
  16.2 4.7 %shard_map.73 = (s32[128]{0:T(128)}, s32[4,8]{1,0:T(4,128)}) custom-call(s32[64]{0:T(128)} %term_order.1, s32[32,64]{1,0:T(8,128)} %bitcast.12, s32[32]{0:T(128)} %sector_at.1, s32[32]{0:T(128)} %sector_rows.1), custom_call_target="tpu_custom_call" | custom-call | bytes 8388608 | tf_op jit(solution)/shard_map/pallas_call | solution.py:168
  20.8 0.0 copy-start.2
  20.8 3.5 %all-to-all-done.own = bf16[16,64,128]{2,1,0:T(8,128)(2,1)S(1)} async-done(((bf16[16,64,128]{2,1,0:T(8,128)(2,1)}), bf16[16,64,128]{2,1,0:T(8,128)(2,1)S(1)}, u32[]{:S(2)}, u32[]{:S(2)}) %all-to-all-start) | async-done | bytes 262176 | tf_op jit(solution)/shard_map/all_to_all | solution.py:185
  24.4 0.0 collective-permute-start
  24.4 4.2 %collective-permute-done.3.refs_2_ = bf16[2,256,512]{2,1,0:T(8,128)(2,1)S(1)} collective-permute-done((bf16[2,256,512]{2,1,0:T(8,128)(2,1)S(1)}, bf16[2,256,512]{2,1,0:T(8,128)(2,1)S(1)}, u32[]{:S(2)}, u32[]{:S(2)}) %collective-permute-start.3) | collective-permute-done | bytes 524320 | tf_op jit(solution)/shard_map/ppermute | solution.py:166
  28.5 0.0 collective-permute-start.5
  28.5 0.0 collective-permute-done.2.refs_1_
  28.5 0.8 collective-permute-start.4
  29.3 0.0 collective-permute-done.other
  29.3 0.7 copy-done.3
  30.0 3.7 %shard_map.74 = bf16[128,64,128]{2,1,0:T(8,128)(2,1)} custom-call(s32[128]{0:T(128)S(1)} %copy-done.3, bf16[16,64,128]{2,1,0:T(8,128)(2,1)S(1)} %all-to-all-done.own, bf16[16,64,128]{2,1,0:T(8,128)(2,1)S(1)} %collective-permute-done.other), custom_call_target="tpu_custom_call" | custom-call | tf_op jit(solution)/shard_map/pallas_call | solution.py:190
  33.6 7.4 %all-to-all-start.1 = ((bf16[128,64,128]{2,1,0:T(8,128)(2,1)}), bf16[128,64,128]{2,1,0:T(8,128)(2,1)}, u32[]{:S(2)}, u32[]{:S(2)}) async-start(bf16[128,64,128]{2,1,0:T(8,128)(2,1)} %shard_map.74), calls=%async_computation.1 | async-start | bytes 4194304 | tf_op jit(solution)/shard_map/all_to_all | solution.py:197
  41.1 0.0 collective-permute-done.5.refs_4_
  41.1 1.5 %collective-permute-start.7 = (bf16[2,256,512]{2,1,0:T(8,128)(2,1)S(1)}, bf16[2,256,512]{2,1,0:T(8,128)(2,1)S(1)}, u32[]{:S(2)}, u32[]{:S(2)}) collective-permute-start(bf16[2,256,512]{2,1,0:T(8,128)(2,1)S(1)} %collective-permute-done.5.refs_4_), channel_id=1, source_target_pairs={{0,2},{1,15},{2,4},{3,1},{4,6},{5,3},{6,8},{7,5},{8,10},{9,7},{10,... | collective-permute-start | bytes 1572872 | tf_op jit(solution)/shard_map/ppermute | solution.py:166
  42.6 1.9 %collective-permute-done.4.refs_3_ = bf16[2,256,512]{2,1,0:T(8,128)(2,1)S(1)} collective-permute-done((bf16[2,256,512]{2,1,0:T(8,128)(2,1)S(1)}, bf16[2,256,512]{2,1,0:T(8,128)(2,1)S(1)}, u32[]{:S(2)}, u32[]{:S(2)}) %collective-permute-start.4) | collective-permute-done | bytes 524320 | tf_op jit(solution)/shard_map/ppermute | solution.py:166
  44.5 0.8 collective-permute-start.6
  45.3 0.0 collective-permute-start.16
  45.3 0.5 collective-permute-start.14
  45.8 5.8 %collective-permute-done.7.refs_6_ = bf16[2,256,512]{2,1,0:T(8,128)(2,1)S(1)} collective-permute-done((bf16[2,256,512]{2,1,0:T(8,128)(2,1)S(1)}, bf16[2,256,512]{2,1,0:T(8,128)(2,1)S(1)}, u32[]{:S(2)}, u32[]{:S(2)}) %collective-permute-start.7) | collective-permute-done | bytes 524320 | tf_op jit(solution)/shard_map/ppermute | solution.py:166
  51.6 0.4 collective-permute-start.9
  52.0 5.2 %collective-permute-done.6.refs_5_ = bf16[2,256,512]{2,1,0:T(8,128)(2,1)S(1)} collective-permute-done((bf16[2,256,512]{2,1,0:T(8,128)(2,1)S(1)}, bf16[2,256,512]{2,1,0:T(8,128)(2,1)S(1)}, u32[]{:S(2)}, u32[]{:S(2)}) %collective-permute-start.6) | collective-permute-done | bytes 524320 | tf_op jit(solution)/shard_map/ppermute | solution.py:166
  57.2 0.4 collective-permute-start.8
  57.6 0.2 collective-permute-start.15
  57.8 0.0 collective-permute-done.16.refs_15_
  57.8 0.3 collective-permute-start.12
  58.1 0.0 collective-permute-done.14.refs_13_
  58.1 0.2 collective-permute-start.13
  58.4 0.8 copy-done
  59.1 3.8 %collective-permute-done.9.refs_8_ = bf16[2,256,512]{2,1,0:T(8,128)(2,1)} collective-permute-done((bf16[2,256,512]{2,1,0:T(8,128)(2,1)S(1)}, bf16[2,256,512]{2,1,0:T(8,128)(2,1)}, u32[]{:S(2)}, u32[]{:S(2)}) %collective-permute-start.9) | collective-permute-done | bytes 524320 | tf_op jit(solution)/shard_map/ppermute | solution.py:166
  62.9 5.6 %collective-permute-done.8.refs_7_ = bf16[2,256,512]{2,1,0:T(8,128)(2,1)} collective-permute-done((bf16[2,256,512]{2,1,0:T(8,128)(2,1)S(1)}, bf16[2,256,512]{2,1,0:T(8,128)(2,1)}, u32[]{:S(2)}, u32[]{:S(2)}) %collective-permute-start.8) | collective-permute-done | bytes 524320 | tf_op jit(solution)/shard_map/ppermute | solution.py:166
  68.5 0.0 collective-permute-done.15.refs_14_
  68.5 0.0 collective-permute-done.12.refs_11_
  68.6 0.8 copy-done.6
  69.4 0.9 copy-done.7
  70.3 0.0 all-to-all-done.1
  70.3 0.5 collective-permute-done.11.refs_10_
  70.8 1.0 copy-done.1
  71.8 13.6 %shard_map.75 = f32[512,512]{1,0:T(8,128)} custom-call(s32[4,8]{1,0:T(4,128)S(1)} %copy-done.2, bf16[16,8,64,128]{3,2,1,0:T(8,128)(2,1)} %bitcast.2.front, bf16[8,1,512,512]{3,2,1,0:T(8,128)(2,1)} %left.1, bf16[8,512,512]{2,1,0:T(8,128)(2,1)} %right.1, bf16[2,256,512]{2,1,0:T(8,128)(2,1)S(1)} %pad_maximum_fusion.refs_0_, ...), custom_call_target="tpu_custom_call" | custom-call | tf_op jit(solution)/shard_map/pallas_call | solution.py:215
  85.4 21.8 %all_to_all.15 = f32[8,64,512]{2,1,0:T(8,128)S(1)} all-to-all(f32[8,64,512]{2,1,0:T(8,128)} %bitcast.10), channel_id=1, replica_groups=mesh['term'=8,'sector'=32] {'term'}, dimensions={0} | all-to-all | bytes 2097152 | tf_op jit(solution)/shard_map/all_to_all | solution.py:237
  107.1 0.7 reduce_sum.9
  (16 shorter events, 0.0 us)
Async XLA Ops:
  1.0 13.6 %collective-permute-start.1 = (bf16[256,512]{1,0:T(8,128)(2,1)S(1)}, bf16[256,512]{1,0:T(8,128)(2,1)S(1)}, u32[]{:S(2)}, u32[]{:S(2)}) collective-permute-start(bf16[256,512]{1,0:T(8,128)(2,1)S(1)} %get-tuple-element.14), channel_id=1, source_target_pairs={{0,48},{1,49},{2,50},{3,51},{4,52},{5,53},{6,54},{7,55},{8,56},{9,... | collective-permute-start | bytes 786440 | tf_op jit(solution)/shard_map/ppermute | solution.py:166
  3.1 21.3 %all-to-all-start = ((bf16[16,64,128]{2,1,0:T(8,128)(2,1)}), bf16[16,64,128]{2,1,0:T(8,128)(2,1)S(1)}, u32[]{:S(2)}, u32[]{:S(2)}) async-start(bf16[16,64,128]{2,1,0:T(8,128)(2,1)} %bitcast.1), calls=%async_computation | async-start | bytes 524288 | tf_op jit(solution)/shard_map/all_to_all | solution.py:185
  14.6 13.9 %collective-permute-start.3 = (bf16[2,256,512]{2,1,0:T(8,128)(2,1)S(1)}, bf16[2,256,512]{2,1,0:T(8,128)(2,1)S(1)}, u32[]{:S(2)}, u32[]{:S(2)}) collective-permute-start(bf16[2,256,512]{2,1,0:T(8,128)(2,1)S(1)} %pad_maximum_fusion.refs_0_), channel_id=1, source_target_pairs={{0,2},{1,15},{2,4},{3,1},{4,6},{5,3},{6,8},{7,5},{8,10},{9,7},{10,... | collective-permute-start | bytes 1572872 | tf_op jit(solution)/shard_map/ppermute | solution.py:166
  16.2 12.4 %collective-permute-start.2 = (bf16[2,256,512]{2,1,0:T(8,128)(2,1)S(1)}, bf16[2,256,512]{2,1,0:T(8,128)(2,1)S(1)}, u32[]{:S(2)}, u32[]{:S(2)}) collective-permute-start(bf16[2,256,512]{2,1,0:T(8,128)(2,1)S(1)} %pad_maximum_fusion.refs_0_), channel_id=1, source_target_pairs={{0,1},{1,0},{2,3},{3,2},{4,5},{5,4},{6,7},{7,6},{8,9},{9,8},{10,11... | collective-permute-start | bytes 1572872 | tf_op jit(solution)/shard_map/ppermute | solution.py:166
  20.8 50.0 %copy-start.2 = (s32[4,8]{1,0:T(4,128)S(1)}, s32[4,8]{1,0:T(4,128)}, u32[]{:S(2)}) copy-start(s32[4,8]{1,0:T(4,128)} %get-tuple-element.9.mine) | copy-start | bytes 388
  24.4 5.0 %collective-permute-start = (bf16[16,64,128]{2,1,0:T(8,128)(2,1)S(1)}, bf16[16,64,128]{2,1,0:T(8,128)(2,1)S(1)}, u32[]{:S(2)}, u32[]{:S(2)}) collective-permute-start(bf16[16,64,128]{2,1,0:T(8,128)(2,1)S(1)} %all-to-all-done.own), channel_id=1, source_target_pairs={{0,1},{1,0},{2,3},{3,2},{4,5},{5,4},{6,7},{7,6},{8,9},{9,8},{10,11... | collective-permute-start | bytes 786440 | tf_op jit(solution)/shard_map/ppermute | solution.py:166
  28.5 12.6 %collective-permute-start.5 = (bf16[2,256,512]{2,1,0:T(8,128)(2,1)S(1)}, bf16[2,256,512]{2,1,0:T(8,128)(2,1)S(1)}, u32[]{:S(2)}, u32[]{:S(2)}) collective-permute-start(bf16[2,256,512]{2,1,0:T(8,128)(2,1)S(1)} %collective-permute-done.3.refs_2_), channel_id=1, source_target_pairs={{0,2},{1,15},{2,4},{3,1},{4,6},{5,3},{6,8},{7,5},{8,10},{9,7},{10,... | collective-permute-start | bytes 1572872 | tf_op jit(solution)/shard_map/ppermute | solution.py:166
  28.5 16.0 %collective-permute-start.4 = (bf16[2,256,512]{2,1,0:T(8,128)(2,1)S(1)}, bf16[2,256,512]{2,1,0:T(8,128)(2,1)S(1)}, u32[]{:S(2)}, u32[]{:S(2)}) collective-permute-start(bf16[2,256,512]{2,1,0:T(8,128)(2,1)S(1)} %collective-permute-done.2.refs_1_), channel_id=1, source_target_pairs={{0,2},{1,15},{2,4},{3,1},{4,6},{5,3},{6,8},{7,5},{8,10},{9,7},{10,... | collective-permute-start | bytes 1572872 | tf_op jit(solution)/shard_map/ppermute | solution.py:166
  29.3 0.7 copy-start.3
  33.6 36.7 %all-to-all-start.1 = ((bf16[128,64,128]{2,1,0:T(8,128)(2,1)}), bf16[128,64,128]{2,1,0:T(8,128)(2,1)}, u32[]{:S(2)}, u32[]{:S(2)}) async-start(bf16[128,64,128]{2,1,0:T(8,128)(2,1)} %shard_map.74), calls=%async_computation.1 | async-start | bytes 4194304 | tf_op jit(solution)/shard_map/all_to_all | solution.py:197
  41.1 10.5 %collective-permute-start.7 = (bf16[2,256,512]{2,1,0:T(8,128)(2,1)S(1)}, bf16[2,256,512]{2,1,0:T(8,128)(2,1)S(1)}, u32[]{:S(2)}, u32[]{:S(2)}) collective-permute-start(bf16[2,256,512]{2,1,0:T(8,128)(2,1)S(1)} %collective-permute-done.5.refs_4_), channel_id=1, source_target_pairs={{0,2},{1,15},{2,4},{3,1},{4,6},{5,3},{6,8},{7,5},{8,10},{9,7},{10,... | collective-permute-start | bytes 1572872 | tf_op jit(solution)/shard_map/ppermute | solution.py:166
  44.5 12.6 %collective-permute-start.6 = (bf16[2,256,512]{2,1,0:T(8,128)(2,1)S(1)}, bf16[2,256,512]{2,1,0:T(8,128)(2,1)S(1)}, u32[]{:S(2)}, u32[]{:S(2)}) collective-permute-start(bf16[2,256,512]{2,1,0:T(8,128)(2,1)S(1)} %collective-permute-done.4.refs_3_), channel_id=1, source_target_pairs={{0,2},{1,15},{2,4},{3,1},{4,6},{5,3},{6,8},{7,5},{8,10},{9,7},{10,... | collective-permute-start | bytes 1572872 | tf_op jit(solution)/shard_map/ppermute | solution.py:166
  45.3 12.5 %collective-permute-start.16 = (bf16[2,256,512]{2,1,0:T(8,128)(2,1)S(1)}, bf16[2,256,512]{2,1,0:T(8,128)(2,1)S(1)}, u32[]{:S(2)}, u32[]{:S(2)}) collective-permute-start(bf16[2,256,512]{2,1,0:T(8,128)(2,1)S(1)} %collective-permute-done.3.refs_2_), channel_id=1, source_target_pairs={{0,1},{1,0},{2,3},{3,2},{4,5},{5,4},{6,7},{7,6},{8,9},{9,8},{10,11... | collective-permute-start | bytes 1572872 | tf_op jit(solution)/shard_map/ppermute | solution.py:166
  45.3 12.8 %collective-permute-start.14 = (bf16[2,256,512]{2,1,0:T(8,128)(2,1)S(1)}, bf16[2,256,512]{2,1,0:T(8,128)(2,1)S(1)}, u32[]{:S(2)}, u32[]{:S(2)}) collective-permute-start(bf16[2,256,512]{2,1,0:T(8,128)(2,1)S(1)} %collective-permute-done.5.refs_4_), channel_id=1, source_target_pairs={{0,1},{1,0},{2,3},{3,2},{4,5},{5,4},{6,7},{7,6},{8,9},{9,8},{10,11... | collective-permute-start | bytes 1572872 | tf_op jit(solution)/shard_map/ppermute | solution.py:166
  51.6 11.3 %collective-permute-start.9 = (bf16[2,256,512]{2,1,0:T(8,128)(2,1)S(1)}, bf16[2,256,512]{2,1,0:T(8,128)(2,1)}, u32[]{:S(2)}, u32[]{:S(2)}) collective-permute-start(bf16[2,256,512]{2,1,0:T(8,128)(2,1)S(1)} %collective-permute-done.7.refs_6_), channel_id=1, source_target_pairs={{0,2},{1,15},{2,4},{3,1},{4,6},{5,3},{6,8},{7,5},{8,10},{9,7},{10,... | collective-permute-start | bytes 1572872 | tf_op jit(solution)/shard_map/ppermute | solution.py:166
  57.2 11.3 %collective-permute-start.8 = (bf16[2,256,512]{2,1,0:T(8,128)(2,1)S(1)}, bf16[2,256,512]{2,1,0:T(8,128)(2,1)}, u32[]{:S(2)}, u32[]{:S(2)}) collective-permute-start(bf16[2,256,512]{2,1,0:T(8,128)(2,1)S(1)} %collective-permute-done.6.refs_5_), channel_id=1, source_target_pairs={{0,2},{1,15},{2,4},{3,1},{4,6},{5,3},{6,8},{7,5},{8,10},{9,7},{10,... | collective-permute-start | bytes 1572872 | tf_op jit(solution)/shard_map/ppermute | solution.py:166
  57.6 10.9 %collective-permute-start.15 = (bf16[2,256,512]{2,1,0:T(8,128)(2,1)S(1)}, bf16[2,256,512]{2,1,0:T(8,128)(2,1)S(1)}, u32[]{:S(2)}, u32[]{:S(2)}) collective-permute-start(bf16[2,256,512]{2,1,0:T(8,128)(2,1)S(1)} %collective-permute-done.4.refs_3_), channel_id=1, source_target_pairs={{0,1},{1,0},{2,3},{3,2},{4,5},{5,4},{6,7},{7,6},{8,9},{9,8},{10,11... | collective-permute-start | bytes 1572872 | tf_op jit(solution)/shard_map/ppermute | solution.py:166
  57.8 10.7 %copy-start.4 = (bf16[2,256,512]{2,1,0:T(8,128)(2,1)}, bf16[2,256,512]{2,1,0:T(8,128)(2,1)S(1)}, u32[]{:S(2)}) copy-start(bf16[2,256,512]{2,1,0:T(8,128)(2,1)S(1)} %collective-permute-done.16.refs_15_) | copy-start | bytes 1572868
  57.8 10.7 %collective-permute-start.12 = (bf16[2,256,512]{2,1,0:T(8,128)(2,1)S(1)}, bf16[2,256,512]{2,1,0:T(8,128)(2,1)S(1)}, u32[]{:S(2)}, u32[]{:S(2)}) collective-permute-start(bf16[2,256,512]{2,1,0:T(8,128)(2,1)S(1)} %collective-permute-done.7.refs_6_), channel_id=1, source_target_pairs={{0,1},{1,0},{2,3},{3,2},{4,5},{5,4},{6,7},{7,6},{8,9},{9,8},{10,11... | collective-permute-start | bytes 1572872 | tf_op jit(solution)/shard_map/ppermute | solution.py:166
  58.1 10.4 %copy-start.5 = (bf16[2,256,512]{2,1,0:T(8,128)(2,1)}, bf16[2,256,512]{2,1,0:T(8,128)(2,1)S(1)}, u32[]{:S(2)}) copy-start(bf16[2,256,512]{2,1,0:T(8,128)(2,1)S(1)} %collective-permute-done.14.refs_13_) | copy-start | bytes 1572868
  58.1 12.1 %collective-permute-start.13 = (bf16[2,256,512]{2,1,0:T(8,128)(2,1)S(1)}, bf16[2,256,512]{2,1,0:T(8,128)(2,1)}, u32[]{:S(2)}, u32[]{:S(2)}) collective-permute-start(bf16[2,256,512]{2,1,0:T(8,128)(2,1)S(1)} %collective-permute-done.6.refs_5_), channel_id=1, source_target_pairs={{0,1},{1,0},{2,3},{3,2},{4,5},{5,4},{6,7},{7,6},{8,9},{9,8},{10,11... | collective-permute-start | bytes 1572872 | tf_op jit(solution)/shard_map/ppermute | solution.py:166
  58.4 0.8 copy-start
  62.9 7.4 %collective-permute-start.10 = (bf16[2,256,512]{2,1,0:T(8,128)(2,1)}, bf16[2,256,512]{2,1,0:T(8,128)(2,1)}, u32[]{:S(2)}, u32[]{:S(2)}) collective-permute-start(bf16[2,256,512]{2,1,0:T(8,128)(2,1)} %collective-permute-done.9.refs_8_), channel_id=1, source_target_pairs={{0,1},{1,0},{2,3},{3,2},{4,5},{5,4},{6,7},{7,6},{8,9},{9,8},{10,11... | collective-permute-start | bytes 1572872 | tf_op jit(solution)/shard_map/ppermute | solution.py:166
  68.5 2.3 %collective-permute-start.11 = (bf16[2,256,512]{2,1,0:T(8,128)(2,1)}, bf16[2,256,512]{2,1,0:T(8,128)(2,1)}, u32[]{:S(2)}, u32[]{:S(2)}) collective-permute-start(bf16[2,256,512]{2,1,0:T(8,128)(2,1)} %collective-permute-done.8.refs_7_), channel_id=1, source_target_pairs={{0,1},{1,0},{2,3},{3,2},{4,5},{5,4},{6,7},{7,6},{8,9},{9,8},{10,11... | collective-permute-start | bytes 1572872 | tf_op jit(solution)/shard_map/ppermute | solution.py:166
  68.5 0.9 copy-start.6
  69.4 0.9 copy-start.7
  70.8 1.0 copy-start.1

commit v4 on v3

v4 whole, which is shorter than its diff:
```python
import functools

import jax
import jax.numpy as jnp
from jax import lax
from jax.experimental import pallas as pl
from jax.experimental.pallas import tpu as pltpu
from jax.sharding import PartitionSpec as P

GROUPS = 8
SLOTS = 8
PLACES = 32
BLK = 512
PEERS = 16
FRONT = 256
REST = BLK - FRONT
PART = FRONT // PEERS
BOTH = ("term", "sector")
LN2 = 0.6931471805599453
LEVELS = 64.0
STEPS = 32766.0
VMEM_LIMIT = 48 * 1024 * 1024


def flat(t, s):
    return t * PLACES + s


def place_of(h, z, c):
    return (h * 8 + z % 8) * 2 + c


def pairs(f):
    return [(flat(t, s), f(t, s)) for t in range(GROUPS) for s in range(PLACES)]


def ring_target(t, s):
    h, z, c = s // 16, s // 2 % 8, s % 2
    return flat(t, place_of(h, z + 1 - 2 * c, c))


FAR = pairs(lambda t, s: flat(t ^ 1, s ^ 16))
SWAP = pairs(lambda t, s: flat(t, s ^ 1))
RING = pairs(ring_target)
SAME_CORE = [[place_of(h, z, c) for h in range(2) for z in range(8)] for c in range(2)]
PEER_GROUPS = [
    [flat(t, place_of(h, z, c)) for t in range(GROUPS) for h in range(2)]
    for z in range(8)
    for c in range(2)
]


def index_kernel(term_order, connect, sector_at, sector_rows, front, mine, position):
    group, place = lax.axis_index("term"), lax.axis_index("sector")
    core = lax.rem(place, 2)
    half = lax.div(place, 16)
    z = lax.rem(lax.div(place, 2), 8)

    def put(p, carry):
        position[sector_at[p]] = p
        return carry

    lax.fori_loop(0, PLACES, put, 0)

    def note(k, carry):
        source = connect[sector_at[place], term_order[group * SLOTS + k]]
        p = position[source]
        step = lax.rem(lax.div(p, 2), 8) - z
        step = lax.rem(jnp.where(core == 0, -step, step) + 8, 8)
        side = jnp.where(lax.div(p, 16) == half, 0, 1)
        parity = jnp.where(lax.rem(p, 2) == core, 0, 1)
        mine[0, k] = step * 2 + parity
        mine[1, k] = side
        mine[2, k] = sector_rows[source]
        mine[3, k] = sector_rows[sector_at[place]]
        return carry

    lax.fori_loop(0, SLOTS, note, 0)

    def peer(m, carry):
        their_group = lax.div(m, 2)
        target = sector_at[lax.rem(m, 2) * 16 + lax.rem(place, 16)]

        def slot(k, carry):
            p = position[connect[target, term_order[their_group * SLOTS + k]]]
            front[m * SLOTS + k] = lax.div(p, 2) + jnp.where(lax.rem(p, 2) == core, 0, 16)
            return carry

        return lax.fori_loop(0, SLOTS, slot, carry)

    lax.fori_loop(0, PEERS, peer, 0)


def select_kernel(front, own, other, out, held, sem):
    def peer(m, carry):
        for k in range(SLOTS):
            at = front[m * SLOTS + k]

            @pl.when(at < 16)
            def _(k=k, at=at):
                held[m, k] = own[at]

            @pl.when(at >= 16)
            def _(k=k, at=at):
                held[m, k] = other[at - 16]

        pltpu.make_async_copy(held.at[m], out.at[m], sem).start()
        return carry

    lax.fori_loop(0, PEERS, peer, 0)
    pltpu.make_async_copy(held, out, sem).wait()


def product_kernel(mine, front, left, right, *refs):
    blocks, refs = refs[:PEERS], refs[PEERS:]
    out, fronts, rests, lefts, rights, block, acc, front_sem, rest_sem, left_sem, right_sem = refs

    def fetch(j, carry):
        pltpu.make_async_copy(right.at[j], rights.at[j], right_sem.at[j]).start()
        pltpu.make_async_copy(front.at[:, j], fronts.at[j], front_sem.at[j]).start()
        for i, ref in enumerate(blocks):

            @pl.when(mine[0, j] == i)
            def _(ref=ref):
                pltpu.make_async_copy(ref.at[mine[1, j]], rests.at[j], rest_sem.at[j]).start()

        pltpu.make_async_copy(left.at[j, 0], lefts.at[j], left_sem.at[j]).start()
        return carry

    lax.fori_loop(0, SLOTS, fetch, 0)

    def arrived(buffer, sem, k):
        pltpu.make_async_copy(buffer.at[k], buffer.at[k], sem.at[k]).wait()
        return buffer[k]

    def dot(a, b):
        return jnp.dot(a, b, preferred_element_type=jnp.float32)

    rows = lax.broadcasted_iota(jnp.int32, (BLK, BLK), 0)
    for k in range(SLOTS):
        block[k % 2, :FRONT] = arrived(fronts, front_sem, k).reshape(FRONT, BLK)
        block[k % 2, FRONT:] = arrived(rests, rest_sem, k)
        t = dot(block[k % 2], arrived(rights, right_sem, k))
        t = jnp.where(rows < mine[2, k], t, 0.0)
        hi = t.astype(jnp.bfloat16)
        lo = (t - hi.astype(jnp.float32)).astype(jnp.bfloat16)
        left_k = arrived(lefts, left_sem, k)
        part = dot(left_k, hi) + dot(left_k, lo)
        if k == 0:
            acc[...] = part
        else:
            acc[...] += part
    total = jnp.where(rows < mine[3, 0], acc[...], 0.0).T
    largest = jnp.maximum(jnp.max(jnp.abs(total), axis=1, keepdims=True), 1e-30)
    level = jnp.ceil(jnp.log(largest) * (LEVELS / LN2)) + 1.0
    steps = total * (STEPS * jnp.exp(level * (-LN2 / LEVELS)))
    out[:, :BLK] = jnp.round(steps).astype(jnp.int32).astype(jnp.int16)
    out[:, BLK:] = jnp.broadcast_to(level, (BLK, 128)).astype(jnp.int32).astype(jnp.int16)


def total_kernel(parts, out):
    total = None
    for g in range(GROUPS):
        level = parts[g, :, BLK:].astype(jnp.int32).astype(jnp.float32)[:, :1]
        size = jnp.exp(level * (LN2 / LEVELS)) * (1.0 / STEPS)
        part = parts[g, :, :BLK].astype(jnp.int32).astype(jnp.float32) * size
        total = part if total is None else total + part
    out[...] = total


def on_device(psi, left_blocks, right_ops, sector_rows, connect, term_order, sector_at):
    group = lax.axis_index("term")
    smem = pl.BlockSpec(memory_space=pltpu.SMEM)
    vmem = pl.BlockSpec(memory_space=pltpu.VMEM)
    anywhere = pl.BlockSpec(memory_space=pl.ANY)
    params = pltpu.CompilerParams(vmem_limit_bytes=VMEM_LIMIT)
    psi = psi[0]

    def hop(x, perm):
        return lax.ppermute(x, BOTH, perm)

    front_index, mine = pl.pallas_call(
        index_kernel,
        out_shape=(
            jax.ShapeDtypeStruct((PEERS * SLOTS,), jnp.int32),
            jax.ShapeDtypeStruct((4, SLOTS), jnp.int32),
        ),
        in_specs=[smem] * 4,
        out_specs=(smem, smem),
        scratch_shapes=[pltpu.SMEM((PLACES,), jnp.int32)],
        cost_estimate=pl.CostEstimate(flops=0, bytes_accessed=8 * 1024 * 1024, transcendentals=0),
    )(term_order, connect.T, sector_at, sector_rows)

    def after(x, y):
        return lax.optimization_barrier((x, y))[0]

    x = [jnp.stack([psi[FRONT:], hop(psi[FRONT:], FAR)])]
    y = [hop(x[0], SWAP)]
    pieces = lax.dynamic_slice(psi, (group * 2 * PART, 0), (2 * PART, BLK)).reshape(2, 1, PART, BLK)
    copies = jnp.broadcast_to(pieces, (2, PLACES // 4, PART, BLK)).reshape(PEERS, PART, BLK)
    own = lax.all_to_all(copies, "sector", 0, 0, axis_index_groups=SAME_CORE, tiled=True)
    own = after(own, front_index)
    other = hop(own, SWAP)
    chosen = pl.pallas_call(
        select_kernel,
        out_shape=pltpu.HBM((PEERS, SLOTS, PART, BLK), psi.dtype),
        in_specs=[smem] + [vmem] * 2,
        out_specs=anywhere,
        scratch_shapes=[
            pltpu.VMEM((PEERS, SLOTS, PART, BLK), psi.dtype),
            pltpu.SemaphoreType.DMA,
        ],
        cost_estimate=pl.CostEstimate(flops=0, bytes_accessed=8 * 1024 * 1024, transcendentals=0),
        compiler_params=params,
    )(front_index, own, other)
    front = lax.all_to_all(chosen, BOTH, 0, 0, axis_index_groups=PEER_GROUPS, tiled=True)
    for step in range(1, 5):
        x.append(hop(x[-1], RING))
        if step < 4:
            y.append(hop(y[-1], RING))
    x_swapped = [None] + [hop(v, SWAP) for v in x[1:]]
    y_swapped = [None] + [hop(v, SWAP) for v in y[1:]]
    blocks = []
    for step in range(4):
        blocks += [x[step], y[step]]
    blocks += [x[4], x_swapped[4]]
    for step in (3, 2, 1):
        blocks += [y_swapped[step], x_swapped[step]]

    summed = pl.pallas_call(
        product_kernel,
        out_shape=jax.ShapeDtypeStruct((BLK, BLK + 128), jnp.int16),
        in_specs=[smem] + [anywhere] * (3 + PEERS),
        out_specs=vmem,
        scratch_shapes=[
            pltpu.VMEM((SLOTS, PEERS, PART, BLK), jnp.bfloat16),
            pltpu.VMEM((SLOTS, REST, BLK), jnp.bfloat16),
            pltpu.VMEM((SLOTS, BLK, BLK), jnp.bfloat16),
            pltpu.VMEM((SLOTS, BLK, BLK), jnp.bfloat16),
            pltpu.VMEM((2, BLK, BLK), jnp.bfloat16),
            pltpu.VMEM((BLK, BLK), jnp.float32),
        ]
        + [pltpu.SemaphoreType.DMA((SLOTS,))] * 4,
        compiler_params=params,
    )(
        mine,
        front,
        left_blocks,
        right_ops,
        *[pltpu.with_memory_space_constraint(b, pltpu.HBM) for b in blocks],
    )
    parts = lax.all_to_all(
        summed.reshape(GROUPS, BLK // GROUPS, BLK + 128), "term", 0, 0, tiled=True
    )
    total = pl.pallas_call(
        total_kernel,
        out_shape=jax.ShapeDtypeStruct((BLK // GROUPS, BLK), jnp.float32),
        in_specs=[vmem],
        out_specs=vmem,
    )(parts)
    return total.T[None]


def solution(mesh):
    placed = (
        P("sector", None, None),
        P("term", "sector", None, None),
        P("term", None, None),
        P(),
        P(),
        P(),
        P(),
    )
    return jax.shard_map(
        on_device, mesh=mesh, in_specs=placed, out_specs=P("sector", None, "term"), check_vma=False
    )
```

time: 108 us -> 101 us (0.935)
  blocking collectives: 21.8 us -> 16.6 us
  local copies, waits for them, and re-layouts: 6.67 us -> 4.65 us
  waiting for transfers between devices: 30.5 us -> 32.1 us
  Pallas kernels: 21.9 us -> 20.8 us
    all_to_all x1, blocking collectives: 21.8 us -> 16.6 us  [on_device(): lax.all_to_all(summed.reshape(GROUPS, BLK // GROUPS, BLK + 128), 'term',...]
    unnamed x16 -> x20, local copies, waits for them, and re-layouts: 4.2 us -> 2.18 us
    ppermute x17, waiting for transfers between devices: 26.9 us -> 28.6 us  [hop(): return lax.ppermute(x, BOTH, perm)]
    pallas_call x2 -> x3, Pallas kernels: 17.2 us -> 16.1 us  [the longest x1 11.2 us: on_device(): pl.pallas_call(product_kernel, out_shape=jax.ShapeDtypeStruct((BLK, BLK +...]
  transfers between devices with their start and end apart: 19 -> 19, of which waited for: 8 -> 8; matrix products, arithmetic and copies ran while one was open for 1% -> 2% of each run, Pallas kernels for 8% -> 8%
where the time goes in v4:
time: 101 us; the launch traced here: 100 us
  waiting for transfers between devices  32.1 us (32%)
  starting transfers between devices  25.7 us (25%)
  Pallas kernels  20.8 us (21%)
  blocking collectives  16.6 us (16%)
  local copies, waits for them, and re-layouts  4.65 us (5%)
    ppermute x17, waiting for transfers between devices, hop(): return lax.ppermute(x, BOTH, perm)  28.6 us
    all_to_all x1, blocking collectives, on_device(): lax.all_to_all(summed.reshape(GROUPS, BLK // GROUPS, BLK + 128), 'term',...  16.6 us
    all_to_all x1, starting transfers between devices, on_device(): lax.all_to_all(copies, 'sector', 0, 0, axis_index_groups=SAME_CORE, tiled...  11.4 us
    pallas_call x1, Pallas kernels, on_device(): pl.pallas_call(product_kernel, out_shape=jax.ShapeDtypeStruct((BLK, BLK +...  11.2 us
    all_to_all x1, starting transfers between devices, on_device(): lax.all_to_all(chosen, BOTH, 0, 0, axis_index_groups=PEER_GROUPS, tiled=T...  7.46 us
    ppermute x17, starting transfers between devices, hop(): return lax.ppermute(x, BOTH, perm)  6.74 us
    pallas_call x1, Pallas kernels, on_device(): pl.pallas_call(index_kernel, out_shape=(jax.ShapeDtypeStruct((PEERS * SLO...  4.65 us
    all_to_all x1, waiting for transfers between devices, on_device(): lax.all_to_all(copies, 'sector', 0, 0, axis_index_groups=SAME_CORE, tiled...  3.53 us
  transfers between devices with their start and end apart: 19, of which 8 were waited for; matrix products, arithmetic and copies ran while one was open for 2% of the time, Pallas kernels for 8%

profile of v4, /device:TPU:4, one launch (start us, length us, event | category | flops | bytes accessed | tf_op | source)
XLA Modules:
  0.0 100.1 jit_solution(7238321657451551584)
XLA Ops:
  0.0 1.0 fusion
  1.0 0.6 collective-permute-start.1
  1.6 0.8 constant_dynamic-slice_fusion
  2.4 0.7 broadcast_in_dim.11
  3.1 11.4 %all-to-all-start = ((bf16[16,16,512]{2,1,0:T(8,128)(2,1)}), bf16[16,16,512]{2,1,0:T(8,128)(2,1)S(1)}, u32[]{:S(2)}, u32[]{:S(2)}) async-start(bf16[16,16,512]{2,1,0:T(8,128)(2,1)} %bitcast.2), calls=%async_computation | async-start | bytes 524288 | tf_op jit(solution)/shard_map/all_to_all | solution.py:201
  14.5 0.0 collective-permute-done.1
  14.5 0.1 pad_maximum_fusion.refs_0_
  14.6 1.5 %collective-permute-start.3 = (bf16[2,256,512]{2,1,0:T(8,128)(2,1)S(1)}, bf16[2,256,512]{2,1,0:T(8,128)(2,1)S(1)}, u32[]{:S(2)}, u32[]{:S(2)}) collective-permute-start(bf16[2,256,512]{2,1,0:T(8,128)(2,1)S(1)} %pad_maximum_fusion.refs_0_), channel_id=1, source_target_pairs={{0,2},{1,15},{2,4},{3,1},{4,6},{5,3},{6,8},{7,5},{8,10},{9,7},{10,... | collective-permute-start | bytes 1572872 | tf_op jit(solution)/shard_map/ppermute | solution.py:180
  16.2 0.0 collective-permute-start.2
  16.2 4.7 %shard_map.73 = (s32[128]{0:T(128)}, s32[4,8]{1,0:T(4,128)}) custom-call(s32[64]{0:T(128)} %term_order.1, s32[32,64]{1,0:T(8,128)} %bitcast.13, s32[32]{0:T(128)} %sector_at.1, s32[32]{0:T(128)} %sector_rows.1), custom_call_target="tpu_custom_call" | custom-call | bytes 8388608 | tf_op jit(solution)/shard_map/pallas_call | solution.py:182
  20.8 0.0 copy-start
  20.8 3.5 %all-to-all-done.own = bf16[16,16,512]{2,1,0:T(8,128)(2,1)S(1)} async-done(((bf16[16,16,512]{2,1,0:T(8,128)(2,1)}), bf16[16,16,512]{2,1,0:T(8,128)(2,1)S(1)}, u32[]{:S(2)}, u32[]{:S(2)}) %all-to-all-start) | async-done | bytes 262176 | tf_op jit(solution)/shard_map/all_to_all | solution.py:201
  24.4 0.0 collective-permute-start
  24.4 4.2 %collective-permute-done.3.refs_2_ = bf16[2,256,512]{2,1,0:T(8,128)(2,1)S(1)} collective-permute-done((bf16[2,256,512]{2,1,0:T(8,128)(2,1)S(1)}, bf16[2,256,512]{2,1,0:T(8,128)(2,1)S(1)}, u32[]{:S(2)}, u32[]{:S(2)}) %collective-permute-start.3) | collective-permute-done | bytes 524320 | tf_op jit(solution)/shard_map/ppermute | solution.py:180
  28.5 0.0 collective-permute-start.5
  28.5 0.0 collective-permute-done.2.refs_1_
  28.5 0.8 collective-permute-start.4
  29.3 0.0 collective-permute-done.other
  29.3 0.6 copy-done.1
  29.9 3.0 %shard_map.74 = bf16[16,8,16,512]{3,2,1,0:T(8,128)(2,1)} custom-call(s32[128]{0:T(128)S(1)} %copy-done.1, bf16[16,16,512]{2,1,0:T(8,128)(2,1)S(1)} %all-to-all-done.own, bf16[16,16,512]{2,1,0:T(8,128)(2,1)S(1)} %collective-permute-done.other), custom_call_target="tpu_custom_call" | custom-call | bytes 8388608 | tf_op jit(solution)/shard_map/pallas_call | solution.py:204
  32.9 7.5 %all-to-all-start.1 = ((bf16[16,8,16,512]{3,2,1,0:T(8,128)(2,1)}), bf16[16,8,16,512]{3,2,1,0:T(8,128)(2,1)S(1)}, u32[]{:S(2)}, u32[]{:S(2)}) async-start(bf16[16,8,16,512]{3,2,1,0:T(8,128)(2,1)} %shard_map.74), calls=%async_computation.1 | async-start | bytes 4194304 | tf_op jit(solution)/shard_map/all_to_all | solution.py:216
  40.4 0.0 collective-permute-done.5.refs_4_
  40.4 1.5 %collective-permute-start.7 = (bf16[2,256,512]{2,1,0:T(8,128)(2,1)}, bf16[2,256,512]{2,1,0:T(8,128)(2,1)S(1)}, u32[]{:S(2)}, u32[]{:S(2)}) collective-permute-start(bf16[2,256,512]{2,1,0:T(8,128)(2,1)} %collective-permute-done.5.refs_4_), channel_id=1, source_target_pairs={{0,2},{1,15},{2,4},{3,1},{4,6},{5,3},{6,8},{7,5},{8,10},{9,7},{10,... | collective-permute-start | bytes 1572872 | tf_op jit(solution)/shard_map/ppermute | solution.py:180
  41.9 2.7 %collective-permute-done.4.refs_3_ = bf16[2,256,512]{2,1,0:T(8,128)(2,1)} collective-permute-done((bf16[2,256,512]{2,1,0:T(8,128)(2,1)}, bf16[2,256,512]{2,1,0:T(8,128)(2,1)}, u32[]{:S(2)}, u32[]{:S(2)}) %collective-permute-start.4) | collective-permute-done | bytes 524320 | tf_op jit(solution)/shard_map/ppermute | solution.py:180
  44.6 0.0 collective-permute-start.6
  44.6 0.0 collective-permute-start.16
  44.6 0.5 collective-permute-start.14
  45.2 5.9 %collective-permute-done.7.refs_6_ = bf16[2,256,512]{2,1,0:T(8,128)(2,1)S(1)} collective-permute-done((bf16[2,256,512]{2,1,0:T(8,128)(2,1)}, bf16[2,256,512]{2,1,0:T(8,128)(2,1)S(1)}, u32[]{:S(2)}, u32[]{:S(2)}) %collective-permute-start.7) | collective-permute-done | bytes 524320 | tf_op jit(solution)/shard_map/ppermute | solution.py:180
  51.1 0.6 collective-permute-start.9
  51.6 5.1 %collective-permute-done.6.refs_5_ = bf16[2,256,512]{2,1,0:T(8,128)(2,1)S(1)} collective-permute-done((bf16[2,256,512]{2,1,0:T(8,128)(2,1)}, bf16[2,256,512]{2,1,0:T(8,128)(2,1)S(1)}, u32[]{:S(2)}, u32[]{:S(2)}) %collective-permute-start.6) | collective-permute-done | bytes 524320 | tf_op jit(solution)/shard_map/ppermute | solution.py:180
  56.7 0.6 collective-permute-start.8
  57.3 0.0 collective-permute-start.15
  57.3 0.5 collective-permute-start.12
  57.8 0.1 collective-permute-start.13
  57.9 4.5 %collective-permute-done.9.refs_8_ = bf16[2,256,512]{2,1,0:T(8,128)(2,1)} collective-permute-done((bf16[2,256,512]{2,1,0:T(8,128)(2,1)S(1)}, bf16[2,256,512]{2,1,0:T(8,128)(2,1)}, u32[]{:S(2)}, u32[]{:S(2)}) %collective-permute-start.9) | collective-permute-done | bytes 524320 | tf_op jit(solution)/shard_map/ppermute | solution.py:180
  62.4 0.0 collective-permute-start.10
  62.4 5.6 %collective-permute-done.8.refs_7_ = bf16[2,256,512]{2,1,0:T(8,128)(2,1)} collective-permute-done((bf16[2,256,512]{2,1,0:T(8,128)(2,1)S(1)}, bf16[2,256,512]{2,1,0:T(8,128)(2,1)}, u32[]{:S(2)}, u32[]{:S(2)}) %collective-permute-start.8) | collective-permute-done | bytes 524320 | tf_op jit(solution)/shard_map/ppermute | solution.py:180
  68.0 0.0 collective-permute-start.11
  68.0 0.0 collective-permute-done.15.refs_14_
  68.1 0.7 copy-done.8
  68.8 0.8 copy-done.9
  69.7 0.0 collective-permute-done.13.refs_12_
  69.7 0.0 all-to-all-done.1.front
  69.7 0.0 collective-permute-done.10.refs_9_
  69.7 0.6 collective-permute-done.11.refs_10_
  70.3 11.2 %shard_map.75 = s16[512,640]{1,0:T(8,128)(2,1)S(1)} custom-call(s32[4,8]{1,0:T(4,128)S(1)} %copy-done, bf16[16,8,16,512]{3,2,1,0:T(8,128)(2,1)S(1)} %all-to-all-done.1.front, bf16[8,1,512,512]{3,2,1,0:T(8,128)(2,1)} %left.1, bf16[8,512,512]{2,1,0:T(8,128)(2,1)} %right.1, bf16[2,256,512]{2,1,0:T(8,128)(2,1)} %copy-done.2, ...), custom_call_target="tpu_custom_call" | custom-call | tf_op jit(solution)/shard_map/pallas_call | solution.py:230
  81.5 16.6 %all_to_all.15.parts = s16[8,64,640]{2,1,0:T(8,128)(2,1)} all-to-all(s16[8,64,640]{2,1,0:T(8,128)(2,1)S(1)} %bitcast.10), channel_id=1, replica_groups=mesh['term'=8,'sector'=32] {'term'}, dimensions={0} | all-to-all | bytes 1310720 | tf_op jit(solution)/shard_map/all_to_all | solution.py:252
  98.1 1.9 %shard_map.76 = f32[64,512]{1,0:T(8,128)} custom-call(s16[8,64,640]{2,1,0:T(8,128)(2,1)} %all_to_all.15.parts), custom_call_target="tpu_custom_call" | custom-call | tf_op jit(solution)/shard_map/pallas_call | solution.py:255
  (19 shorter events, 0.0 us)
Async XLA Ops:
  1.0 13.6 %collective-permute-start.1 = (bf16[256,512]{1,0:T(8,128)(2,1)S(1)}, bf16[256,512]{1,0:T(8,128)(2,1)S(1)}, u32[]{:S(2)}, u32[]{:S(2)}) collective-permute-start(bf16[256,512]{1,0:T(8,128)(2,1)S(1)} %get-tuple-element.12), channel_id=1, source_target_pairs={{0,48},{1,49},{2,50},{3,51},{4,52},{5,53},{6,54},{7,55},{8,56},{9,... | collective-permute-start | bytes 786440 | tf_op jit(solution)/shard_map/ppermute | solution.py:180
  3.1 21.3 %all-to-all-start = ((bf16[16,16,512]{2,1,0:T(8,128)(2,1)}), bf16[16,16,512]{2,1,0:T(8,128)(2,1)S(1)}, u32[]{:S(2)}, u32[]{:S(2)}) async-start(bf16[16,16,512]{2,1,0:T(8,128)(2,1)} %bitcast.2), calls=%async_computation | async-start | bytes 524288 | tf_op jit(solution)/shard_map/all_to_all | solution.py:201
  14.6 55.7 %copy-start.2 = (bf16[2,256,512]{2,1,0:T(8,128)(2,1)}, bf16[2,256,512]{2,1,0:T(8,128)(2,1)S(1)}, u32[]{:S(2)}) copy-start(bf16[2,256,512]{2,1,0:T(8,128)(2,1)S(1)} %pad_maximum_fusion.refs_0_) | copy-start | bytes 1572868
  14.6 13.9 %collective-permute-start.3 = (bf16[2,256,512]{2,1,0:T(8,128)(2,1)S(1)}, bf16[2,256,512]{2,1,0:T(8,128)(2,1)S(1)}, u32[]{:S(2)}, u32[]{:S(2)}) collective-permute-start(bf16[2,256,512]{2,1,0:T(8,128)(2,1)S(1)} %pad_maximum_fusion.refs_0_), channel_id=1, source_target_pairs={{0,2},{1,15},{2,4},{3,1},{4,6},{5,3},{6,8},{7,5},{8,10},{9,7},{10,... | collective-permute-start | bytes 1572872 | tf_op jit(solution)/shard_map/ppermute | solution.py:180
  16.2 12.4 %collective-permute-start.2 = (bf16[2,256,512]{2,1,0:T(8,128)(2,1)S(1)}, bf16[2,256,512]{2,1,0:T(8,128)(2,1)}, u32[]{:S(2)}, u32[]{:S(2)}) collective-permute-start(bf16[2,256,512]{2,1,0:T(8,128)(2,1)S(1)} %pad_maximum_fusion.refs_0_), channel_id=1, source_target_pairs={{0,1},{1,0},{2,3},{3,2},{4,5},{5,4},{6,7},{7,6},{8,9},{9,8},{10,11... | collective-permute-start | bytes 1572872 | tf_op jit(solution)/shard_map/ppermute | solution.py:180
  20.8 49.5 %copy-start = (s32[4,8]{1,0:T(4,128)S(1)}, s32[4,8]{1,0:T(4,128)}, u32[]{:S(2)}) copy-start(s32[4,8]{1,0:T(4,128)} %get-tuple-element.8.mine) | copy-start | bytes 388
  24.4 5.0 %collective-permute-start = (bf16[16,16,512]{2,1,0:T(8,128)(2,1)S(1)}, bf16[16,16,512]{2,1,0:T(8,128)(2,1)S(1)}, u32[]{:S(2)}, u32[]{:S(2)}) collective-permute-start(bf16[16,16,512]{2,1,0:T(8,128)(2,1)S(1)} %all-to-all-done.own), channel_id=1, source_target_pairs={{0,1},{1,0},{2,3},{3,2},{4,5},{5,4},{6,7},{7,6},{8,9},{9,8},{10,11... | collective-permute-start | bytes 786440 | tf_op jit(solution)/shard_map/ppermute | solution.py:180
  28.5 41.8 %copy-start.3 = (bf16[2,256,512]{2,1,0:T(8,128)(2,1)}, bf16[2,256,512]{2,1,0:T(8,128)(2,1)S(1)}, u32[]{:S(2)}) copy-start(bf16[2,256,512]{2,1,0:T(8,128)(2,1)S(1)} %collective-permute-done.3.refs_2_) | copy-start | bytes 1572868
  28.5 11.9 %collective-permute-start.5 = (bf16[2,256,512]{2,1,0:T(8,128)(2,1)S(1)}, bf16[2,256,512]{2,1,0:T(8,128)(2,1)}, u32[]{:S(2)}, u32[]{:S(2)}) collective-permute-start(bf16[2,256,512]{2,1,0:T(8,128)(2,1)S(1)} %collective-permute-done.3.refs_2_), channel_id=1, source_target_pairs={{0,2},{1,15},{2,4},{3,1},{4,6},{5,3},{6,8},{7,5},{8,10},{9,7},{10,... | collective-permute-start | bytes 1572872 | tf_op jit(solution)/shard_map/ppermute | solution.py:180
  28.5 16.1 %collective-permute-start.4 = (bf16[2,256,512]{2,1,0:T(8,128)(2,1)}, bf16[2,256,512]{2,1,0:T(8,128)(2,1)}, u32[]{:S(2)}, u32[]{:S(2)}) collective-permute-start(bf16[2,256,512]{2,1,0:T(8,128)(2,1)} %collective-permute-done.2.refs_1_), channel_id=1, source_target_pairs={{0,2},{1,15},{2,4},{3,1},{4,6},{5,3},{6,8},{7,5},{8,10},{9,7},{10,... | collective-permute-start | bytes 1572872 | tf_op jit(solution)/shard_map/ppermute | solution.py:180
  29.3 0.6 copy-start.1
  32.9 36.8 %all-to-all-start.1 = ((bf16[16,8,16,512]{3,2,1,0:T(8,128)(2,1)}), bf16[16,8,16,512]{3,2,1,0:T(8,128)(2,1)S(1)}, u32[]{:S(2)}, u32[]{:S(2)}) async-start(bf16[16,8,16,512]{3,2,1,0:T(8,128)(2,1)} %shard_map.74), calls=%async_computation.1 | async-start | bytes 4194304 | tf_op jit(solution)/shard_map/all_to_all | solution.py:216
  40.4 10.7 %collective-permute-start.7 = (bf16[2,256,512]{2,1,0:T(8,128)(2,1)}, bf16[2,256,512]{2,1,0:T(8,128)(2,1)S(1)}, u32[]{:S(2)}, u32[]{:S(2)}) collective-permute-start(bf16[2,256,512]{2,1,0:T(8,128)(2,1)} %collective-permute-done.5.refs_4_), channel_id=1, source_target_pairs={{0,2},{1,15},{2,4},{3,1},{4,6},{5,3},{6,8},{7,5},{8,10},{9,7},{10,... | collective-permute-start | bytes 1572872 | tf_op jit(solution)/shard_map/ppermute | solution.py:180
  44.6 12.1 %collective-permute-start.6 = (bf16[2,256,512]{2,1,0:T(8,128)(2,1)}, bf16[2,256,512]{2,1,0:T(8,128)(2,1)S(1)}, u32[]{:S(2)}, u32[]{:S(2)}) collective-permute-start(bf16[2,256,512]{2,1,0:T(8,128)(2,1)} %collective-permute-done.4.refs_3_), channel_id=1, source_target_pairs={{0,2},{1,15},{2,4},{3,1},{4,6},{5,3},{6,8},{7,5},{8,10},{9,7},{10,... | collective-permute-start | bytes 1572872 | tf_op jit(solution)/shard_map/ppermute | solution.py:180
  44.6 12.6 %collective-permute-start.16 = (bf16[2,256,512]{2,1,0:T(8,128)(2,1)S(1)}, bf16[2,256,512]{2,1,0:T(8,128)(2,1)S(1)}, u32[]{:S(2)}, u32[]{:S(2)}) collective-permute-start(bf16[2,256,512]{2,1,0:T(8,128)(2,1)S(1)} %collective-permute-done.3.refs_2_), channel_id=1, source_target_pairs={{0,1},{1,0},{2,3},{3,2},{4,5},{5,4},{6,7},{7,6},{8,9},{9,8},{10,11... | collective-permute-start | bytes 1572872 | tf_op jit(solution)/shard_map/ppermute | solution.py:180
  44.6 13.1 %collective-permute-start.14 = (bf16[2,256,512]{2,1,0:T(8,128)(2,1)}, bf16[2,256,512]{2,1,0:T(8,128)(2,1)S(1)}, u32[]{:S(2)}, u32[]{:S(2)}) collective-permute-start(bf16[2,256,512]{2,1,0:T(8,128)(2,1)} %collective-permute-done.5.refs_4_), channel_id=1, source_target_pairs={{0,1},{1,0},{2,3},{3,2},{4,5},{5,4},{6,7},{7,6},{8,9},{9,8},{10,11... | collective-permute-start | bytes 1572872 | tf_op jit(solution)/shard_map/ppermute | solution.py:180
  51.1 17.0 %copy-start.4 = (bf16[2,256,512]{2,1,0:T(8,128)(2,1)}, bf16[2,256,512]{2,1,0:T(8,128)(2,1)S(1)}, u32[]{:S(2)}) copy-start(bf16[2,256,512]{2,1,0:T(8,128)(2,1)S(1)} %collective-permute-done.7.refs_6_) | copy-start | bytes 1572868
  51.1 11.3 %collective-permute-start.9 = (bf16[2,256,512]{2,1,0:T(8,128)(2,1)S(1)}, bf16[2,256,512]{2,1,0:T(8,128)(2,1)}, u32[]{:S(2)}, u32[]{:S(2)}) collective-permute-start(bf16[2,256,512]{2,1,0:T(8,128)(2,1)S(1)} %collective-permute-done.7.refs_6_), channel_id=1, source_target_pairs={{0,2},{1,15},{2,4},{3,1},{4,6},{5,3},{6,8},{7,5},{8,10},{9,7},{10,... | collective-permute-start | bytes 1572872 | tf_op jit(solution)/shard_map/ppermute | solution.py:180
  56.7 11.4 %copy-start.5 = (bf16[2,256,512]{2,1,0:T(8,128)(2,1)}, bf16[2,256,512]{2,1,0:T(8,128)(2,1)S(1)}, u32[]{:S(2)}) copy-start(bf16[2,256,512]{2,1,0:T(8,128)(2,1)S(1)} %collective-permute-done.6.refs_5_) | copy-start | bytes 1572868
  56.7 11.3 %collective-permute-start.8 = (bf16[2,256,512]{2,1,0:T(8,128)(2,1)S(1)}, bf16[2,256,512]{2,1,0:T(8,128)(2,1)}, u32[]{:S(2)}, u32[]{:S(2)}) collective-permute-start(bf16[2,256,512]{2,1,0:T(8,128)(2,1)S(1)} %collective-permute-done.6.refs_5_), channel_id=1, source_target_pairs={{0,2},{1,15},{2,4},{3,1},{4,6},{5,3},{6,8},{7,5},{8,10},{9,7},{10,... | collective-permute-start | bytes 1572872 | tf_op jit(solution)/shard_map/ppermute | solution.py:180
  57.3 10.8 %collective-permute-start.15 = (bf16[2,256,512]{2,1,0:T(8,128)(2,1)}, bf16[2,256,512]{2,1,0:T(8,128)(2,1)S(1)}, u32[]{:S(2)}, u32[]{:S(2)}) collective-permute-start(bf16[2,256,512]{2,1,0:T(8,128)(2,1)} %collective-permute-done.4.refs_3_), channel_id=1, source_target_pairs={{0,1},{1,0},{2,3},{3,2},{4,5},{5,4},{6,7},{7,6},{8,9},{9,8},{10,11... | collective-permute-start | bytes 1572872 | tf_op jit(solution)/shard_map/ppermute | solution.py:180
  57.3 10.8 %copy-start.6 = (bf16[2,256,512]{2,1,0:T(8,128)(2,1)}, bf16[2,256,512]{2,1,0:T(8,128)(2,1)S(1)}, u32[]{:S(2)}) copy-start(bf16[2,256,512]{2,1,0:T(8,128)(2,1)S(1)} %collective-permute-done.16.refs_15_) | copy-start | bytes 1572868
  57.3 10.8 %collective-permute-start.12 = (bf16[2,256,512]{2,1,0:T(8,128)(2,1)S(1)}, bf16[2,256,512]{2,1,0:T(8,128)(2,1)S(1)}, u32[]{:S(2)}, u32[]{:S(2)}) collective-permute-start(bf16[2,256,512]{2,1,0:T(8,128)(2,1)S(1)} %collective-permute-done.7.refs_6_), channel_id=1, source_target_pairs={{0,1},{1,0},{2,3},{3,2},{4,5},{5,4},{6,7},{7,6},{8,9},{9,8},{10,11... | collective-permute-start | bytes 1572872 | tf_op jit(solution)/shard_map/ppermute | solution.py:180
  57.8 10.3 %copy-start.7 = (bf16[2,256,512]{2,1,0:T(8,128)(2,1)}, bf16[2,256,512]{2,1,0:T(8,128)(2,1)S(1)}, u32[]{:S(2)}) copy-start(bf16[2,256,512]{2,1,0:T(8,128)(2,1)S(1)} %collective-permute-done.14.refs_13_) | copy-start | bytes 1572868
  57.8 11.9 %collective-permute-start.13 = (bf16[2,256,512]{2,1,0:T(8,128)(2,1)S(1)}, bf16[2,256,512]{2,1,0:T(8,128)(2,1)}, u32[]{:S(2)}, u32[]{:S(2)}) collective-permute-start(bf16[2,256,512]{2,1,0:T(8,128)(2,1)S(1)} %collective-permute-done.6.refs_5_), channel_id=1, source_target_pairs={{0,1},{1,0},{2,3},{3,2},{4,5},{5,4},{6,7},{7,6},{8,9},{9,8},{10,11... | collective-permute-start | bytes 1572872 | tf_op jit(solution)/shard_map/ppermute | solution.py:180
  62.4 7.3 %collective-permute-start.10 = (bf16[2,256,512]{2,1,0:T(8,128)(2,1)}, bf16[2,256,512]{2,1,0:T(8,128)(2,1)}, u32[]{:S(2)}, u32[]{:S(2)}) collective-permute-start(bf16[2,256,512]{2,1,0:T(8,128)(2,1)} %collective-permute-done.9.refs_8_), channel_id=1, source_target_pairs={{0,1},{1,0},{2,3},{3,2},{4,5},{5,4},{6,7},{7,6},{8,9},{9,8},{10,11... | collective-permute-start | bytes 1572872 | tf_op jit(solution)/shard_map/ppermute | solution.py:180
  68.0 2.3 %collective-permute-start.11 = (bf16[2,256,512]{2,1,0:T(8,128)(2,1)}, bf16[2,256,512]{2,1,0:T(8,128)(2,1)}, u32[]{:S(2)}, u32[]{:S(2)}) collective-permute-start(bf16[2,256,512]{2,1,0:T(8,128)(2,1)} %collective-permute-done.8.refs_7_), channel_id=1, source_target_pairs={{0,1},{1,0},{2,3},{3,2},{4,5},{5,4},{6,7},{7,6},{8,9},{9,8},{10,11... | collective-permute-start | bytes 1572872 | tf_op jit(solution)/shard_map/ppermute | solution.py:180
  68.0 0.8 copy-start.8
  68.8 0.8 copy-start.9

commit v5 on v4

--- a/solution.py
+++ b/solution.py
@@ -19,6 +19,7 @@
 LN2 = 0.6931471805599453
 LEVELS = 64.0
 STEPS = 32766.0
+WIDTH = BLK // GROUPS
 VMEM_LIMIT = 48 * 1024 * 1024
 
 
@@ -91,19 +92,13 @@
     lax.fori_loop(0, PEERS, peer, 0)
 
 
-def select_kernel(front, own, other, out, held, sem):
+def select_kernel(front, own, other, out, both, held, sem):
+    both[:16] = own[...]
+    both[16:] = other[...]
+
     def peer(m, carry):
         for k in range(SLOTS):
-            at = front[m * SLOTS + k]
-
-            @pl.when(at < 16)
-            def _(k=k, at=at):
-                held[m, k] = own[at]
-
-            @pl.when(at >= 16)
-            def _(k=k, at=at):
-                held[m, k] = other[at - 16]
-
+            held[m, k] = both[front[m * SLOTS + k]]
         pltpu.make_async_copy(held.at[m], out.at[m], sem).start()
         return carry
 
@@ -115,15 +110,26 @@
     blocks, refs = refs[:PEERS], refs[PEERS:]
     out, fronts, rests, lefts, rights, block, acc, front_sem, rest_sem, left_sem, right_sem = refs
 
+    def fetch_rest(j, low, high):
+        if high - low == 1:
+            ref = blocks[low]
+            pltpu.make_async_copy(ref.at[mine[1, j]], rests.at[j], rest_sem.at[j]).start()
+            return
+        middle = (low + high) // 2
+        below = mine[0, j] < middle
+
+        @pl.when(below)
+        def _():
+            fetch_rest(j, low, middle)
+
+        @pl.when(jnp.logical_not(below))
+        def _():
+            fetch_rest(j, middle, high)
+
     def fetch(j, carry):
         pltpu.make_async_copy(right.at[j], rights.at[j], right_sem.at[j]).start()
         pltpu.make_async_copy(front.at[:, j], fronts.at[j], front_sem.at[j]).start()
-        for i, ref in enumerate(blocks):
-
-            @pl.when(mine[0, j] == i)
-            def _(ref=ref):
-                pltpu.make_async_copy(ref.at[mine[1, j]], rests.at[j], rest_sem.at[j]).start()
-
+        fetch_rest(j, 0, PEERS)
         pltpu.make_async_copy(left.at[j, 0], lefts.at[j], left_sem.at[j]).start()
         return carry
 
@@ -151,21 +157,13 @@
         else:
             acc[...] += part
     total = jnp.where(rows < mine[3, 0], acc[...], 0.0).T
-    largest = jnp.maximum(jnp.max(jnp.abs(total), axis=1, keepdims=True), 1e-30)
-    level = jnp.ceil(jnp.log(largest) * (LEVELS / LN2)) + 1.0
-    steps = total * (STEPS * jnp.exp(level * (-LN2 / LEVELS)))
-    out[:, :BLK] = jnp.round(steps).astype(jnp.int32).astype(jnp.int16)
-    out[:, BLK:] = jnp.broadcast_to(level, (BLK, 128)).astype(jnp.int32).astype(jnp.int16)
-
-
-def total_kernel(parts, out):
-    total = None
     for g in range(GROUPS):
-        level = parts[g, :, BLK:].astype(jnp.int32).astype(jnp.float32)[:, :1]
-        size = jnp.exp(level * (LN2 / LEVELS)) * (1.0 / STEPS)
-        part = parts[g, :, :BLK].astype(jnp.int32).astype(jnp.float32) * size
-        total = part if total is None else total + part
-    out[...] = total
+        piece = total[g * WIDTH : (g + 1) * WIDTH]
+        largest = jnp.maximum(jnp.max(jnp.abs(piece), axis=0, keepdims=True), 1e-30)
+        level = jnp.ceil(jnp.log(largest) * (LEVELS / LN2)) + 1.0
+        steps = piece * (STEPS * jnp.exp(level * (-LN2 / LEVELS)))
+        out[g, :WIDTH] = jnp.round(steps).astype(jnp.int32).astype(jnp.int16)
+        out[g, WIDTH:] = jnp.broadcast_to(level, (16, BLK)).astype(jnp.int32).astype(jnp.int16)
 
 
 def on_device(psi, left_blocks, right_ops, sector_rows, connect, term_order, sector_at):
@@ -207,6 +205,7 @@
         in_specs=[smem] + [vmem] * 2,
         out_specs=anywhere,
         scratch_shapes=[
+            pltpu.VMEM((PLACES, PART, BLK), psi.dtype),
             pltpu.VMEM((PEERS, SLOTS, PART, BLK), psi.dtype),
             pltpu.SemaphoreType.DMA,
         ],
@@ -229,7 +228,7 @@
 
     summed = pl.pallas_call(
         product_kernel,
-        out_shape=jax.ShapeDtypeStruct((BLK, BLK + 128), jnp.int16),
+        out_shape=jax.ShapeDtypeStruct((GROUPS, WIDTH + 16, BLK), jnp.int16),
         in_specs=[smem] + [anywhere] * (3 + PEERS),
         out_specs=vmem,
         scratch_shapes=[
@@ -249,16 +248,9 @@
         right_ops,
         *[pltpu.with_memory_space_constraint(b, pltpu.HBM) for b in blocks],
     )
-    parts = lax.all_to_all(
-        summed.reshape(GROUPS, BLK // GROUPS, BLK + 128), "term", 0, 0, tiled=True
-    )
-    total = pl.pallas_call(
-        total_kernel,
-        out_shape=jax.ShapeDtypeStruct((BLK // GROUPS, BLK), jnp.float32),
-        in_specs=[vmem],
-        out_specs=vmem,
-    )(parts)
-    return total.T[None]
+    parts = lax.all_to_all(summed, "term", 0, 0, tiled=True).astype(jnp.float32)
+    sizes = jnp.exp(parts[:, WIDTH:WIDTH + 1] * (LN2 / LEVELS)) * (1.0 / STEPS)
+    return jnp.sum(parts[:, :WIDTH] * sizes, axis=0).T[None]
 
 
 def solution(mesh):

time: 101 us -> 98.6 us (0.976)
  Pallas kernels: 20.8 us -> 17.6 us
  waiting for transfers between devices: 32.1 us -> 33.4 us
  other arithmetic: 0.05 us -> 1.06 us
    pallas_call x2 -> x1, Pallas kernels: 13.1 us -> 11 us  [on_device(): pl.pallas_call(product_kernel, out_shape=jax.ShapeDtypeStruct((GROUPS, WI...]
    pallas_call x1, Pallas kernels: 3.03 us -> 1.95 us  [on_device(): pl.pallas_call(select_kernel, out_shape=pltpu.HBM((PEERS, SLOTS, PART, BL...]
    unnamed x20 -> x21, local copies, waits for them, and re-layouts: 2.18 us -> 1.36 us
  transfers between devices with their start and end apart: 19 -> 19, of which waited for: 8 -> 9; matrix products, arithmetic and copies ran while one was open for 2% -> 2% of each run, Pallas kernels for 8% -> 7%
where the time goes in v5:
time: 98.6 us; the launch traced here: 98.2 us
  waiting for transfers between devices  33.4 us (34%)
  starting transfers between devices  25.4 us (26%)
  Pallas kernels  17.6 us (18%)
  blocking collectives  16.7 us (17%)
  local copies, waits for them, and re-layouts  3.84 us (4%)
  other arithmetic  1.06 us (1%)
    ppermute x17, waiting for transfers between devices, hop(): return lax.ppermute(x, BOTH, perm)  29.3 us
    all_to_all x1, blocking collectives, on_device(): parts = lax.all_to_all(summed, 'term', 0, 0, tiled=True).astype(jnp.float32)  16.7 us
    all_to_all x1, starting transfers between devices, on_device(): lax.all_to_all(copies, 'sector', 0, 0, axis_index_groups=SAME_CORE, tiled...  11.4 us
    pallas_call x1, Pallas kernels, on_device(): pl.pallas_call(product_kernel, out_shape=jax.ShapeDtypeStruct((GROUPS, WI...  11 us
    all_to_all x1, starting transfers between devices, on_device(): lax.all_to_all(chosen, BOTH, 0, 0, axis_index_groups=PEER_GROUPS, tiled=T...  7.46 us
    ppermute x17, starting transfers between devices, hop(): return lax.ppermute(x, BOTH, perm)  6.46 us
    pallas_call x1, Pallas kernels, on_device(): pl.pallas_call(index_kernel, out_shape=(jax.ShapeDtypeStruct((PEERS * SLO...  4.65 us
    all_to_all x1, waiting for transfers between devices, on_device(): lax.all_to_all(copies, 'sector', 0, 0, axis_index_groups=SAME_CORE, tiled...  3.54 us
  transfers between devices with their start and end apart: 19, of which 9 were waited for; matrix products, arithmetic and copies ran while one was open for 2% of the time, Pallas kernels for 7%

profile of v5, /device:TPU:4, one launch (start us, length us, event | category | flops | bytes accessed | tf_op | source)
XLA Modules:
  0.0 98.2 jit_solution(8855730276046643632)
XLA Ops:
  0.0 1.0 %fusion.3 = (bf16[1,256,512]{2,1,0:T(8,128)(2,1)S(1)}, bf16[256,512]{1,0:T(8,128)(2,1)S(1)}) fusion(bf16[1,512,512]{2,1,0:T(8,128)(2,1)} %param.7), kind=kLoop, calls=%fused_computation.9 | loop fusion | bytes 786432 | tf_op jit(solution)/shard_map/slice | solution.py:195
  1.0 0.6 collective-permute-start.1
  1.6 0.8 constant_dynamic-slice_fusion
  2.4 0.7 broadcast_in_dim.11
  3.1 11.4 %all-to-all-start = ((bf16[16,16,512]{2,1,0:T(8,128)(2,1)}), bf16[16,16,512]{2,1,0:T(8,128)(2,1)S(1)}, u32[]{:S(2)}, u32[]{:S(2)}) async-start(bf16[16,16,512]{2,1,0:T(8,128)(2,1)} %bitcast.2), calls=%async_computation | async-start | bytes 524288 | tf_op jit(solution)/shard_map/all_to_all | solution.py:199
  14.6 0.0 collective-permute-done.1
  14.6 0.1 pad_maximum_fusion.refs_0_
  14.6 1.5 %collective-permute-start.3 = (bf16[2,256,512]{2,1,0:T(8,128)(2,1)S(1)}, bf16[2,256,512]{2,1,0:T(8,128)(2,1)S(1)}, u32[]{:S(2)}, u32[]{:S(2)}) collective-permute-start(bf16[2,256,512]{2,1,0:T(8,128)(2,1)S(1)} %pad_maximum_fusion.refs_0_), channel_id=1, source_target_pairs={{0,2},{1,15},{2,4},{3,1},{4,6},{5,3},{6,8},{7,5},{8,10},{9,7},{10,... | collective-permute-start | bytes 1572872 | tf_op jit(solution)/shard_map/ppermute | solution.py:178
  16.2 0.0 collective-permute-start.2
  16.2 4.7 %shard_map.73 = (s32[128]{0:T(128)}, s32[4,8]{1,0:T(4,128)}) custom-call(s32[64]{0:T(128)} %term_order.1, s32[32,64]{1,0:T(8,128)} %bitcast.15, s32[32]{0:T(128)} %sector_at.1, s32[32]{0:T(128)} %sector_rows.1), custom_call_target="tpu_custom_call" | custom-call | bytes 8388608 | tf_op jit(solution)/shard_map/pallas_call | solution.py:180
  20.8 3.5 %all-to-all-done.own = bf16[16,16,512]{2,1,0:T(8,128)(2,1)S(1)} async-done(((bf16[16,16,512]{2,1,0:T(8,128)(2,1)}), bf16[16,16,512]{2,1,0:T(8,128)(2,1)S(1)}, u32[]{:S(2)}, u32[]{:S(2)}) %all-to-all-start) | async-done | bytes 262176 | tf_op jit(solution)/shard_map/all_to_all | solution.py:199
  24.4 0.0 collective-permute-start
  24.4 4.2 %collective-permute-done.3.refs_2_ = bf16[2,256,512]{2,1,0:T(8,128)(2,1)S(1)} collective-permute-done((bf16[2,256,512]{2,1,0:T(8,128)(2,1)S(1)}, bf16[2,256,512]{2,1,0:T(8,128)(2,1)S(1)}, u32[]{:S(2)}, u32[]{:S(2)}) %collective-permute-start.3) | collective-permute-done | bytes 524320 | tf_op jit(solution)/shard_map/ppermute | solution.py:178
  28.5 0.0 collective-permute-start.5
  28.5 0.0 collective-permute-done.2.refs_1_
  28.5 0.8 collective-permute-start.4
  29.3 0.0 collective-permute-done.other
  29.3 0.6 copy-done.1
  29.9 1.9 %shard_map.74 = bf16[16,8,16,512]{3,2,1,0:T(8,128)(2,1)} custom-call(s32[128]{0:T(128)S(1)} %copy-done.1, bf16[16,16,512]{2,1,0:T(8,128)(2,1)S(1)} %all-to-all-done.own, bf16[16,16,512]{2,1,0:T(8,128)(2,1)S(1)} %collective-permute-done.other), custom_call_target="tpu_custom_call" | custom-call | bytes 8388608 | tf_op jit(solution)/shard_map/pallas_call | solution.py:202
  31.9 0.0 copy-start
  31.9 7.5 %all-to-all-start.1 = ((bf16[16,8,16,512]{3,2,1,0:T(8,128)(2,1)}), bf16[16,8,16,512]{3,2,1,0:T(8,128)(2,1)S(1)}, u32[]{:S(2)}, u32[]{:S(2)}) async-start(bf16[16,8,16,512]{3,2,1,0:T(8,128)(2,1)} %shard_map.74), calls=%async_computation.1 | async-start | bytes 4194304 | tf_op jit(solution)/shard_map/all_to_all | solution.py:215
  39.3 0.0 collective-permute-done.5.refs_4_
  39.3 1.5 %collective-permute-start.7 = (bf16[2,256,512]{2,1,0:T(8,128)(2,1)}, bf16[2,256,512]{2,1,0:T(8,128)(2,1)S(1)}, u32[]{:S(2)}, u32[]{:S(2)}) collective-permute-start(bf16[2,256,512]{2,1,0:T(8,128)(2,1)} %collective-permute-done.5.refs_4_), channel_id=1, source_target_pairs={{0,2},{1,15},{2,4},{3,1},{4,6},{5,3},{6,8},{7,5},{8,10},{9,7},{10,... | collective-permute-start | bytes 1572872 | tf_op jit(solution)/shard_map/ppermute | solution.py:178
  40.9 3.8 %collective-permute-done.4.refs_3_ = bf16[2,256,512]{2,1,0:T(8,128)(2,1)} collective-permute-done((bf16[2,256,512]{2,1,0:T(8,128)(2,1)}, bf16[2,256,512]{2,1,0:T(8,128)(2,1)}, u32[]{:S(2)}, u32[]{:S(2)}) %collective-permute-start.4) | collective-permute-done | bytes 524320 | tf_op jit(solution)/shard_map/ppermute | solution.py:178
  44.6 0.0 collective-permute-start.6
  44.7 0.0 collective-permute-start.16
  44.7 0.5 collective-permute-start.14
  45.2 5.0 %collective-permute-done.7.refs_6_ = bf16[2,256,512]{2,1,0:T(8,128)(2,1)S(1)} collective-permute-done((bf16[2,256,512]{2,1,0:T(8,128)(2,1)}, bf16[2,256,512]{2,1,0:T(8,128)(2,1)S(1)}, u32[]{:S(2)}, u32[]{:S(2)}) %collective-permute-start.7) | collective-permute-done | bytes 524320 | tf_op jit(solution)/shard_map/ppermute | solution.py:178
  50.2 0.4 collective-permute-start.9
  50.6 5.2 %collective-permute-done.6.refs_5_ = bf16[2,256,512]{2,1,0:T(8,128)(2,1)S(1)} collective-permute-done((bf16[2,256,512]{2,1,0:T(8,128)(2,1)}, bf16[2,256,512]{2,1,0:T(8,128)(2,1)S(1)}, u32[]{:S(2)}, u32[]{:S(2)}) %collective-permute-start.6) | collective-permute-done | bytes 524320 | tf_op jit(solution)/shard_map/ppermute | solution.py:178
  55.8 0.4 collective-permute-start.8
  56.2 0.0 collective-permute-start.15
  56.2 0.5 collective-permute-start.12
  56.7 0.1 collective-permute-start.13
  56.8 4.7 %collective-permute-done.9.refs_8_ = bf16[2,256,512]{2,1,0:T(8,128)(2,1)} collective-permute-done((bf16[2,256,512]{2,1,0:T(8,128)(2,1)S(1)}, bf16[2,256,512]{2,1,0:T(8,128)(2,1)}, u32[]{:S(2)}, u32[]{:S(2)}) %collective-permute-start.9) | collective-permute-done | bytes 524320 | tf_op jit(solution)/shard_map/ppermute | solution.py:178
  61.5 0.0 collective-permute-start.10
  61.5 5.6 %collective-permute-done.8.refs_7_ = bf16[2,256,512]{2,1,0:T(8,128)(2,1)} collective-permute-done((bf16[2,256,512]{2,1,0:T(8,128)(2,1)S(1)}, bf16[2,256,512]{2,1,0:T(8,128)(2,1)}, u32[]{:S(2)}, u32[]{:S(2)}) %collective-permute-start.8) | collective-permute-done | bytes 524320 | tf_op jit(solution)/shard_map/ppermute | solution.py:178
  67.1 0.0 collective-permute-start.11
  67.1 0.0 collective-permute-done.15.refs_14_
  67.1 0.0 collective-permute-done.12.refs_11_
  67.2 0.8 copy-done.8
  67.9 0.5 all-to-all-done.1.front
  68.4 0.0 collective-permute-done.10.refs_9_
  68.5 0.9 collective-permute-done.11.refs_10_
  69.4 11.0 %shard_map.75 = s16[8,80,512]{2,1,0:T(8,128)(2,1)S(1)} custom-call(s32[4,8]{1,0:T(4,128)S(1)} %copy-done, bf16[16,8,16,512]{3,2,1,0:T(8,128)(2,1)S(1)} %all-to-all-done.1.front, bf16[8,1,512,512]{3,2,1,0:T(8,128)(2,1)} %left.1, bf16[8,512,512]{2,1,0:T(8,128)(2,1)} %right.1, bf16[2,256,512]{2,1,0:T(8,128)(2,1)} %copy-done.2, ...), custom_call_target="tpu_custom_call" | custom-call | tf_op jit(solution)/shard_map/pallas_call | solution.py:229
  80.4 16.7 %all_to_all.15 = s16[8,80,512]{2,1,0:T(8,128)(2,1)S(1)} all-to-all(s16[8,80,512]{2,1,0:T(8,128)(2,1)S(1)} %shard_map.75), channel_id=1, replica_groups=mesh['term'=8,'sector'=32] {'term'}, dimensions={0} | all-to-all | bytes 1310720 | tf_op jit(solution)/shard_map/all_to_all | solution.py:251
  97.1 0.2 convert_element_type.3
  97.4 0.8 fusion
  (22 shorter events, 0.1 us)
Async XLA Ops:
  1.0 13.6 %collective-permute-start.1 = (bf16[256,512]{1,0:T(8,128)(2,1)S(1)}, bf16[256,512]{1,0:T(8,128)(2,1)S(1)}, u32[]{:S(2)}, u32[]{:S(2)}) collective-permute-start(bf16[256,512]{1,0:T(8,128)(2,1)S(1)} %get-tuple-element.12), channel_id=1, source_target_pairs={{0,48},{1,49},{2,50},{3,51},{4,52},{5,53},{6,54},{7,55},{8,56},{9,... | collective-permute-start | bytes 786440 | tf_op jit(solution)/shard_map/ppermute | solution.py:178
  3.1 21.3 %all-to-all-start = ((bf16[16,16,512]{2,1,0:T(8,128)(2,1)}), bf16[16,16,512]{2,1,0:T(8,128)(2,1)S(1)}, u32[]{:S(2)}, u32[]{:S(2)}) async-start(bf16[16,16,512]{2,1,0:T(8,128)(2,1)} %bitcast.2), calls=%async_computation | async-start | bytes 524288 | tf_op jit(solution)/shard_map/all_to_all | solution.py:199
  14.6 17.3 %copy-start.2 = (bf16[2,256,512]{2,1,0:T(8,128)(2,1)}, bf16[2,256,512]{2,1,0:T(8,128)(2,1)S(1)}, u32[]{:S(2)}) copy-start(bf16[2,256,512]{2,1,0:T(8,128)(2,1)S(1)} %pad_maximum_fusion.refs_0_) | copy-start | bytes 1572868
  14.6 13.9 %collective-permute-start.3 = (bf16[2,256,512]{2,1,0:T(8,128)(2,1)S(1)}, bf16[2,256,512]{2,1,0:T(8,128)(2,1)S(1)}, u32[]{:S(2)}, u32[]{:S(2)}) collective-permute-start(bf16[2,256,512]{2,1,0:T(8,128)(2,1)S(1)} %pad_maximum_fusion.refs_0_), channel_id=1, source_target_pairs={{0,2},{1,15},{2,4},{3,1},{4,6},{5,3},{6,8},{7,5},{8,10},{9,7},{10,... | collective-permute-start | bytes 1572872 | tf_op jit(solution)/shard_map/ppermute | solution.py:178
  16.2 12.4 %collective-permute-start.2 = (bf16[2,256,512]{2,1,0:T(8,128)(2,1)S(1)}, bf16[2,256,512]{2,1,0:T(8,128)(2,1)}, u32[]{:S(2)}, u32[]{:S(2)}) collective-permute-start(bf16[2,256,512]{2,1,0:T(8,128)(2,1)S(1)} %pad_maximum_fusion.refs_0_), channel_id=1, source_target_pairs={{0,1},{1,0},{2,3},{3,2},{4,5},{5,4},{6,7},{7,6},{8,9},{9,8},{10,11... | collective-permute-start | bytes 1572872 | tf_op jit(solution)/shard_map/ppermute | solution.py:178
  24.4 5.0 %collective-permute-start = (bf16[16,16,512]{2,1,0:T(8,128)(2,1)S(1)}, bf16[16,16,512]{2,1,0:T(8,128)(2,1)S(1)}, u32[]{:S(2)}, u32[]{:S(2)}) collective-permute-start(bf16[16,16,512]{2,1,0:T(8,128)(2,1)S(1)} %all-to-all-done.own), channel_id=1, source_target_pairs={{0,1},{1,0},{2,3},{3,2},{4,5},{5,4},{6,7},{7,6},{8,9},{9,8},{10,11... | collective-permute-start | bytes 786440 | tf_op jit(solution)/shard_map/ppermute | solution.py:178
  28.5 16.1 %copy-start.3 = (bf16[2,256,512]{2,1,0:T(8,128)(2,1)}, bf16[2,256,512]{2,1,0:T(8,128)(2,1)S(1)}, u32[]{:S(2)}) copy-start(bf16[2,256,512]{2,1,0:T(8,128)(2,1)S(1)} %collective-permute-done.3.refs_2_) | copy-start | bytes 1572868
  28.5 10.8 %collective-permute-start.5 = (bf16[2,256,512]{2,1,0:T(8,128)(2,1)S(1)}, bf16[2,256,512]{2,1,0:T(8,128)(2,1)}, u32[]{:S(2)}, u32[]{:S(2)}) collective-permute-start(bf16[2,256,512]{2,1,0:T(8,128)(2,1)S(1)} %collective-permute-done.3.refs_2_), channel_id=1, source_target_pairs={{0,2},{1,15},{2,4},{3,1},{4,6},{5,3},{6,8},{7,5},{8,10},{9,7},{10,... | collective-permute-start | bytes 1572872 | tf_op jit(solution)/shard_map/ppermute | solution.py:178
  28.5 16.1 %collective-permute-start.4 = (bf16[2,256,512]{2,1,0:T(8,128)(2,1)}, bf16[2,256,512]{2,1,0:T(8,128)(2,1)}, u32[]{:S(2)}, u32[]{:S(2)}) collective-permute-start(bf16[2,256,512]{2,1,0:T(8,128)(2,1)} %collective-permute-done.2.refs_1_), channel_id=1, source_target_pairs={{0,2},{1,15},{2,4},{3,1},{4,6},{5,3},{6,8},{7,5},{8,10},{9,7},{10,... | collective-permute-start | bytes 1572872 | tf_op jit(solution)/shard_map/ppermute | solution.py:178
  29.3 0.6 copy-start.1
  31.9 37.5 %copy-start = (s32[4,8]{1,0:T(4,128)S(1)}, s32[4,8]{1,0:T(4,128)}, u32[]{:S(2)}) copy-start(s32[4,8]{1,0:T(4,128)} %get-tuple-element.8.mine) | copy-start | bytes 388
  31.9 36.6 %all-to-all-start.1 = ((bf16[16,8,16,512]{3,2,1,0:T(8,128)(2,1)}), bf16[16,8,16,512]{3,2,1,0:T(8,128)(2,1)S(1)}, u32[]{:S(2)}, u32[]{:S(2)}) async-start(bf16[16,8,16,512]{3,2,1,0:T(8,128)(2,1)} %shard_map.74), calls=%async_computation.1 | async-start | bytes 4194304 | tf_op jit(solution)/shard_map/all_to_all | solution.py:215
  39.3 10.8 %collective-permute-start.7 = (bf16[2,256,512]{2,1,0:T(8,128)(2,1)}, bf16[2,256,512]{2,1,0:T(8,128)(2,1)S(1)}, u32[]{:S(2)}, u32[]{:S(2)}) collective-permute-start(bf16[2,256,512]{2,1,0:T(8,128)(2,1)} %collective-permute-done.5.refs_4_), channel_id=1, source_target_pairs={{0,2},{1,15},{2,4},{3,1},{4,6},{5,3},{6,8},{7,5},{8,10},{9,7},{10,... | collective-permute-start | bytes 1572872 | tf_op jit(solution)/shard_map/ppermute | solution.py:178
  44.6 11.1 %collective-permute-start.6 = (bf16[2,256,512]{2,1,0:T(8,128)(2,1)}, bf16[2,256,512]{2,1,0:T(8,128)(2,1)S(1)}, u32[]{:S(2)}, u32[]{:S(2)}) collective-permute-start(bf16[2,256,512]{2,1,0:T(8,128)(2,1)} %collective-permute-done.4.refs_3_), channel_id=1, source_target_pairs={{0,2},{1,15},{2,4},{3,1},{4,6},{5,3},{6,8},{7,5},{8,10},{9,7},{10,... | collective-permute-start | bytes 1572872 | tf_op jit(solution)/shard_map/ppermute | solution.py:178
  44.7 11.6 %collective-permute-start.16 = (bf16[2,256,512]{2,1,0:T(8,128)(2,1)S(1)}, bf16[2,256,512]{2,1,0:T(8,128)(2,1)S(1)}, u32[]{:S(2)}, u32[]{:S(2)}) collective-permute-start(bf16[2,256,512]{2,1,0:T(8,128)(2,1)S(1)} %collective-permute-done.3.refs_2_), channel_id=1, source_target_pairs={{0,1},{1,0},{2,3},{3,2},{4,5},{5,4},{6,7},{7,6},{8,9},{9,8},{10,11... | collective-permute-start | bytes 1572872 | tf_op jit(solution)/shard_map/ppermute | solution.py:178
  44.7 12.1 %collective-permute-start.14 = (bf16[2,256,512]{2,1,0:T(8,128)(2,1)}, bf16[2,256,512]{2,1,0:T(8,128)(2,1)S(1)}, u32[]{:S(2)}, u32[]{:S(2)}) collective-permute-start(bf16[2,256,512]{2,1,0:T(8,128)(2,1)} %collective-permute-done.5.refs_4_), channel_id=1, source_target_pairs={{0,1},{1,0},{2,3},{3,2},{4,5},{5,4},{6,7},{7,6},{8,9},{9,8},{10,11... | collective-permute-start | bytes 1572872 | tf_op jit(solution)/shard_map/ppermute | solution.py:178
  50.2 19.2 %copy-start.4 = (bf16[2,256,512]{2,1,0:T(8,128)(2,1)}, bf16[2,256,512]{2,1,0:T(8,128)(2,1)S(1)}, u32[]{:S(2)}) copy-start(bf16[2,256,512]{2,1,0:T(8,128)(2,1)S(1)} %collective-permute-done.7.refs_6_) | copy-start | bytes 1572868
  50.2 11.3 %collective-permute-start.9 = (bf16[2,256,512]{2,1,0:T(8,128)(2,1)S(1)}, bf16[2,256,512]{2,1,0:T(8,128)(2,1)}, u32[]{:S(2)}, u32[]{:S(2)}) collective-permute-start(bf16[2,256,512]{2,1,0:T(8,128)(2,1)S(1)} %collective-permute-done.7.refs_6_), channel_id=1, source_target_pairs={{0,2},{1,15},{2,4},{3,1},{4,6},{5,3},{6,8},{7,5},{8,10},{9,7},{10,... | collective-permute-start | bytes 1572872 | tf_op jit(solution)/shard_map/ppermute | solution.py:178
  55.8 11.4 %copy-start.5 = (bf16[2,256,512]{2,1,0:T(8,128)(2,1)}, bf16[2,256,512]{2,1,0:T(8,128)(2,1)S(1)}, u32[]{:S(2)}) copy-start(bf16[2,256,512]{2,1,0:T(8,128)(2,1)S(1)} %collective-permute-done.6.refs_5_) | copy-start | bytes 1572868
  55.8 11.3 %collective-permute-start.8 = (bf16[2,256,512]{2,1,0:T(8,128)(2,1)S(1)}, bf16[2,256,512]{2,1,0:T(8,128)(2,1)}, u32[]{:S(2)}, u32[]{:S(2)}) collective-permute-start(bf16[2,256,512]{2,1,0:T(8,128)(2,1)S(1)} %collective-permute-done.6.refs_5_), channel_id=1, source_target_pairs={{0,2},{1,15},{2,4},{3,1},{4,6},{5,3},{6,8},{7,5},{8,10},{9,7},{10,... | collective-permute-start | bytes 1572872 | tf_op jit(solution)/shard_map/ppermute | solution.py:178
  56.2 10.9 %collective-permute-start.15 = (bf16[2,256,512]{2,1,0:T(8,128)(2,1)}, bf16[2,256,512]{2,1,0:T(8,128)(2,1)S(1)}, u32[]{:S(2)}, u32[]{:S(2)}) collective-permute-start(bf16[2,256,512]{2,1,0:T(8,128)(2,1)} %collective-permute-done.4.refs_3_), channel_id=1, source_target_pairs={{0,1},{1,0},{2,3},{3,2},{4,5},{5,4},{6,7},{7,6},{8,9},{9,8},{10,11... | collective-permute-start | bytes 1572872 | tf_op jit(solution)/shard_map/ppermute | solution.py:178
  56.2 10.9 %copy-start.6 = (bf16[2,256,512]{2,1,0:T(8,128)(2,1)}, bf16[2,256,512]{2,1,0:T(8,128)(2,1)S(1)}, u32[]{:S(2)}) copy-start(bf16[2,256,512]{2,1,0:T(8,128)(2,1)S(1)} %collective-permute-done.16.refs_15_) | copy-start | bytes 1572868
  56.2 10.9 %collective-permute-start.12 = (bf16[2,256,512]{2,1,0:T(8,128)(2,1)S(1)}, bf16[2,256,512]{2,1,0:T(8,128)(2,1)S(1)}, u32[]{:S(2)}, u32[]{:S(2)}) collective-permute-start(bf16[2,256,512]{2,1,0:T(8,128)(2,1)S(1)} %collective-permute-done.7.refs_6_), channel_id=1, source_target_pairs={{0,1},{1,0},{2,3},{3,2},{4,5},{5,4},{6,7},{7,6},{8,9},{9,8},{10,11... | collective-permute-start | bytes 1572872 | tf_op jit(solution)/shard_map/ppermute | solution.py:178
  56.7 10.4 %copy-start.7 = (bf16[2,256,512]{2,1,0:T(8,128)(2,1)}, bf16[2,256,512]{2,1,0:T(8,128)(2,1)S(1)}, u32[]{:S(2)}) copy-start(bf16[2,256,512]{2,1,0:T(8,128)(2,1)S(1)} %collective-permute-done.14.refs_13_) | copy-start | bytes 1572868
  56.7 11.2 %collective-permute-start.13 = (bf16[2,256,512]{2,1,0:T(8,128)(2,1)S(1)}, bf16[2,256,512]{2,1,0:T(8,128)(2,1)}, u32[]{:S(2)}, u32[]{:S(2)}) collective-permute-start(bf16[2,256,512]{2,1,0:T(8,128)(2,1)S(1)} %collective-permute-done.6.refs_5_), channel_id=1, source_target_pairs={{0,1},{1,0},{2,3},{3,2},{4,5},{5,4},{6,7},{7,6},{8,9},{9,8},{10,11... | collective-permute-start | bytes 1572872 | tf_op jit(solution)/shard_map/ppermute | solution.py:178
  61.5 7.0 %collective-permute-start.10 = (bf16[2,256,512]{2,1,0:T(8,128)(2,1)}, bf16[2,256,512]{2,1,0:T(8,128)(2,1)}, u32[]{:S(2)}, u32[]{:S(2)}) collective-permute-start(bf16[2,256,512]{2,1,0:T(8,128)(2,1)} %collective-permute-done.9.refs_8_), channel_id=1, source_target_pairs={{0,1},{1,0},{2,3},{3,2},{4,5},{5,4},{6,7},{7,6},{8,9},{9,8},{10,11... | collective-permute-start | bytes 1572872 | tf_op jit(solution)/shard_map/ppermute | solution.py:178
  67.1 2.3 %collective-permute-start.11 = (bf16[2,256,512]{2,1,0:T(8,128)(2,1)}, bf16[2,256,512]{2,1,0:T(8,128)(2,1)}, u32[]{:S(2)}, u32[]{:S(2)}) collective-permute-start(bf16[2,256,512]{2,1,0:T(8,128)(2,1)} %collective-permute-done.8.refs_7_), channel_id=1, source_target_pairs={{0,1},{1,0},{2,3},{3,2},{4,5},{5,4},{6,7},{7,6},{8,9},{9,8},{10,11... | collective-permute-start | bytes 1572872 | tf_op jit(solution)/shard_map/ppermute | solution.py:178
  67.1 0.8 copy-start.8
  67.9 1.5 %copy-start.9 = (bf16[2,256,512]{2,1,0:T(8,128)(2,1)}, bf16[2,256,512]{2,1,0:T(8,128)(2,1)S(1)}, u32[]{:S(2)}) copy-start(bf16[2,256,512]{2,1,0:T(8,128)(2,1)S(1)} %collective-permute-done.12.refs_11_) | copy-start | bytes 1572868

commit v6 on v5

--- a/solution.py
+++ b/solution.py
@@ -92,6 +92,19 @@
     lax.fori_loop(0, PEERS, peer, 0)
 
 
+def prepare_kernel(first, psi, copies, part, pieces, sem):
+    start = pl.multiple_of(first[0], 2 * PART)
+    near = pltpu.make_async_copy(psi.at[pl.ds(start, 2 * PART)], pieces, sem.at[0])
+    rest = pltpu.make_async_copy(psi.at[pl.ds(FRONT, REST)], part, sem.at[1])
+    near.start()
+    rest.start()
+    near.wait()
+    for h in range(2):
+        for z in range(PEERS // 2):
+            copies[h * (PEERS // 2) + z] = pieces[h * PART : (h + 1) * PART]
+    rest.wait()
+
+
 def select_kernel(front, own, other, out, both, held, sem):
     both[:16] = own[...]
     both[16:] = other[...]
@@ -137,21 +150,34 @@
 
     def arrived(buffer, sem, k):
         pltpu.make_async_copy(buffer.at[k], buffer.at[k], sem.at[k]).wait()
-        return buffer[k]
 
     def dot(a, b):
         return jnp.dot(a, b, preferred_element_type=jnp.float32)
 
     rows = lax.broadcasted_iota(jnp.int32, (BLK, BLK), 0)
-    for k in range(SLOTS):
-        block[k % 2, :FRONT] = arrived(fronts, front_sem, k).reshape(FRONT, BLK)
-        block[k % 2, FRONT:] = arrived(rests, rest_sem, k)
-        t = dot(block[k % 2], arrived(rights, right_sem, k))
+
+    def wait(k):
+        arrived(fronts, front_sem, k)
+        arrived(rests, rest_sem, k)
+        arrived(rights, right_sem, k)
+        arrived(lefts, left_sem, k)
+
+    def first_product(k):
+        block[k % 2, :FRONT] = fronts[k].reshape(FRONT, BLK)
+        block[k % 2, FRONT:] = rests[k]
+        t = dot(block[k % 2], rights[k])
         t = jnp.where(rows < mine[2, k], t, 0.0)
         hi = t.astype(jnp.bfloat16)
-        lo = (t - hi.astype(jnp.float32)).astype(jnp.bfloat16)
-        left_k = arrived(lefts, left_sem, k)
-        part = dot(left_k, hi) + dot(left_k, lo)
+        return hi, (t - hi.astype(jnp.float32)).astype(jnp.bfloat16)
+
+    wait(0)
+    following = first_product(0)
+    for k in range(SLOTS):
+        hi, lo = following
+        if k + 1 < SLOTS:
+            wait(k + 1)
+            following = first_product(k + 1)
+        part = dot(lefts[k], hi) + dot(lefts[k], lo)
         if k == 0:
             acc[...] = part
         else:
@@ -192,10 +218,25 @@
     def after(x, y):
         return lax.optimization_barrier((x, y))[0]
 
-    x = [jnp.stack([psi[FRONT:], hop(psi[FRONT:], FAR)])]
+    copies, part = pl.pallas_call(
+        prepare_kernel,
+        out_shape=(
+            jax.ShapeDtypeStruct((PEERS, PART, BLK), psi.dtype),
+            jax.ShapeDtypeStruct((REST, BLK), psi.dtype),
+        ),
+        in_specs=[smem, anywhere],
+        out_specs=(vmem, vmem),
+        scratch_shapes=[
+            pltpu.VMEM((2 * PART, BLK), psi.dtype),
+            pltpu.SemaphoreType.DMA((2,)),
+        ],
+        compiler_params=params,
+    )(
+        (group * 2 * PART).astype(jnp.int32)[None],
+        pltpu.with_memory_space_constraint(psi, pltpu.HBM),
+    )
+    x = [jnp.stack([part, hop(part, FAR)])]
     y = [hop(x[0], SWAP)]
-    pieces = lax.dynamic_slice(psi, (group * 2 * PART, 0), (2 * PART, BLK)).reshape(2, 1, PART, BLK)
-    copies = jnp.broadcast_to(pieces, (2, PLACES // 4, PART, BLK)).reshape(PEERS, PART, BLK)
     own = lax.all_to_all(copies, "sector", 0, 0, axis_index_groups=SAME_CORE, tiled=True)
     own = after(own, front_index)
     other = hop(own, SWAP)
@@ -211,7 +252,7 @@
         ],
         cost_estimate=pl.CostEstimate(flops=0, bytes_accessed=8 * 1024 * 1024, transcendentals=0),
         compiler_params=params,
-    )(front_index, own, other)
+    )(pltpu.with_memory_space_constraint(front_index, pltpu.HBM), own, other)
     front = lax.all_to_all(chosen, BOTH, 0, 0, axis_index_groups=PEER_GROUPS, tiled=True)
     for step in range(1, 5):
         x.append(hop(x[-1], RING))

time: 98.6 us -> 96.5 us (0.979)
  local copies, waits for them, and re-layouts: 3.84 us -> 0.78 us
  waiting for transfers between devices: 33.4 us -> 34.8 us
  starting transfers between devices: 25.4 us -> 24.4 us
    ppermute x17, waiting for transfers between devices: 29.3 us -> 31.2 us  [hop(): return lax.ppermute(x, BOTH, perm)]
    pallas_call x0 -> x1, Pallas kernels: none -> 1.68 us  [on_device(): pl.pallas_call(prepare_kernel, out_shape=(jax.ShapeDtypeStruct((PEERS, PA...]
    pallas_call x1, Pallas kernels: 11 us -> 9.76 us  [on_device(): pl.pallas_call(product_kernel, out_shape=jax.ShapeDtypeStruct((GROUPS, WI...]
    ppermute x17, starting transfers between devices: 6.46 us -> 5.47 us  [hop(): return lax.ppermute(x, BOTH, perm)]
  transfers between devices with their start and end apart: 19 -> 19, of which waited for: 9 -> 10; matrix products, arithmetic and copies ran while one was open for 2% -> 0% of each run, Pallas kernels for 7% -> 7%
where the time goes in v6:
time: 96.5 us; the launch traced here: 96.1 us
  waiting for transfers between devices  34.8 us (36%)
  starting transfers between devices  24.4 us (25%)
  Pallas kernels  18.2 us (19%)
  blocking collectives  16.7 us (17%)
  other arithmetic  1.06 us (1%)
    ppermute x17, waiting for transfers between devices, hop(): return lax.ppermute(x, BOTH, perm)  31.2 us
    all_to_all x1, blocking collectives, on_device(): parts = lax.all_to_all(summed, 'term', 0, 0, tiled=True).astype(jnp.float32)  16.7 us
    all_to_all x1, starting transfers between devices, on_device(): lax.all_to_all(copies, 'sector', 0, 0, axis_index_groups=SAME_CORE, tiled...  11.4 us
    pallas_call x1, Pallas kernels, on_device(): pl.pallas_call(product_kernel, out_shape=jax.ShapeDtypeStruct((GROUPS, WI...  9.76 us
    all_to_all x1, starting transfers between devices, on_device(): lax.all_to_all(chosen, BOTH, 0, 0, axis_index_groups=PEER_GROUPS, tiled=T...  7.46 us
    ppermute x17, starting transfers between devices, hop(): return lax.ppermute(x, BOTH, perm)  5.47 us
    pallas_call x1, Pallas kernels, on_device(): pl.pallas_call(index_kernel, out_shape=(jax.ShapeDtypeStruct((PEERS * SLO...  4.65 us
    all_to_all x1, waiting for transfers between devices, on_device(): lax.all_to_all(copies, 'sector', 0, 0, axis_index_groups=SAME_CORE, tiled...  3.54 us
  transfers between devices with their start and end apart: 19, of which 10 were waited for; matrix products, arithmetic and copies ran while one was open for 0% of the time, Pallas kernels for 7%

profile of v6, /device:TPU:4, one launch (start us, length us, event | category | flops | bytes accessed | tf_op | source)
XLA Modules:
  0.0 96.1 jit_solution(13911953478660492838)
XLA Ops:
  0.0 1.7 %shard_map.74 = (bf16[16,16,512]{2,1,0:T(8,128)(2,1)}, bf16[256,512]{1,0:T(8,128)(2,1)S(1)}) custom-call(s32[1]{0:T(128)} %bitcast.1.first, bf16[512,512]{1,0:T(8,128)(2,1)} %bitcast.12), custom_call_target="tpu_custom_call" | custom-call | tf_op jit(solution)/shard_map/pallas_call | solution.py:221
  1.7 0.6 collective-permute-start.1
  2.3 11.4 %all-to-all-start = ((bf16[16,16,512]{2,1,0:T(8,128)(2,1)}), bf16[16,16,512]{2,1,0:T(8,128)(2,1)S(1)}, u32[]{:S(2)}, u32[]{:S(2)}) async-start(bf16[16,16,512]{2,1,0:T(8,128)(2,1)} %get-tuple-element.12), calls=%async_computation | async-start | bytes 524288 | tf_op jit(solution)/shard_map/all_to_all | solution.py:240
  13.8 0.0 collective-permute-done.1
  13.8 0.1 pad_maximum_fusion.refs_0_
  13.8 1.5 %collective-permute-start.3 = (bf16[2,256,512]{2,1,0:T(8,128)(2,1)S(1)}, bf16[2,256,512]{2,1,0:T(8,128)(2,1)S(1)}, u32[]{:S(2)}, u32[]{:S(2)}) collective-permute-start(bf16[2,256,512]{2,1,0:T(8,128)(2,1)S(1)} %pad_maximum_fusion.refs_0_), channel_id=1, source_target_pairs={{0,2},{1,15},{2,4},{3,1},{4,6},{5,3},{6,8},{7,5},{8,10},{9,7},{10,... | collective-permute-start | bytes 1572872 | tf_op jit(solution)/shard_map/ppermute | solution.py:204
  15.4 0.0 collective-permute-start.2
  15.4 4.7 %shard_map.73 = (s32[128]{0:T(128)}, s32[4,8]{1,0:T(4,128)}) custom-call(s32[64]{0:T(128)} %term_order.1, s32[32,64]{1,0:T(8,128)} %bitcast.15, s32[32]{0:T(128)} %sector_at.1, s32[32]{0:T(128)} %sector_rows.1), custom_call_target="tpu_custom_call" | custom-call | bytes 8388608 | tf_op jit(solution)/shard_map/pallas_call | solution.py:206
  20.0 3.5 %all-to-all-done.own = bf16[16,16,512]{2,1,0:T(8,128)(2,1)S(1)} async-done(((bf16[16,16,512]{2,1,0:T(8,128)(2,1)}), bf16[16,16,512]{2,1,0:T(8,128)(2,1)S(1)}, u32[]{:S(2)}, u32[]{:S(2)}) %all-to-all-start) | async-done | bytes 262176 | tf_op jit(solution)/shard_map/all_to_all | solution.py:240
  23.6 0.0 collective-permute-start
  23.6 4.2 %collective-permute-done.3.refs_2_ = bf16[2,256,512]{2,1,0:T(8,128)(2,1)S(1)} collective-permute-done((bf16[2,256,512]{2,1,0:T(8,128)(2,1)S(1)}, bf16[2,256,512]{2,1,0:T(8,128)(2,1)S(1)}, u32[]{:S(2)}, u32[]{:S(2)}) %collective-permute-start.3) | collective-permute-done | bytes 524320 | tf_op jit(solution)/shard_map/ppermute | solution.py:204
  27.7 0.0 collective-permute-start.5
  27.7 0.0 collective-permute-done.2.refs_1_
  27.8 0.8 collective-permute-start.4
  28.5 0.0 collective-permute-done.other
  28.5 2.1 %shard_map.75 = bf16[16,8,16,512]{3,2,1,0:T(8,128)(2,1)} custom-call(s32[128]{0:T(128)} %get-tuple-element.11.front, bf16[16,16,512]{2,1,0:T(8,128)(2,1)S(1)} %all-to-all-done.own, bf16[16,16,512]{2,1,0:T(8,128)(2,1)S(1)} %collective-permute-done.other), custom_call_target="tpu_custom_call" | custom-call | bytes 8388608 | tf_op jit(solution)/shard_map/pallas_call | solution.py:243
  30.6 0.0 copy-start
  30.6 7.5 %all-to-all-start.1 = ((bf16[16,8,16,512]{3,2,1,0:T(8,128)(2,1)}), bf16[16,8,16,512]{3,2,1,0:T(8,128)(2,1)S(1)}, u32[]{:S(2)}, u32[]{:S(2)}) async-start(bf16[16,8,16,512]{3,2,1,0:T(8,128)(2,1)} %shard_map.75), calls=%async_computation.1 | async-start | bytes 4194304 | tf_op jit(solution)/shard_map/all_to_all | solution.py:256
  38.1 0.2 collective-permute-done.5.refs_4_
  38.2 1.4 %collective-permute-start.7 = (bf16[2,256,512]{2,1,0:T(8,128)(2,1)}, bf16[2,256,512]{2,1,0:T(8,128)(2,1)S(1)}, u32[]{:S(2)}, u32[]{:S(2)}) collective-permute-start(bf16[2,256,512]{2,1,0:T(8,128)(2,1)} %collective-permute-done.5.refs_4_), channel_id=1, source_target_pairs={{0,2},{1,15},{2,4},{3,1},{4,6},{5,3},{6,8},{7,5},{8,10},{9,7},{10,... | collective-permute-start | bytes 1572872 | tf_op jit(solution)/shard_map/ppermute | solution.py:204
  39.6 4.2 %collective-permute-done.4.refs_3_ = bf16[2,256,512]{2,1,0:T(8,128)(2,1)} collective-permute-done((bf16[2,256,512]{2,1,0:T(8,128)(2,1)}, bf16[2,256,512]{2,1,0:T(8,128)(2,1)}, u32[]{:S(2)}, u32[]{:S(2)}) %collective-permute-start.4) | collective-permute-done | bytes 524320 | tf_op jit(solution)/shard_map/ppermute | solution.py:204
  43.9 0.0 collective-permute-start.6
  43.9 0.0 collective-permute-start.16
  43.9 0.5 collective-permute-start.14
  44.4 5.0 %collective-permute-done.7.refs_6_ = bf16[2,256,512]{2,1,0:T(8,128)(2,1)S(1)} collective-permute-done((bf16[2,256,512]{2,1,0:T(8,128)(2,1)}, bf16[2,256,512]{2,1,0:T(8,128)(2,1)S(1)}, u32[]{:S(2)}, u32[]{:S(2)}) %collective-permute-start.7) | collective-permute-done | bytes 524320 | tf_op jit(solution)/shard_map/ppermute | solution.py:204
  49.4 0.0 collective-permute-start.9
  49.4 5.6 %collective-permute-done.6.refs_5_ = bf16[2,256,512]{2,1,0:T(8,128)(2,1)S(1)} collective-permute-done((bf16[2,256,512]{2,1,0:T(8,128)(2,1)}, bf16[2,256,512]{2,1,0:T(8,128)(2,1)S(1)}, u32[]{:S(2)}, u32[]{:S(2)}) %collective-permute-start.6) | collective-permute-done | bytes 524320 | tf_op jit(solution)/shard_map/ppermute | solution.py:204
  55.0 0.0 collective-permute-start.8
  55.0 0.0 collective-permute-start.15
  55.0 0.0 collective-permute-done.16.refs_15_
  55.0 0.5 collective-permute-start.12
  55.5 0.0 collective-permute-done.14.refs_13_
  55.5 0.1 collective-permute-start.13
  55.6 5.1 %collective-permute-done.9.refs_8_ = bf16[2,256,512]{2,1,0:T(8,128)(2,1)} collective-permute-done((bf16[2,256,512]{2,1,0:T(8,128)(2,1)S(1)}, bf16[2,256,512]{2,1,0:T(8,128)(2,1)}, u32[]{:S(2)}, u32[]{:S(2)}) %collective-permute-start.9) | collective-permute-done | bytes 524320 | tf_op jit(solution)/shard_map/ppermute | solution.py:204
  60.7 0.0 collective-permute-start.10
  60.7 5.6 %collective-permute-done.8.refs_7_ = bf16[2,256,512]{2,1,0:T(8,128)(2,1)} collective-permute-done((bf16[2,256,512]{2,1,0:T(8,128)(2,1)S(1)}, bf16[2,256,512]{2,1,0:T(8,128)(2,1)}, u32[]{:S(2)}, u32[]{:S(2)}) %collective-permute-start.8) | collective-permute-done | bytes 524320 | tf_op jit(solution)/shard_map/ppermute | solution.py:204
  66.3 0.0 collective-permute-start.11
  66.3 0.0 collective-permute-done.15.refs_14_
  66.3 0.0 collective-permute-done.12.refs_11_
  66.4 0.7 copy-done.7
  67.1 0.0 collective-permute-done.13.refs_12_
  67.1 0.1 all-to-all-done.1.front
  67.2 0.0 collective-permute-done.10.refs_9_
  67.2 1.4 %collective-permute-done.11.refs_10_ = bf16[2,256,512]{2,1,0:T(8,128)(2,1)} collective-permute-done((bf16[2,256,512]{2,1,0:T(8,128)(2,1)}, bf16[2,256,512]{2,1,0:T(8,128)(2,1)}, u32[]{:S(2)}, u32[]{:S(2)}) %collective-permute-start.11) | collective-permute-done | bytes 524320 | tf_op jit(solution)/shard_map/ppermute | solution.py:204
  68.6 9.8 %shard_map.76 = s16[8,80,512]{2,1,0:T(8,128)(2,1)S(1)} custom-call(s32[4,8]{1,0:T(4,128)S(1)} %copy-done, bf16[16,8,16,512]{3,2,1,0:T(8,128)(2,1)S(1)} %all-to-all-done.1.front, bf16[8,1,512,512]{3,2,1,0:T(8,128)(2,1)} %left.1, bf16[8,512,512]{2,1,0:T(8,128)(2,1)} %right.1, bf16[2,256,512]{2,1,0:T(8,128)(2,1)} %copy-done.1, ...), custom_call_target="tpu_custom_call" | custom-call | tf_op jit(solution)/shard_map/pallas_call | solution.py:270
  78.4 16.7 %all_to_all.15 = s16[8,80,512]{2,1,0:T(8,128)(2,1)S(1)} all-to-all(s16[8,80,512]{2,1,0:T(8,128)(2,1)S(1)} %shard_map.76), channel_id=1, replica_groups=mesh['term'=8,'sector'=32] {'term'}, dimensions={0} | all-to-all | bytes 1310720 | tf_op jit(solution)/shard_map/all_to_all | solution.py:292
  95.1 0.2 convert_element_type.3
  95.4 0.8 fusion
  (18 shorter events, 0.1 us)
Async XLA Ops:
  1.7 12.1 %collective-permute-start.1 = (bf16[256,512]{1,0:T(8,128)(2,1)S(1)}, bf16[256,512]{1,0:T(8,128)(2,1)S(1)}, u32[]{:S(2)}, u32[]{:S(2)}) collective-permute-start(bf16[256,512]{1,0:T(8,128)(2,1)S(1)} %get-tuple-element.14), channel_id=1, source_target_pairs={{0,48},{1,49},{2,50},{3,51},{4,52},{5,53},{6,54},{7,55},{8,56},{9,... | collective-permute-start | bytes 786440 | tf_op jit(solution)/shard_map/ppermute | solution.py:204
  2.3 21.3 %all-to-all-start = ((bf16[16,16,512]{2,1,0:T(8,128)(2,1)}), bf16[16,16,512]{2,1,0:T(8,128)(2,1)S(1)}, u32[]{:S(2)}, u32[]{:S(2)}) async-start(bf16[16,16,512]{2,1,0:T(8,128)(2,1)} %get-tuple-element.12), calls=%async_computation | async-start | bytes 524288 | tf_op jit(solution)/shard_map/all_to_all | solution.py:240
  13.8 16.8 %copy-start.1 = (bf16[2,256,512]{2,1,0:T(8,128)(2,1)}, bf16[2,256,512]{2,1,0:T(8,128)(2,1)S(1)}, u32[]{:S(2)}) copy-start(bf16[2,256,512]{2,1,0:T(8,128)(2,1)S(1)} %pad_maximum_fusion.refs_0_) | copy-start | bytes 1572868
  13.8 13.9 %collective-permute-start.3 = (bf16[2,256,512]{2,1,0:T(8,128)(2,1)S(1)}, bf16[2,256,512]{2,1,0:T(8,128)(2,1)S(1)}, u32[]{:S(2)}, u32[]{:S(2)}) collective-permute-start(bf16[2,256,512]{2,1,0:T(8,128)(2,1)S(1)} %pad_maximum_fusion.refs_0_), channel_id=1, source_target_pairs={{0,2},{1,15},{2,4},{3,1},{4,6},{5,3},{6,8},{7,5},{8,10},{9,7},{10,... | collective-permute-start | bytes 1572872 | tf_op jit(solution)/shard_map/ppermute | solution.py:204
  15.4 12.4 %collective-permute-start.2 = (bf16[2,256,512]{2,1,0:T(8,128)(2,1)S(1)}, bf16[2,256,512]{2,1,0:T(8,128)(2,1)}, u32[]{:S(2)}, u32[]{:S(2)}) collective-permute-start(bf16[2,256,512]{2,1,0:T(8,128)(2,1)S(1)} %pad_maximum_fusion.refs_0_), channel_id=1, source_target_pairs={{0,1},{1,0},{2,3},{3,2},{4,5},{5,4},{6,7},{7,6},{8,9},{9,8},{10,11... | collective-permute-start | bytes 1572872 | tf_op jit(solution)/shard_map/ppermute | solution.py:204
  23.6 5.0 %collective-permute-start = (bf16[16,16,512]{2,1,0:T(8,128)(2,1)S(1)}, bf16[16,16,512]{2,1,0:T(8,128)(2,1)S(1)}, u32[]{:S(2)}, u32[]{:S(2)}) collective-permute-start(bf16[16,16,512]{2,1,0:T(8,128)(2,1)S(1)} %all-to-all-done.own), channel_id=1, source_target_pairs={{0,1},{1,0},{2,3},{3,2},{4,5},{5,4},{6,7},{7,6},{8,9},{9,8},{10,11... | collective-permute-start | bytes 786440 | tf_op jit(solution)/shard_map/ppermute | solution.py:204
  27.7 16.1 %copy-start.2 = (bf16[2,256,512]{2,1,0:T(8,128)(2,1)}, bf16[2,256,512]{2,1,0:T(8,128)(2,1)S(1)}, u32[]{:S(2)}) copy-start(bf16[2,256,512]{2,1,0:T(8,128)(2,1)S(1)} %collective-permute-done.3.refs_2_) | copy-start | bytes 1572868
  27.7 10.5 %collective-permute-start.5 = (bf16[2,256,512]{2,1,0:T(8,128)(2,1)S(1)}, bf16[2,256,512]{2,1,0:T(8,128)(2,1)}, u32[]{:S(2)}, u32[]{:S(2)}) collective-permute-start(bf16[2,256,512]{2,1,0:T(8,128)(2,1)S(1)} %collective-permute-done.3.refs_2_), channel_id=1, source_target_pairs={{0,2},{1,15},{2,4},{3,1},{4,6},{5,3},{6,8},{7,5},{8,10},{9,7},{10,... | collective-permute-start | bytes 1572872 | tf_op jit(solution)/shard_map/ppermute | solution.py:204
  27.8 16.1 %collective-permute-start.4 = (bf16[2,256,512]{2,1,0:T(8,128)(2,1)}, bf16[2,256,512]{2,1,0:T(8,128)(2,1)}, u32[]{:S(2)}, u32[]{:S(2)}) collective-permute-start(bf16[2,256,512]{2,1,0:T(8,128)(2,1)} %collective-permute-done.2.refs_1_), channel_id=1, source_target_pairs={{0,2},{1,15},{2,4},{3,1},{4,6},{5,3},{6,8},{7,5},{8,10},{9,7},{10,... | collective-permute-start | bytes 1572872 | tf_op jit(solution)/shard_map/ppermute | solution.py:204
  30.6 38.0 %copy-start = (s32[4,8]{1,0:T(4,128)S(1)}, s32[4,8]{1,0:T(4,128)}, u32[]{:S(2)}) copy-start(s32[4,8]{1,0:T(4,128)} %get-tuple-element.10.mine) | copy-start | bytes 388
  30.6 36.6 %all-to-all-start.1 = ((bf16[16,8,16,512]{3,2,1,0:T(8,128)(2,1)}), bf16[16,8,16,512]{3,2,1,0:T(8,128)(2,1)S(1)}, u32[]{:S(2)}, u32[]{:S(2)}) async-start(bf16[16,8,16,512]{3,2,1,0:T(8,128)(2,1)} %shard_map.75), calls=%async_computation.1 | async-start | bytes 4194304 | tf_op jit(solution)/shard_map/all_to_all | solution.py:256
  38.2 11.1 %collective-permute-start.7 = (bf16[2,256,512]{2,1,0:T(8,128)(2,1)}, bf16[2,256,512]{2,1,0:T(8,128)(2,1)S(1)}, u32[]{:S(2)}, u32[]{:S(2)}) collective-permute-start(bf16[2,256,512]{2,1,0:T(8,128)(2,1)} %collective-permute-done.5.refs_4_), channel_id=1, source_target_pairs={{0,2},{1,15},{2,4},{3,1},{4,6},{5,3},{6,8},{7,5},{8,10},{9,7},{10,... | collective-permute-start | bytes 1572872 | tf_op jit(solution)/shard_map/ppermute | solution.py:204
  43.9 11.1 %collective-permute-start.6 = (bf16[2,256,512]{2,1,0:T(8,128)(2,1)}, bf16[2,256,512]{2,1,0:T(8,128)(2,1)S(1)}, u32[]{:S(2)}, u32[]{:S(2)}) collective-permute-start(bf16[2,256,512]{2,1,0:T(8,128)(2,1)} %collective-permute-done.4.refs_3_), channel_id=1, source_target_pairs={{0,2},{1,15},{2,4},{3,1},{4,6},{5,3},{6,8},{7,5},{8,10},{9,7},{10,... | collective-permute-start | bytes 1572872 | tf_op jit(solution)/shard_map/ppermute | solution.py:204
  43.9 11.1 %collective-permute-start.16 = (bf16[2,256,512]{2,1,0:T(8,128)(2,1)S(1)}, bf16[2,256,512]{2,1,0:T(8,128)(2,1)S(1)}, u32[]{:S(2)}, u32[]{:S(2)}) collective-permute-start(bf16[2,256,512]{2,1,0:T(8,128)(2,1)S(1)} %collective-permute-done.3.refs_2_), channel_id=1, source_target_pairs={{0,1},{1,0},{2,3},{3,2},{4,5},{5,4},{6,7},{7,6},{8,9},{9,8},{10,11... | collective-permute-start | bytes 1572872 | tf_op jit(solution)/shard_map/ppermute | solution.py:204
  43.9 11.6 %collective-permute-start.14 = (bf16[2,256,512]{2,1,0:T(8,128)(2,1)}, bf16[2,256,512]{2,1,0:T(8,128)(2,1)S(1)}, u32[]{:S(2)}, u32[]{:S(2)}) collective-permute-start(bf16[2,256,512]{2,1,0:T(8,128)(2,1)} %collective-permute-done.5.refs_4_), channel_id=1, source_target_pairs={{0,1},{1,0},{2,3},{3,2},{4,5},{5,4},{6,7},{7,6},{8,9},{9,8},{10,11... | collective-permute-start | bytes 1572872 | tf_op jit(solution)/shard_map/ppermute | solution.py:204
  49.4 19.2 %copy-start.3 = (bf16[2,256,512]{2,1,0:T(8,128)(2,1)}, bf16[2,256,512]{2,1,0:T(8,128)(2,1)S(1)}, u32[]{:S(2)}) copy-start(bf16[2,256,512]{2,1,0:T(8,128)(2,1)S(1)} %collective-permute-done.7.refs_6_) | copy-start | bytes 1572868
  49.4 11.3 %collective-permute-start.9 = (bf16[2,256,512]{2,1,0:T(8,128)(2,1)S(1)}, bf16[2,256,512]{2,1,0:T(8,128)(2,1)}, u32[]{:S(2)}, u32[]{:S(2)}) collective-permute-start(bf16[2,256,512]{2,1,0:T(8,128)(2,1)S(1)} %collective-permute-done.7.refs_6_), channel_id=1, source_target_pairs={{0,2},{1,15},{2,4},{3,1},{4,6},{5,3},{6,8},{7,5},{8,10},{9,7},{10,... | collective-permute-start | bytes 1572872 | tf_op jit(solution)/shard_map/ppermute | solution.py:204
  55.0 11.4 %copy-start.4 = (bf16[2,256,512]{2,1,0:T(8,128)(2,1)}, bf16[2,256,512]{2,1,0:T(8,128)(2,1)S(1)}, u32[]{:S(2)}) copy-start(bf16[2,256,512]{2,1,0:T(8,128)(2,1)S(1)} %collective-permute-done.6.refs_5_) | copy-start | bytes 1572868
  55.0 11.3 %collective-permute-start.8 = (bf16[2,256,512]{2,1,0:T(8,128)(2,1)S(1)}, bf16[2,256,512]{2,1,0:T(8,128)(2,1)}, u32[]{:S(2)}, u32[]{:S(2)}) collective-permute-start(bf16[2,256,512]{2,1,0:T(8,128)(2,1)S(1)} %collective-permute-done.6.refs_5_), channel_id=1, source_target_pairs={{0,2},{1,15},{2,4},{3,1},{4,6},{5,3},{6,8},{7,5},{8,10},{9,7},{10,... | collective-permute-start | bytes 1572872 | tf_op jit(solution)/shard_map/ppermute | solution.py:204
  55.0 11.3 %collective-permute-start.15 = (bf16[2,256,512]{2,1,0:T(8,128)(2,1)}, bf16[2,256,512]{2,1,0:T(8,128)(2,1)S(1)}, u32[]{:S(2)}, u32[]{:S(2)}) collective-permute-start(bf16[2,256,512]{2,1,0:T(8,128)(2,1)} %collective-permute-done.4.refs_3_), channel_id=1, source_target_pairs={{0,1},{1,0},{2,3},{3,2},{4,5},{5,4},{6,7},{7,6},{8,9},{9,8},{10,11... | collective-permute-start | bytes 1572872 | tf_op jit(solution)/shard_map/ppermute | solution.py:204
  55.0 11.4 %copy-start.5 = (bf16[2,256,512]{2,1,0:T(8,128)(2,1)}, bf16[2,256,512]{2,1,0:T(8,128)(2,1)S(1)}, u32[]{:S(2)}) copy-start(bf16[2,256,512]{2,1,0:T(8,128)(2,1)S(1)} %collective-permute-done.16.refs_15_) | copy-start | bytes 1572868
  55.0 11.3 %collective-permute-start.12 = (bf16[2,256,512]{2,1,0:T(8,128)(2,1)S(1)}, bf16[2,256,512]{2,1,0:T(8,128)(2,1)S(1)}, u32[]{:S(2)}, u32[]{:S(2)}) collective-permute-start(bf16[2,256,512]{2,1,0:T(8,128)(2,1)S(1)} %collective-permute-done.7.refs_6_), channel_id=1, source_target_pairs={{0,1},{1,0},{2,3},{3,2},{4,5},{5,4},{6,7},{7,6},{8,9},{9,8},{10,11... | collective-permute-start | bytes 1572872 | tf_op jit(solution)/shard_map/ppermute | solution.py:204
  55.5 10.9 %copy-start.6 = (bf16[2,256,512]{2,1,0:T(8,128)(2,1)}, bf16[2,256,512]{2,1,0:T(8,128)(2,1)S(1)}, u32[]{:S(2)}) copy-start(bf16[2,256,512]{2,1,0:T(8,128)(2,1)S(1)} %collective-permute-done.14.refs_13_) | copy-start | bytes 1572868
  55.5 11.6 %collective-permute-start.13 = (bf16[2,256,512]{2,1,0:T(8,128)(2,1)S(1)}, bf16[2,256,512]{2,1,0:T(8,128)(2,1)}, u32[]{:S(2)}, u32[]{:S(2)}) collective-permute-start(bf16[2,256,512]{2,1,0:T(8,128)(2,1)S(1)} %collective-permute-done.6.refs_5_), channel_id=1, source_target_pairs={{0,1},{1,0},{2,3},{3,2},{4,5},{5,4},{6,7},{7,6},{8,9},{9,8},{10,11... | collective-permute-start | bytes 1572872 | tf_op jit(solution)/shard_map/ppermute | solution.py:204
  60.7 6.5 %collective-permute-start.10 = (bf16[2,256,512]{2,1,0:T(8,128)(2,1)}, bf16[2,256,512]{2,1,0:T(8,128)(2,1)}, u32[]{:S(2)}, u32[]{:S(2)}) collective-permute-start(bf16[2,256,512]{2,1,0:T(8,128)(2,1)} %collective-permute-done.9.refs_8_), channel_id=1, source_target_pairs={{0,1},{1,0},{2,3},{3,2},{4,5},{5,4},{6,7},{7,6},{8,9},{9,8},{10,11... | collective-permute-start | bytes 1572872 | tf_op jit(solution)/shard_map/ppermute | solution.py:204
  66.3 2.3 %collective-permute-start.11 = (bf16[2,256,512]{2,1,0:T(8,128)(2,1)}, bf16[2,256,512]{2,1,0:T(8,128)(2,1)}, u32[]{:S(2)}, u32[]{:S(2)}) collective-permute-start(bf16[2,256,512]{2,1,0:T(8,128)(2,1)} %collective-permute-done.8.refs_7_), channel_id=1, source_target_pairs={{0,1},{1,0},{2,3},{3,2},{4,5},{5,4},{6,7},{7,6},{8,9},{9,8},{10,11... | collective-permute-start | bytes 1572872 | tf_op jit(solution)/shard_map/ppermute | solution.py:204
  66.3 0.8 copy-start.7
  67.1 1.5 %copy-start.8 = (bf16[2,256,512]{2,1,0:T(8,128)(2,1)}, bf16[2,256,512]{2,1,0:T(8,128)(2,1)S(1)}, u32[]{:S(2)}) copy-start(bf16[2,256,512]{2,1,0:T(8,128)(2,1)S(1)} %collective-permute-done.12.refs_11_) | copy-start | bytes 1572868

commit v7 on v6

--- a/solution.py
+++ b/solution.py
@@ -101,7 +101,11 @@
     near.wait()
     for h in range(2):
         for z in range(PEERS // 2):
-            copies[h * (PEERS // 2) + z] = pieces[h * PART : (h + 1) * PART]
+            spread = pltpu.make_async_copy(
+                pieces.at[pl.ds(h * PART, PART)], copies.at[h * (PEERS // 2) + z], sem.at[2]
+            )
+            spread.start()
+    pltpu.make_async_copy(copies, copies, sem.at[2]).wait()
     rest.wait()
 
 
@@ -188,8 +192,8 @@
         largest = jnp.maximum(jnp.max(jnp.abs(piece), axis=0, keepdims=True), 1e-30)
         level = jnp.ceil(jnp.log(largest) * (LEVELS / LN2)) + 1.0
         steps = piece * (STEPS * jnp.exp(level * (-LN2 / LEVELS)))
-        out[g, :WIDTH] = jnp.round(steps).astype(jnp.int32).astype(jnp.int16)
-        out[g, WIDTH:] = jnp.broadcast_to(level, (16, BLK)).astype(jnp.int32).astype(jnp.int16)
+        out[g % 2 * 4 + g // 2, :WIDTH] = jnp.round(steps).astype(jnp.int32).astype(jnp.int16)
+        out[g % 2 * 4 + g // 2, WIDTH:] = jnp.broadcast_to(level, (16, BLK)).astype(jnp.int32).astype(jnp.int16)
 
 
 def on_device(psi, left_blocks, right_ops, sector_rows, connect, term_order, sector_at):
@@ -221,14 +225,14 @@
     copies, part = pl.pallas_call(
         prepare_kernel,
         out_shape=(
-            jax.ShapeDtypeStruct((PEERS, PART, BLK), psi.dtype),
+            pltpu.HBM((PEERS, PART, BLK), psi.dtype),
             jax.ShapeDtypeStruct((REST, BLK), psi.dtype),
         ),
         in_specs=[smem, anywhere],
-        out_specs=(vmem, vmem),
+        out_specs=(anywhere, vmem),
         scratch_shapes=[
             pltpu.VMEM((2 * PART, BLK), psi.dtype),
-            pltpu.SemaphoreType.DMA((2,)),
+            pltpu.SemaphoreType.DMA((3,)),
         ],
         compiler_params=params,
     )(
@@ -289,7 +293,9 @@
         right_ops,
         *[pltpu.with_memory_space_constraint(b, pltpu.HBM) for b in blocks],
     )
-    parts = lax.all_to_all(summed, "term", 0, 0, tiled=True).astype(jnp.float32)
+    parts = lax.all_to_all(
+        summed, "term", 0, 0, axis_index_groups=[[y * 2 + x for x in range(2) for y in range(4)]], tiled=True
+    ).astype(jnp.float32)
     sizes = jnp.exp(parts[:, WIDTH:WIDTH + 1] * (LN2 / LEVELS)) * (1.0 / STEPS)
     return jnp.sum(parts[:, :WIDTH] * sizes, axis=0).T[None]
 

time: 96.5 us -> 96.2 us (level)
  no operation moved by 1% of the time
where the time goes in v7:
time: 96.2 us; the launch traced here: 95.8 us
  waiting for transfers between devices  34.8 us (36%)
  starting transfers between devices  24.4 us (25%)
  Pallas kernels  17.9 us (19%)
  blocking collectives  16.6 us (17%)
  other arithmetic  1.06 us (1%)
    ppermute x17, waiting for transfers between devices, hop(): return lax.ppermute(x, BOTH, perm)  31.2 us
    all_to_all x1, blocking collectives, on_device(): lax.all_to_all(summed, 'term', 0, 0, axis_index_groups=[[y * 2 + x for x...  16.6 us
    all_to_all x1, starting transfers between devices, on_device(): lax.all_to_all(copies, 'sector', 0, 0, axis_index_groups=SAME_CORE, tiled...  11.4 us
    pallas_call x1, Pallas kernels, on_device(): pl.pallas_call(product_kernel, out_shape=jax.ShapeDtypeStruct((GROUPS, WI...  9.76 us
    all_to_all x1, starting transfers between devices, on_device(): lax.all_to_all(chosen, BOTH, 0, 0, axis_index_groups=PEER_GROUPS, tiled=T...  7.46 us
    ppermute x17, starting transfers between devices, hop(): return lax.ppermute(x, BOTH, perm)  5.47 us
    pallas_call x1, Pallas kernels, on_device(): pl.pallas_call(index_kernel, out_shape=(jax.ShapeDtypeStruct((PEERS * SLO...  4.65 us
    all_to_all x1, waiting for transfers between devices, on_device(): lax.all_to_all(copies, 'sector', 0, 0, axis_index_groups=SAME_CORE, tiled...  3.54 us
  transfers between devices with their start and end apart: 19, of which 10 were waited for; matrix products, arithmetic and copies ran while one was open for 0% of the time, Pallas kernels for 7%

profile of v7, /device:TPU:4, one launch (start us, length us, event | category | flops | bytes accessed | tf_op | source)
XLA Modules:
  0.0 95.8 jit_solution(2734261357992675840)
XLA Ops:
  0.0 1.5 %shard_map.74 = (bf16[16,16,512]{2,1,0:T(8,128)(2,1)}, bf16[256,512]{1,0:T(8,128)(2,1)S(1)}) custom-call(s32[1]{0:T(128)} %bitcast.1.first, bf16[512,512]{1,0:T(8,128)(2,1)} %bitcast.12), custom_call_target="tpu_custom_call" | custom-call | tf_op jit(solution)/shard_map/pallas_call | solution.py:225
  1.5 0.6 collective-permute-start.1
  2.1 11.4 %all-to-all-start = ((bf16[16,16,512]{2,1,0:T(8,128)(2,1)}), bf16[16,16,512]{2,1,0:T(8,128)(2,1)S(1)}, u32[]{:S(2)}, u32[]{:S(2)}) async-start(bf16[16,16,512]{2,1,0:T(8,128)(2,1)} %get-tuple-element.12), calls=%async_computation | async-start | bytes 524288 | tf_op jit(solution)/shard_map/all_to_all | solution.py:244
  13.6 0.0 collective-permute-done.1
  13.6 0.1 pad_maximum_fusion.refs_0_
  13.6 1.5 %collective-permute-start.3 = (bf16[2,256,512]{2,1,0:T(8,128)(2,1)S(1)}, bf16[2,256,512]{2,1,0:T(8,128)(2,1)S(1)}, u32[]{:S(2)}, u32[]{:S(2)}) collective-permute-start(bf16[2,256,512]{2,1,0:T(8,128)(2,1)S(1)} %pad_maximum_fusion.refs_0_), channel_id=1, source_target_pairs={{0,2},{1,15},{2,4},{3,1},{4,6},{5,3},{6,8},{7,5},{8,10},{9,7},{10,... | collective-permute-start | bytes 1572872 | tf_op jit(solution)/shard_map/ppermute | solution.py:208
  15.2 0.0 collective-permute-start.2
  15.2 4.7 %shard_map.73 = (s32[128]{0:T(128)}, s32[4,8]{1,0:T(4,128)}) custom-call(s32[64]{0:T(128)} %term_order.1, s32[32,64]{1,0:T(8,128)} %bitcast.15, s32[32]{0:T(128)} %sector_at.1, s32[32]{0:T(128)} %sector_rows.1), custom_call_target="tpu_custom_call" | custom-call | bytes 8388608 | tf_op jit(solution)/shard_map/pallas_call | solution.py:210
  19.8 3.5 %all-to-all-done.own = bf16[16,16,512]{2,1,0:T(8,128)(2,1)S(1)} async-done(((bf16[16,16,512]{2,1,0:T(8,128)(2,1)}), bf16[16,16,512]{2,1,0:T(8,128)(2,1)S(1)}, u32[]{:S(2)}, u32[]{:S(2)}) %all-to-all-start) | async-done | bytes 262176 | tf_op jit(solution)/shard_map/all_to_all | solution.py:244
  23.4 0.0 collective-permute-start
  23.4 4.2 %collective-permute-done.3.refs_2_ = bf16[2,256,512]{2,1,0:T(8,128)(2,1)S(1)} collective-permute-done((bf16[2,256,512]{2,1,0:T(8,128)(2,1)S(1)}, bf16[2,256,512]{2,1,0:T(8,128)(2,1)S(1)}, u32[]{:S(2)}, u32[]{:S(2)}) %collective-permute-start.3) | collective-permute-done | bytes 524320 | tf_op jit(solution)/shard_map/ppermute | solution.py:208
  27.5 0.0 collective-permute-start.5
  27.5 0.0 collective-permute-done.2.refs_1_
  27.6 0.8 collective-permute-start.4
  28.3 0.0 collective-permute-done.other
  28.3 2.1 %shard_map.75 = bf16[16,8,16,512]{3,2,1,0:T(8,128)(2,1)} custom-call(s32[128]{0:T(128)} %get-tuple-element.11.front, bf16[16,16,512]{2,1,0:T(8,128)(2,1)S(1)} %all-to-all-done.own, bf16[16,16,512]{2,1,0:T(8,128)(2,1)S(1)} %collective-permute-done.other), custom_call_target="tpu_custom_call" | custom-call | bytes 8388608 | tf_op jit(solution)/shard_map/pallas_call | solution.py:247
  30.4 0.0 copy-start
  30.4 7.5 %all-to-all-start.1 = ((bf16[16,8,16,512]{3,2,1,0:T(8,128)(2,1)}), bf16[16,8,16,512]{3,2,1,0:T(8,128)(2,1)S(1)}, u32[]{:S(2)}, u32[]{:S(2)}) async-start(bf16[16,8,16,512]{3,2,1,0:T(8,128)(2,1)} %shard_map.75), calls=%async_computation.1 | async-start | bytes 4194304 | tf_op jit(solution)/shard_map/all_to_all | solution.py:260
  37.9 0.2 collective-permute-done.5.refs_4_
  38.0 1.4 %collective-permute-start.7 = (bf16[2,256,512]{2,1,0:T(8,128)(2,1)}, bf16[2,256,512]{2,1,0:T(8,128)(2,1)S(1)}, u32[]{:S(2)}, u32[]{:S(2)}) collective-permute-start(bf16[2,256,512]{2,1,0:T(8,128)(2,1)} %collective-permute-done.5.refs_4_), channel_id=1, source_target_pairs={{0,2},{1,15},{2,4},{3,1},{4,6},{5,3},{6,8},{7,5},{8,10},{9,7},{10,... | collective-permute-start | bytes 1572872 | tf_op jit(solution)/shard_map/ppermute | solution.py:208
  39.4 4.2 %collective-permute-done.4.refs_3_ = bf16[2,256,512]{2,1,0:T(8,128)(2,1)} collective-permute-done((bf16[2,256,512]{2,1,0:T(8,128)(2,1)}, bf16[2,256,512]{2,1,0:T(8,128)(2,1)}, u32[]{:S(2)}, u32[]{:S(2)}) %collective-permute-start.4) | collective-permute-done | bytes 524320 | tf_op jit(solution)/shard_map/ppermute | solution.py:208
  43.7 0.0 collective-permute-start.6
  43.7 0.0 collective-permute-start.16
  43.7 0.5 collective-permute-start.14
  44.2 5.0 %collective-permute-done.7.refs_6_ = bf16[2,256,512]{2,1,0:T(8,128)(2,1)S(1)} collective-permute-done((bf16[2,256,512]{2,1,0:T(8,128)(2,1)}, bf16[2,256,512]{2,1,0:T(8,128)(2,1)S(1)}, u32[]{:S(2)}, u32[]{:S(2)}) %collective-permute-start.7) | collective-permute-done | bytes 524320 | tf_op jit(solution)/shard_map/ppermute | solution.py:208
  49.2 0.0 collective-permute-start.9
  49.2 5.6 %collective-permute-done.6.refs_5_ = bf16[2,256,512]{2,1,0:T(8,128)(2,1)S(1)} collective-permute-done((bf16[2,256,512]{2,1,0:T(8,128)(2,1)}, bf16[2,256,512]{2,1,0:T(8,128)(2,1)S(1)}, u32[]{:S(2)}, u32[]{:S(2)}) %collective-permute-start.6) | collective-permute-done | bytes 524320 | tf_op jit(solution)/shard_map/ppermute | solution.py:208
  54.8 0.0 collective-permute-start.8
  54.8 0.0 collective-permute-start.15
  54.8 0.0 collective-permute-done.16.refs_15_
  54.8 0.5 collective-permute-start.12
  55.3 0.0 collective-permute-done.14.refs_13_
  55.3 0.1 collective-permute-start.13
  55.4 5.1 %collective-permute-done.9.refs_8_ = bf16[2,256,512]{2,1,0:T(8,128)(2,1)} collective-permute-done((bf16[2,256,512]{2,1,0:T(8,128)(2,1)S(1)}, bf16[2,256,512]{2,1,0:T(8,128)(2,1)}, u32[]{:S(2)}, u32[]{:S(2)}) %collective-permute-start.9) | collective-permute-done | bytes 524320 | tf_op jit(solution)/shard_map/ppermute | solution.py:208
  60.5 0.0 collective-permute-start.10
  60.5 5.6 %collective-permute-done.8.refs_7_ = bf16[2,256,512]{2,1,0:T(8,128)(2,1)} collective-permute-done((bf16[2,256,512]{2,1,0:T(8,128)(2,1)S(1)}, bf16[2,256,512]{2,1,0:T(8,128)(2,1)}, u32[]{:S(2)}, u32[]{:S(2)}) %collective-permute-start.8) | collective-permute-done | bytes 524320 | tf_op jit(solution)/shard_map/ppermute | solution.py:208
  66.1 0.0 collective-permute-start.11
  66.1 0.0 collective-permute-done.15.refs_14_
  66.1 0.0 collective-permute-done.12.refs_11_
  66.2 0.7 copy-done.7
  66.9 0.0 collective-permute-done.13.refs_12_
  66.9 0.1 all-to-all-done.1.front
  67.0 0.0 collective-permute-done.10.refs_9_
  67.0 1.4 %collective-permute-done.11.refs_10_ = bf16[2,256,512]{2,1,0:T(8,128)(2,1)} collective-permute-done((bf16[2,256,512]{2,1,0:T(8,128)(2,1)}, bf16[2,256,512]{2,1,0:T(8,128)(2,1)}, u32[]{:S(2)}, u32[]{:S(2)}) %collective-permute-start.11) | collective-permute-done | bytes 524320 | tf_op jit(solution)/shard_map/ppermute | solution.py:208
  68.4 9.8 %shard_map.76 = s16[8,80,512]{2,1,0:T(8,128)(2,1)S(1)} custom-call(s32[4,8]{1,0:T(4,128)S(1)} %copy-done, bf16[16,8,16,512]{3,2,1,0:T(8,128)(2,1)S(1)} %all-to-all-done.1.front, bf16[8,1,512,512]{3,2,1,0:T(8,128)(2,1)} %left.1, bf16[8,512,512]{2,1,0:T(8,128)(2,1)} %right.1, bf16[2,256,512]{2,1,0:T(8,128)(2,1)} %copy-done.1, ...), custom_call_target="tpu_custom_call" | custom-call | tf_op jit(solution)/shard_map/pallas_call | solution.py:274
  78.2 16.6 %all_to_all.15 = s16[8,80,512]{2,1,0:T(8,128)(2,1)S(1)} all-to-all(s16[8,80,512]{2,1,0:T(8,128)(2,1)S(1)} %shard_map.76), channel_id=1, replica_groups={{0,64,128,192,32,96,160,224},{1,65,129,193,33,97,161,225},{2,66,130,194..., dimensions={0} | all-to-all | bytes 1310720 | tf_op jit(solution)/shard_map/all_to_all | solution.py:296
  94.8 0.2 convert_element_type.3
  95.0 0.8 fusion
  (18 shorter events, 0.1 us)
Async XLA Ops:
  1.5 12.1 %collective-permute-start.1 = (bf16[256,512]{1,0:T(8,128)(2,1)S(1)}, bf16[256,512]{1,0:T(8,128)(2,1)S(1)}, u32[]{:S(2)}, u32[]{:S(2)}) collective-permute-start(bf16[256,512]{1,0:T(8,128)(2,1)S(1)} %get-tuple-element.14), channel_id=1, source_target_pairs={{0,48},{1,49},{2,50},{3,51},{4,52},{5,53},{6,54},{7,55},{8,56},{9,... | collective-permute-start | bytes 786440 | tf_op jit(solution)/shard_map/ppermute | solution.py:208
  2.1 21.3 %all-to-all-start = ((bf16[16,16,512]{2,1,0:T(8,128)(2,1)}), bf16[16,16,512]{2,1,0:T(8,128)(2,1)S(1)}, u32[]{:S(2)}, u32[]{:S(2)}) async-start(bf16[16,16,512]{2,1,0:T(8,128)(2,1)} %get-tuple-element.12), calls=%async_computation | async-start | bytes 524288 | tf_op jit(solution)/shard_map/all_to_all | solution.py:244
  13.6 16.8 %copy-start.1 = (bf16[2,256,512]{2,1,0:T(8,128)(2,1)}, bf16[2,256,512]{2,1,0:T(8,128)(2,1)S(1)}, u32[]{:S(2)}) copy-start(bf16[2,256,512]{2,1,0:T(8,128)(2,1)S(1)} %pad_maximum_fusion.refs_0_) | copy-start | bytes 1572868
  13.6 13.9 %collective-permute-start.3 = (bf16[2,256,512]{2,1,0:T(8,128)(2,1)S(1)}, bf16[2,256,512]{2,1,0:T(8,128)(2,1)S(1)}, u32[]{:S(2)}, u32[]{:S(2)}) collective-permute-start(bf16[2,256,512]{2,1,0:T(8,128)(2,1)S(1)} %pad_maximum_fusion.refs_0_), channel_id=1, source_target_pairs={{0,2},{1,15},{2,4},{3,1},{4,6},{5,3},{6,8},{7,5},{8,10},{9,7},{10,... | collective-permute-start | bytes 1572872 | tf_op jit(solution)/shard_map/ppermute | solution.py:208
  15.2 12.4 %collective-permute-start.2 = (bf16[2,256,512]{2,1,0:T(8,128)(2,1)S(1)}, bf16[2,256,512]{2,1,0:T(8,128)(2,1)}, u32[]{:S(2)}, u32[]{:S(2)}) collective-permute-start(bf16[2,256,512]{2,1,0:T(8,128)(2,1)S(1)} %pad_maximum_fusion.refs_0_), channel_id=1, source_target_pairs={{0,1},{1,0},{2,3},{3,2},{4,5},{5,4},{6,7},{7,6},{8,9},{9,8},{10,11... | collective-permute-start | bytes 1572872 | tf_op jit(solution)/shard_map/ppermute | solution.py:208
  23.4 5.0 %collective-permute-start = (bf16[16,16,512]{2,1,0:T(8,128)(2,1)S(1)}, bf16[16,16,512]{2,1,0:T(8,128)(2,1)S(1)}, u32[]{:S(2)}, u32[]{:S(2)}) collective-permute-start(bf16[16,16,512]{2,1,0:T(8,128)(2,1)S(1)} %all-to-all-done.own), channel_id=1, source_target_pairs={{0,1},{1,0},{2,3},{3,2},{4,5},{5,4},{6,7},{7,6},{8,9},{9,8},{10,11... | collective-permute-start | bytes 786440 | tf_op jit(solution)/shard_map/ppermute | solution.py:208
  27.5 16.1 %copy-start.2 = (bf16[2,256,512]{2,1,0:T(8,128)(2,1)}, bf16[2,256,512]{2,1,0:T(8,128)(2,1)S(1)}, u32[]{:S(2)}) copy-start(bf16[2,256,512]{2,1,0:T(8,128)(2,1)S(1)} %collective-permute-done.3.refs_2_) | copy-start | bytes 1572868
  27.5 10.5 %collective-permute-start.5 = (bf16[2,256,512]{2,1,0:T(8,128)(2,1)S(1)}, bf16[2,256,512]{2,1,0:T(8,128)(2,1)}, u32[]{:S(2)}, u32[]{:S(2)}) collective-permute-start(bf16[2,256,512]{2,1,0:T(8,128)(2,1)S(1)} %collective-permute-done.3.refs_2_), channel_id=1, source_target_pairs={{0,2},{1,15},{2,4},{3,1},{4,6},{5,3},{6,8},{7,5},{8,10},{9,7},{10,... | collective-permute-start | bytes 1572872 | tf_op jit(solution)/shard_map/ppermute | solution.py:208
  27.6 16.1 %collective-permute-start.4 = (bf16[2,256,512]{2,1,0:T(8,128)(2,1)}, bf16[2,256,512]{2,1,0:T(8,128)(2,1)}, u32[]{:S(2)}, u32[]{:S(2)}) collective-permute-start(bf16[2,256,512]{2,1,0:T(8,128)(2,1)} %collective-permute-done.2.refs_1_), channel_id=1, source_target_pairs={{0,2},{1,15},{2,4},{3,1},{4,6},{5,3},{6,8},{7,5},{8,10},{9,7},{10,... | collective-permute-start | bytes 1572872 | tf_op jit(solution)/shard_map/ppermute | solution.py:208
  30.4 38.0 %copy-start = (s32[4,8]{1,0:T(4,128)S(1)}, s32[4,8]{1,0:T(4,128)}, u32[]{:S(2)}) copy-start(s32[4,8]{1,0:T(4,128)} %get-tuple-element.10.mine) | copy-start | bytes 388
  30.4 36.6 %all-to-all-start.1 = ((bf16[16,8,16,512]{3,2,1,0:T(8,128)(2,1)}), bf16[16,8,16,512]{3,2,1,0:T(8,128)(2,1)S(1)}, u32[]{:S(2)}, u32[]{:S(2)}) async-start(bf16[16,8,16,512]{3,2,1,0:T(8,128)(2,1)} %shard_map.75), calls=%async_computation.1 | async-start | bytes 4194304 | tf_op jit(solution)/shard_map/all_to_all | solution.py:260
  38.0 11.1 %collective-permute-start.7 = (bf16[2,256,512]{2,1,0:T(8,128)(2,1)}, bf16[2,256,512]{2,1,0:T(8,128)(2,1)S(1)}, u32[]{:S(2)}, u32[]{:S(2)}) collective-permute-start(bf16[2,256,512]{2,1,0:T(8,128)(2,1)} %collective-permute-done.5.refs_4_), channel_id=1, source_target_pairs={{0,2},{1,15},{2,4},{3,1},{4,6},{5,3},{6,8},{7,5},{8,10},{9,7},{10,... | collective-permute-start | bytes 1572872 | tf_op jit(solution)/shard_map/ppermute | solution.py:208
  43.7 11.1 %collective-permute-start.6 = (bf16[2,256,512]{2,1,0:T(8,128)(2,1)}, bf16[2,256,512]{2,1,0:T(8,128)(2,1)S(1)}, u32[]{:S(2)}, u32[]{:S(2)}) collective-permute-start(bf16[2,256,512]{2,1,0:T(8,128)(2,1)} %collective-permute-done.4.refs_3_), channel_id=1, source_target_pairs={{0,2},{1,15},{2,4},{3,1},{4,6},{5,3},{6,8},{7,5},{8,10},{9,7},{10,... | collective-permute-start | bytes 1572872 | tf_op jit(solution)/shard_map/ppermute | solution.py:208
  43.7 11.1 %collective-permute-start.16 = (bf16[2,256,512]{2,1,0:T(8,128)(2,1)S(1)}, bf16[2,256,512]{2,1,0:T(8,128)(2,1)S(1)}, u32[]{:S(2)}, u32[]{:S(2)}) collective-permute-start(bf16[2,256,512]{2,1,0:T(8,128)(2,1)S(1)} %collective-permute-done.3.refs_2_), channel_id=1, source_target_pairs={{0,1},{1,0},{2,3},{3,2},{4,5},{5,4},{6,7},{7,6},{8,9},{9,8},{10,11... | collective-permute-start | bytes 1572872 | tf_op jit(solution)/shard_map/ppermute | solution.py:208
  43.7 11.6 %collective-permute-start.14 = (bf16[2,256,512]{2,1,0:T(8,128)(2,1)}, bf16[2,256,512]{2,1,0:T(8,128)(2,1)S(1)}, u32[]{:S(2)}, u32[]{:S(2)}) collective-permute-start(bf16[2,256,512]{2,1,0:T(8,128)(2,1)} %collective-permute-done.5.refs_4_), channel_id=1, source_target_pairs={{0,1},{1,0},{2,3},{3,2},{4,5},{5,4},{6,7},{7,6},{8,9},{9,8},{10,11... | collective-permute-start | bytes 1572872 | tf_op jit(solution)/shard_map/ppermute | solution.py:208
  49.2 19.2 %copy-start.3 = (bf16[2,256,512]{2,1,0:T(8,128)(2,1)}, bf16[2,256,512]{2,1,0:T(8,128)(2,1)S(1)}, u32[]{:S(2)}) copy-start(bf16[2,256,512]{2,1,0:T(8,128)(2,1)S(1)} %collective-permute-done.7.refs_6_) | copy-start | bytes 1572868
  49.2 11.3 %collective-permute-start.9 = (bf16[2,256,512]{2,1,0:T(8,128)(2,1)S(1)}, bf16[2,256,512]{2,1,0:T(8,128)(2,1)}, u32[]{:S(2)}, u32[]{:S(2)}) collective-permute-start(bf16[2,256,512]{2,1,0:T(8,128)(2,1)S(1)} %collective-permute-done.7.refs_6_), channel_id=1, source_target_pairs={{0,2},{1,15},{2,4},{3,1},{4,6},{5,3},{6,8},{7,5},{8,10},{9,7},{10,... | collective-permute-start | bytes 1572872 | tf_op jit(solution)/shard_map/ppermute | solution.py:208
  54.8 11.4 %copy-start.4 = (bf16[2,256,512]{2,1,0:T(8,128)(2,1)}, bf16[2,256,512]{2,1,0:T(8,128)(2,1)S(1)}, u32[]{:S(2)}) copy-start(bf16[2,256,512]{2,1,0:T(8,128)(2,1)S(1)} %collective-permute-done.6.refs_5_) | copy-start | bytes 1572868
  54.8 11.3 %collective-permute-start.8 = (bf16[2,256,512]{2,1,0:T(8,128)(2,1)S(1)}, bf16[2,256,512]{2,1,0:T(8,128)(2,1)}, u32[]{:S(2)}, u32[]{:S(2)}) collective-permute-start(bf16[2,256,512]{2,1,0:T(8,128)(2,1)S(1)} %collective-permute-done.6.refs_5_), channel_id=1, source_target_pairs={{0,2},{1,15},{2,4},{3,1},{4,6},{5,3},{6,8},{7,5},{8,10},{9,7},{10,... | collective-permute-start | bytes 1572872 | tf_op jit(solution)/shard_map/ppermute | solution.py:208
  54.8 11.3 %collective-permute-start.15 = (bf16[2,256,512]{2,1,0:T(8,128)(2,1)}, bf16[2,256,512]{2,1,0:T(8,128)(2,1)S(1)}, u32[]{:S(2)}, u32[]{:S(2)}) collective-permute-start(bf16[2,256,512]{2,1,0:T(8,128)(2,1)} %collective-permute-done.4.refs_3_), channel_id=1, source_target_pairs={{0,1},{1,0},{2,3},{3,2},{4,5},{5,4},{6,7},{7,6},{8,9},{9,8},{10,11... | collective-permute-start | bytes 1572872 | tf_op jit(solution)/shard_map/ppermute | solution.py:208
  54.8 11.4 %copy-start.5 = (bf16[2,256,512]{2,1,0:T(8,128)(2,1)}, bf16[2,256,512]{2,1,0:T(8,128)(2,1)S(1)}, u32[]{:S(2)}) copy-start(bf16[2,256,512]{2,1,0:T(8,128)(2,1)S(1)} %collective-permute-done.16.refs_15_) | copy-start | bytes 1572868
  54.8 11.3 %collective-permute-start.12 = (bf16[2,256,512]{2,1,0:T(8,128)(2,1)S(1)}, bf16[2,256,512]{2,1,0:T(8,128)(2,1)S(1)}, u32[]{:S(2)}, u32[]{:S(2)}) collective-permute-start(bf16[2,256,512]{2,1,0:T(8,128)(2,1)S(1)} %collective-permute-done.7.refs_6_), channel_id=1, source_target_pairs={{0,1},{1,0},{2,3},{3,2},{4,5},{5,4},{6,7},{7,6},{8,9},{9,8},{10,11... | collective-permute-start | bytes 1572872 | tf_op jit(solution)/shard_map/ppermute | solution.py:208
  55.3 10.9 %copy-start.6 = (bf16[2,256,512]{2,1,0:T(8,128)(2,1)}, bf16[2,256,512]{2,1,0:T(8,128)(2,1)S(1)}, u32[]{:S(2)}) copy-start(bf16[2,256,512]{2,1,0:T(8,128)(2,1)S(1)} %collective-permute-done.14.refs_13_) | copy-start | bytes 1572868
  55.3 11.6 %collective-permute-start.13 = (bf16[2,256,512]{2,1,0:T(8,128)(2,1)S(1)}, bf16[2,256,512]{2,1,0:T(8,128)(2,1)}, u32[]{:S(2)}, u32[]{:S(2)}) collective-permute-start(bf16[2,256,512]{2,1,0:T(8,128)(2,1)S(1)} %collective-permute-done.6.refs_5_), channel_id=1, source_target_pairs={{0,1},{1,0},{2,3},{3,2},{4,5},{5,4},{6,7},{7,6},{8,9},{9,8},{10,11... | collective-permute-start | bytes 1572872 | tf_op jit(solution)/shard_map/ppermute | solution.py:208
  60.5 6.5 %collective-permute-start.10 = (bf16[2,256,512]{2,1,0:T(8,128)(2,1)}, bf16[2,256,512]{2,1,0:T(8,128)(2,1)}, u32[]{:S(2)}, u32[]{:S(2)}) collective-permute-start(bf16[2,256,512]{2,1,0:T(8,128)(2,1)} %collective-permute-done.9.refs_8_), channel_id=1, source_target_pairs={{0,1},{1,0},{2,3},{3,2},{4,5},{5,4},{6,7},{7,6},{8,9},{9,8},{10,11... | collective-permute-start | bytes 1572872 | tf_op jit(solution)/shard_map/ppermute | solution.py:208
  66.1 2.3 %collective-permute-start.11 = (bf16[2,256,512]{2,1,0:T(8,128)(2,1)}, bf16[2,256,512]{2,1,0:T(8,128)(2,1)}, u32[]{:S(2)}, u32[]{:S(2)}) collective-permute-start(bf16[2,256,512]{2,1,0:T(8,128)(2,1)} %collective-permute-done.8.refs_7_), channel_id=1, source_target_pairs={{0,1},{1,0},{2,3},{3,2},{4,5},{5,4},{6,7},{7,6},{8,9},{9,8},{10,11... | collective-permute-start | bytes 1572872 | tf_op jit(solution)/shard_map/ppermute | solution.py:208
  66.1 0.8 copy-start.7
  66.9 1.5 %copy-start.8 = (bf16[2,256,512]{2,1,0:T(8,128)(2,1)}, bf16[2,256,512]{2,1,0:T(8,128)(2,1)S(1)}, u32[]{:S(2)}) copy-start(bf16[2,256,512]{2,1,0:T(8,128)(2,1)S(1)} %collective-permute-done.12.refs_11_) | copy-start | bytes 1572868
